TPU v7x, 128 devices: a whole 4x4x4 slice. The times are simulated.
128 devices in a mesh: tok: 32 (over z, y, core), exp: 4 (over x).
Axes of the slice: x: 4, y: 4, z: 4, core: 2. Of those that a mesh axis runs over, the one named last changes fastest.
Arguments:
- tokens: bfloat16 [2, 32, 576, 384], P(None, 'tok', 'exp'), may hold values from -6 to 6
- patch_counts: int32 [2, 32], P(None, 'tok'), may hold values from 196 to 576, as said below
- attn_routes: int32 [2, 32, 576, 4], P(None, 'tok', 'exp'), may hold values from 0 to 11, all different within a row; in each aligned block of 144 rows (0 to 143, 144 to 287, ..., all dimensions but the last counted through in order) at most 64 rows name the same one
- mlp_routes: int32 [2, 32, 576, 4], P(None, 'tok', 'exp'), may hold values from 0 to 11, all different within a row; in each aligned block of 144 rows (0 to 143, 144 to 287, ..., all dimensions but the last counted through in order) at most 64 rows name the same one
- norm1_gain: bfloat16 [384], P(('tok', 'exp')), may hold values from 0.5 to 1.5
- norm1_bias: bfloat16 [384], P(('tok', 'exp')), may hold values from -1.1953125 to 1.1953125
- norm2_gain: bfloat16 [384], P(('tok', 'exp')), may hold values from 0.5 to 1.5
- norm2_bias: bfloat16 [384], P(('tok', 'exp')), may hold values from -1.1953125 to 1.1953125
- key_value_weight: bfloat16 [384, 768], P(('tok', 'exp')), may hold values from -0.3125 to 0.3125
- attn_router: bfloat16 [384, 12], P(('tok', 'exp')), may hold values from -0.15625 to 0.15625
- mlp_router: bfloat16 [384, 12], P(('tok', 'exp')), may hold values from -0.15625 to 0.15625
- query_weight: bfloat16 [12, 384, 384], P('exp', 'tok'), may hold values from -0.3125 to 0.3125
- output_weight: bfloat16 [12, 384, 384], P('exp', 'tok'), may hold values from -2.5 to 2.5
- up_weight: bfloat16 [12, 384, 1536], P('exp', 'tok'), may hold values from -0.3125 to 0.3125
- down_weight: bfloat16 [12, 1536, 384], P('exp', 'tok'), may hold values from -0.15625 to 0.15625
- cotangent: bfloat16 [2, 32, 576, 384], P(None, 'tok', 'exp'), may hold values from -6 to 6
Outputs:
- layer_out: bfloat16 [2, 32, 576, 384], P(None, 'tok', 'exp')
- tokens_grad: bfloat16 [2, 32, 576, 384], P(None, 'tok', 'exp')
- norm1_gain_grad: float32 [384], P(('tok', 'exp'))
- norm1_bias_grad: float32 [384], P(('tok', 'exp'))
- norm2_gain_grad: float32 [384], P(('tok', 'exp'))
- norm2_bias_grad: float32 [384], P(('tok', 'exp'))
- key_value_grad: float32 [384, 768], P(('tok', 'exp'))
- attn_router_grad: float32 [384, 12], P(('tok', 'exp'))
- mlp_router_grad: float32 [384, 12], P(('tok', 'exp'))
- query_grad: float32 [12, 384, 384], P('exp', 'tok')
- output_grad: float32 [12, 384, 384], P('exp', 'tok')
- up_grad: float32 [12, 384, 1536], P('exp', 'tok')
- down_grad: float32 [12, 1536, 384], P('exp', 'tok')
Inputs may be any that keep to these rules, and one draw needn't show every extreme that they name: `patch_counts`: each image has 196 or 576 real patches, its first slots; among the images that one index of tok holds, at least one has 576. `attn_routes`: each token names 4 different experts; within each aligned block of 144 slots (one image's slots on one index of exp) no expert is named by more than 64 tokens, a bound that some block reaches. `mlp_routes`: as for attn_routes: 4 different experts a token, at most 64 tokens of an aligned block of 144 slots for one expert, reached in some blocks.
All inputs are finite; a program needn't handle non-finite values.
Results may differ from a plain program's by a relative error of at most 0.025.
Values may be sent and summed in bfloat16 or wider, within the bound.
No kernel may reach another device: no remote copies, remote signals or barrier semaphores. Data moves between devices by JAX's collectives and lax.ppermute only.
A program may use at most 256 MiB of HBM per device.

v0:
```python
import jax
import jax.numpy as jnp
from jax import lax
from jax.sharding import PartitionSpec as P

HEADS = 6
HEAD_DIM = 64
EXP_DEV = 3
TOP = 4
CAP = 64


EPSILON = 1e-06
PRECISE = lax.Precision.HIGHEST
MASKED = -1e30


def rows_first(arrays, axis, dims):
    turned = [jnp.moveaxis(a, dim, 0) for a, dim in zip(arrays, dims)]
    both = jnp.concatenate([t.reshape(len(t), -1) for t in turned], axis=1)
    out, at, finished = (lax.all_gather(both, axis, axis=0, tiled=True), 0, [])
    for t, dim in zip(turned, dims):
        section = out[:, at : at + t[0].size].reshape(-1, *t.shape[1:])
        finished.append(jnp.moveaxis(section, 0, dim))
        at += t[0].size
    return tuple(finished)


def side_by_side(arrays, axis, dim, along):
    both = jnp.concatenate(arrays, axis=along)
    out, at, finished = (lax.all_gather(both, axis, axis=dim, tiled=True), 0, [])
    for a in arrays:
        finished.append(lax.slice_in_dim(out, at, at + a.shape[along], axis=along))
        at += a.shape[along]
    return tuple(finished)


def cut_along(array, dim, size):
    before, after = (array.shape[:dim], array.shape[dim + 1 :])
    return jnp.moveaxis(array.reshape(*before, size, -1, *after), dim, 0)


def one_scatter(arrays, axis, dims):
    size = lax.axis_size(axis)
    pieces = [cut_along(a, dim, size) for a, dim in zip(arrays, dims)]
    lines = jnp.concatenate([b.reshape(size, -1) for b in pieces], axis=1)
    span = max(16, -(-lines.shape[1] // 1024) * 8)
    lines = jnp.pad(lines, ((0, 0), (0, span * 128 - lines.shape[1]))).reshape(-1, 128)
    flat, at, finished = (lax.psum_scatter(lines, axis, tiled=True).reshape(-1), 0, [])
    for b in pieces:
        part = b[0]
        finished.append(flat[at : at + part.size].reshape(part.shape))
        at += part.size
    return tuple(finished)


def normalize(values, gain_row, bias_row):
    average = jnp.mean(values, -1, keepdims=True)
    centered = values - average
    variance = jnp.mean(centered * centered, -1, keepdims=True)
    inverse = lax.rsqrt(variance + EPSILON)
    normed = centered * inverse
    return (normed * gain_row + bias_row, normed, inverse)


def normalize_back(gradient, normed, inverse, gain_row):
    weighted = gradient * gain_row
    centred_grad = (
        weighted
        - jnp.mean(weighted, -1, keepdims=True)
        - normed * jnp.mean(weighted * normed, -1, keepdims=True)
    )
    feature_count = gradient.shape[-1]
    gain_grad = jnp.sum((gradient * normed).reshape(-1, feature_count), 0)
    bias_grad = jnp.sum(gradient.reshape(-1, feature_count), 0)
    return (centred_grad * inverse, gain_grad, bias_grad)


def exact_gelu(values):
    return jax.nn.gelu(values, approximate=False)


def choose(logits, routes):
    one_hot = (routes[..., None] == jnp.arange(logits.shape[-1], dtype=jnp.int32)).astype(
        jnp.float32
    )
    chosen = jnp.sum(one_hot * logits[:, :, None, :], -1)
    return (jax.nn.softmax(chosen, -1), one_hot)


def router_back(gradient, returned, gates, one_hot):
    gate_grad = jnp.sum(gradient[:, :, None, :] * returned.astype(jnp.float32), -1)
    centred = gates * (gate_grad - jnp.sum(gates * gate_grad, -1, keepdims=True))
    return jnp.sum(one_hot * centred[..., None], 2)


def destinations(routes, expert_count):
    image_count = routes.shape[0]
    flat_routes = routes.reshape(image_count, -1)
    one_hot = (flat_routes[..., None] == jnp.arange(expert_count, dtype=jnp.int32)).astype(
        jnp.int32
    )
    position = jnp.sum((jnp.cumsum(one_hot, 1) - 1) * one_hot, -1)
    owner_rank = flat_routes // EXP_DEV
    within = flat_routes % EXP_DEV
    image_ids = jnp.arange(image_count, dtype=jnp.int32)[:, None]
    return (((owner_rank * image_count + image_ids) * EXP_DEV + within) * CAP + position).reshape(
        -1
    )


def dispatch(expanded, target, owners):
    feature_count = expanded.shape[-1]
    image_count = expanded.shape[0]
    flat_rows = expanded.reshape(-1, feature_count)
    buffer = jnp.zeros((owners * image_count * EXP_DEV * CAP, feature_count), expanded.dtype)
    return (
        buffer.at[target].set(flat_rows).reshape(owners, image_count, EXP_DEV, CAP, feature_count)
    )


def collect(arrived, target, layout):
    feature_count = arrived.shape[-1]
    return arrived.reshape(-1, feature_count)[target].reshape(layout)


def split_heads(image_rows, att_width):
    keys_here = image_rows[:, :att_width].reshape(-1, HEADS, HEAD_DIM)
    values_here = image_rows[:, att_width:].reshape(-1, HEADS, HEAD_DIM)
    return (keys_here, values_here)


def masked_scores(query_heads, keys_here, visible, scale_factor):
    scores = (
        jnp.einsum("sechd,jhd->hsecj", query_heads, keys_here, preferred_element_type=jnp.float32)
        * scale_factor
    )
    return jnp.where(visible, scores, MASKED)


def fetch_weights(
    gain_one,
    bias_one,
    gain_two,
    bias_two,
    kv_weight,
    router_attn,
    router_mlp,
    query_part,
    output_part,
    up_part,
    down_part,
):
    shared_full = rows_first(
        (gain_one, bias_one, gain_two, bias_two, kv_weight, router_attn, router_mlp),
        ("tok", "exp"),
        (0, 0, 0, 0, 0, 0, 0),
    )
    owned_full = (
        *side_by_side((query_part, output_part, up_part), "tok", 1, 2),
        lax.all_gather(down_part, "tok", axis=1, tiled=True),
    )
    return (shared_full, owned_full)


def settle_grads(shared_grads, owned_grads):
    shared_part = (
        lax.psum_scatter(shared_grads[0], ("tok", "exp"), scatter_dimension=0, tiled=True),
        lax.psum_scatter(shared_grads[1], ("tok", "exp"), scatter_dimension=0, tiled=True),
        lax.psum_scatter(shared_grads[2], ("tok", "exp"), scatter_dimension=0, tiled=True),
        lax.psum_scatter(shared_grads[3], ("tok", "exp"), scatter_dimension=0, tiled=True),
        lax.psum_scatter(shared_grads[4], ("tok", "exp"), scatter_dimension=0, tiled=True),
        lax.psum_scatter(shared_grads[5], ("tok", "exp"), scatter_dimension=0, tiled=True),
        lax.psum_scatter(shared_grads[6], ("tok", "exp"), scatter_dimension=0, tiled=True),
    )
    owned_part = tuple(
        (
            part.astype(jnp.float32)
            for part in one_scatter(
                (
                    owned_grads[0].astype(jnp.bfloat16),
                    owned_grads[1].astype(jnp.bfloat16),
                    owned_grads[2].astype(jnp.bfloat16),
                    owned_grads[3].astype(jnp.bfloat16),
                ),
                "tok",
                (1, 1, 1, 1),
            )
        )
    )
    return (tuple(shared_part), tuple(owned_part))


def accumulate(running, addition):
    if running is None:
        return addition
    return jax.tree.map(jnp.add, running, addition)


def micro_step(inputs, lengths, routes_attn, routes_mlp, upstream, shared_full, owned_full, owners):
    gain_one, bias_one, gain_two, bias_two, kv_weight, router_attn, router_mlp = shared_full
    query_full, output_full, up_full, down_full = owned_full
    image_count, slots_here, feature_count = inputs.shape
    expert_count = router_attn.shape[1]
    att_width = query_full.shape[2]
    scale_factor = HEAD_DIM ** (-0.5)
    layout = (image_count, slots_here, TOP, feature_count)
    flat_count = image_count * slots_here
    gain_one_f = gain_one.astype(jnp.float32)
    gain_two_f = gain_two.astype(jnp.float32)
    residual = inputs.astype(jnp.float32)
    normed_one_out, normed_one, inverse_one = normalize(
        residual, gain_one_f, bias_one.astype(jnp.float32)
    )
    attn_in = normed_one_out.astype(jnp.bfloat16)
    flat_attn_in = attn_in.reshape(flat_count, feature_count)
    key_values = jnp.dot(flat_attn_in, kv_weight, preferred_element_type=jnp.float32).astype(
        jnp.bfloat16
    )
    image_keys = lax.all_gather(
        key_values.reshape(image_count, slots_here, 2 * att_width), "exp", axis=1, tiled=True
    )
    logits_attn = jnp.dot(
        flat_attn_in.astype(jnp.float32), router_attn.astype(jnp.float32), precision=PRECISE
    )
    gates_attn, onehot_attn = choose(
        logits_attn.reshape(image_count, slots_here, expert_count), routes_attn
    )
    target_attn = destinations(routes_attn, expert_count)
    expanded_attn = jnp.broadcast_to(attn_in[:, :, None, :], layout)
    arrived_attn = lax.all_to_all(
        dispatch(expanded_attn, target_attn, owners), "exp", split_axis=0, concat_axis=0, tiled=True
    )
    senders = arrived_attn.shape[0]
    queries = jnp.einsum(
        "siecd,edf->siecf", arrived_attn, query_full, preferred_element_type=jnp.float32
    ).astype(jnp.bfloat16)
    slot_index = jnp.arange(image_keys.shape[1], dtype=jnp.int32)
    image_index = 0
    keys_here, values_here = split_heads(image_keys[image_index], att_width)
    visible = slot_index < lengths[image_index]
    query_heads = queries[:, image_index].reshape(senders, EXP_DEV, CAP, HEADS, HEAD_DIM)
    scores = masked_scores(query_heads, keys_here, visible, scale_factor)
    maximum = jnp.max(scores, -1, keepdims=True)
    exponent = jnp.exp(scores - maximum)
    totals = jnp.sum(exponent, -1, keepdims=True)
    probability = exponent / totals
    log_totals = [maximum + jnp.log(totals)]
    attended = jnp.einsum(
        "hsecj,jhd->sechd",
        probability.astype(jnp.bfloat16),
        values_here,
        preferred_element_type=jnp.float32,
    )
    attended_list = [attended.astype(jnp.bfloat16).reshape(senders, EXP_DEV, CAP, att_width)]
    attended_all = jnp.stack(attended_list, 1)
    branch_attn = jnp.einsum(
        "siecf,efd->siecd", attended_all, output_full, preferred_element_type=jnp.float32
    ).astype(jnp.bfloat16)
    returned_attn = collect(
        lax.all_to_all(branch_attn, "exp", split_axis=0, concat_axis=0, tiled=True),
        target_attn,
        layout,
    )
    mixed_one = residual + jnp.sum(gates_attn[..., None] * returned_attn.astype(jnp.float32), 2)
    normed_two_out, normed_two, inverse_two = normalize(
        mixed_one, gain_two_f, bias_two.astype(jnp.float32)
    )
    mlp_in = normed_two_out.astype(jnp.bfloat16)
    flat_mlp_in = mlp_in.reshape(flat_count, feature_count)
    logits_mlp = jnp.dot(
        flat_mlp_in.astype(jnp.float32), router_mlp.astype(jnp.float32), precision=PRECISE
    )
    gates_mlp, onehot_mlp = choose(
        logits_mlp.reshape(image_count, slots_here, expert_count), routes_mlp
    )
    target_mlp = destinations(routes_mlp, expert_count)
    expanded_mlp = jnp.broadcast_to(mlp_in[:, :, None, :], layout)
    arrived_mlp = lax.all_to_all(
        dispatch(expanded_mlp, target_mlp, owners), "exp", split_axis=0, concat_axis=0, tiled=True
    )
    hidden_pre = jnp.einsum(
        "siecd,edf->siecf", arrived_mlp, up_full, preferred_element_type=jnp.float32
    )
    hidden = exact_gelu(hidden_pre).astype(jnp.bfloat16)
    branch_mlp = jnp.einsum(
        "siecf,efd->siecd", hidden, down_full, preferred_element_type=jnp.float32
    ).astype(jnp.bfloat16)
    returned_mlp = collect(
        lax.all_to_all(branch_mlp, "exp", split_axis=0, concat_axis=0, tiled=True),
        target_mlp,
        layout,
    )
    result = mixed_one + jnp.sum(gates_mlp[..., None] * returned_mlp.astype(jnp.float32), 2)
    upstream_f = upstream.astype(jnp.float32)
    grad_rows_mlp = (gates_mlp[..., None] * upstream_f[:, :, None, :]).astype(jnp.bfloat16)
    dlogits_mlp = router_back(upstream_f, returned_mlp, gates_mlp, onehot_mlp).reshape(
        flat_count, expert_count
    )
    router_mlp_grad = jnp.dot(flat_mlp_in.astype(jnp.float32).T, dlogits_mlp, precision=PRECISE)
    grad_router_mlp = jnp.dot(dlogits_mlp, router_mlp.astype(jnp.float32).T, precision=PRECISE)
    arrived_grad_mlp = lax.all_to_all(
        dispatch(grad_rows_mlp, target_mlp, owners), "exp", split_axis=0, concat_axis=0, tiled=True
    )
    down_grad = jnp.einsum(
        "siecf,siecd->efd", hidden, arrived_grad_mlp, preferred_element_type=jnp.float32
    )
    hidden_grad = jnp.einsum(
        "siecd,efd->siecf", arrived_grad_mlp, down_full, preferred_element_type=jnp.float32
    )
    _, gelu_back = jax.vjp(exact_gelu, hidden_pre)
    pre_grad = gelu_back(hidden_grad)[0].astype(jnp.bfloat16)
    up_grad = jnp.einsum(
        "siecd,siecf->edf", arrived_mlp, pre_grad, preferred_element_type=jnp.float32
    )
    rows_back_mlp = jnp.einsum(
        "siecf,edf->siecd", pre_grad, up_full, preferred_element_type=jnp.float32
    ).astype(jnp.bfloat16)
    returned_grad_mlp = collect(
        lax.all_to_all(rows_back_mlp, "exp", split_axis=0, concat_axis=0, tiled=True),
        target_mlp,
        layout,
    )
    grad_mlp_in = jnp.sum(returned_grad_mlp.astype(jnp.float32), 2) + grad_router_mlp.reshape(
        image_count, slots_here, feature_count
    )
    grad_norm_two, gain_two_grad, bias_two_grad = normalize_back(
        grad_mlp_in, normed_two, inverse_two, gain_two_f
    )
    grad_mixed = upstream_f + grad_norm_two
    grad_rows_attn = (gates_attn[..., None] * grad_mixed[:, :, None, :]).astype(jnp.bfloat16)
    dlogits_attn = router_back(grad_mixed, returned_attn, gates_attn, onehot_attn).reshape(
        flat_count, expert_count
    )
    router_attn_grad = jnp.dot(flat_attn_in.astype(jnp.float32).T, dlogits_attn, precision=PRECISE)
    grad_router_attn = jnp.dot(dlogits_attn, router_attn.astype(jnp.float32).T, precision=PRECISE)
    arrived_grad_attn = lax.all_to_all(
        dispatch(grad_rows_attn, target_attn, owners),
        "exp",
        split_axis=0,
        concat_axis=0,
        tiled=True,
    )
    output_grad = jnp.einsum(
        "siecf,siecd->efd", attended_all, arrived_grad_attn, preferred_element_type=jnp.float32
    )
    attended_grad = jnp.einsum(
        "siecd,efd->siecf", arrived_grad_attn, output_full, preferred_element_type=jnp.float32
    ).astype(jnp.bfloat16)
    image_index = 0
    keys_here, values_here = split_heads(image_keys[image_index], att_width)
    visible = slot_index < lengths[image_index]
    query_heads = queries[:, image_index].reshape(senders, EXP_DEV, CAP, HEADS, HEAD_DIM)
    scores = masked_scores(query_heads, keys_here, visible, scale_factor)
    probability = jnp.exp(scores - log_totals[image_index])
    grad_heads = attended_grad[:, image_index].reshape(senders, EXP_DEV, CAP, HEADS, HEAD_DIM)
    prob_grad = jnp.einsum(
        "sechd,jhd->hsecj", grad_heads, values_here, preferred_element_type=jnp.float32
    )
    row_inner = jnp.sum(probability * prob_grad, -1, keepdims=True)
    score_grad = (probability * (prob_grad - row_inner)).astype(jnp.bfloat16)
    query_grad_here = (
        jnp.einsum("hsecj,jhd->sechd", score_grad, keys_here, preferred_element_type=jnp.float32)
        * scale_factor
    )
    query_grad_list = [
        query_grad_here.astype(jnp.bfloat16).reshape(senders, EXP_DEV, CAP, att_width)
    ]
    key_grad = (
        jnp.einsum("hsecj,sechd->jhd", score_grad, query_heads, preferred_element_type=jnp.float32)
        * scale_factor
    )
    value_grad = jnp.einsum(
        "hsecj,sechd->jhd",
        probability.astype(jnp.bfloat16),
        grad_heads,
        preferred_element_type=jnp.float32,
    )
    key_value_list = [
        jnp.concatenate([key_grad.reshape(-1, att_width), value_grad.reshape(-1, att_width)], -1)
    ]
    kv_grad_here = lax.psum_scatter(
        jnp.stack(key_value_list, 0).astype(jnp.bfloat16), "exp", scatter_dimension=1, tiled=True
    )
    flat_kv_grad = kv_grad_here.reshape(flat_count, 2 * att_width)
    kv_weight_grad = jnp.einsum(
        "nd,nf->df", flat_attn_in, flat_kv_grad, preferred_element_type=jnp.float32
    )
    grad_from_kv = jnp.einsum(
        "nf,df->nd", flat_kv_grad, kv_weight, preferred_element_type=jnp.float32
    )
    query_grad_all = jnp.stack(query_grad_list, 1)
    query_weight_grad = jnp.einsum(
        "siecd,siecf->edf", arrived_attn, query_grad_all, preferred_element_type=jnp.float32
    )
    rows_back_attn = jnp.einsum(
        "siecf,edf->siecd", query_grad_all, query_full, preferred_element_type=jnp.float32
    ).astype(jnp.bfloat16)
    returned_grad_attn = collect(
        lax.all_to_all(rows_back_attn, "exp", split_axis=0, concat_axis=0, tiled=True),
        target_attn,
        layout,
    )
    grad_attn_in = jnp.sum(returned_grad_attn.astype(jnp.float32), 2) + (
        grad_router_attn + grad_from_kv
    ).reshape(image_count, slots_here, feature_count)
    grad_norm_one, gain_one_grad, bias_one_grad = normalize_back(
        grad_attn_in, normed_one, inverse_one, gain_one_f
    )
    input_grad = (grad_mixed + grad_norm_one).astype(jnp.bfloat16)
    shared_grads = (
        gain_one_grad,
        bias_one_grad,
        gain_two_grad,
        bias_two_grad,
        kv_weight_grad,
        router_attn_grad,
        router_mlp_grad,
    )
    owned_grads = (query_weight_grad, output_grad, up_grad, down_grad)
    return (result.astype(jnp.bfloat16), input_grad, shared_grads, owned_grads)


def local(
    tokens,
    patch_counts,
    attn_routes,
    mlp_routes,
    norm1_gain,
    norm1_bias,
    norm2_gain,
    norm2_bias,
    key_value_weight,
    attn_router,
    mlp_router,
    query_weight,
    output_weight,
    up_weight,
    down_weight,
    cotangent,
):
    owners = lax.axis_size("exp")
    micro_count = tokens.shape[0]
    shared_total = None
    owned_total = None
    outputs = []
    input_grads = []
    for micro_index in range(micro_count):
        shared_full, owned_full = fetch_weights(
            norm1_gain,
            norm1_bias,
            norm2_gain,
            norm2_bias,
            key_value_weight,
            attn_router,
            mlp_router,
            query_weight,
            output_weight,
            up_weight,
            down_weight,
        )
        result, input_grad, shared_grads, owned_grads = micro_step(
            tokens[micro_index],
            patch_counts[micro_index],
            attn_routes[micro_index],
            mlp_routes[micro_index],
            cotangent[micro_index],
            shared_full,
            owned_full,
            owners,
        )
        outputs.append(result)
        input_grads.append(input_grad)
        shared_part, owned_part = settle_grads(shared_grads, owned_grads)
        shared_total = accumulate(shared_total, shared_part)
        owned_total = accumulate(owned_total, owned_part)
    return (
        jnp.stack(outputs),
        jnp.stack(input_grads),
        shared_total[0],
        shared_total[1],
        shared_total[2],
        shared_total[3],
        shared_total[4],
        shared_total[5],
        shared_total[6],
        owned_total[0],
        owned_total[1],
        owned_total[2],
        owned_total[3],
    )


def solution(mesh):
    placed = (
        P(None, "tok", "exp", None),
        P(None, "tok"),
        P(None, "tok", "exp", None),
        P(None, "tok", "exp", None),
        P(("tok", "exp")),
        P(("tok", "exp")),
        P(("tok", "exp")),
        P(("tok", "exp")),
        P(("tok", "exp"), None),
        P(("tok", "exp"), None),
        P(("tok", "exp"), None),
        P("exp", "tok", None),
        P("exp", "tok", None),
        P("exp", "tok", None),
        P("exp", "tok", None),
        P(None, "tok", "exp", None),
    )
    return jax.shard_map(
        local,
        mesh=mesh,
        in_specs=placed,
        out_specs=(
            P(None, "tok", "exp", None),
            P(None, "tok", "exp", None),
            P(("tok", "exp")),
            P(("tok", "exp")),
            P(("tok", "exp")),
            P(("tok", "exp")),
            P(("tok", "exp"), None),
            P(("tok", "exp"), None),
            P(("tok", "exp"), None),
            P("exp", "tok", None),
            P("exp", "tok", None),
            P("exp", "tok", None),
            P("exp", "tok", None),
        ),
        check_vma=False,
    )
```

profile of v0, /device:TPU:0, one launch (start us, length us, event | category | flops | bytes accessed | tf_op | source)
XLA Modules:
  0.0 977.2 jit_solution(11188310930348688704)
XLA Ops:
  19.1 63.7 %all-gather.2 = bf16[128,3,796]{2,1,0:T(4,128)(2,1)S(1)} all-gather(bf16[1,3,796]{2,1,0:T(4,128)(2,1)S(1)} %bitcast.856), channel_id=1, replica_groups=mesh['tok'=32,'exp'=4] {'tok','exp'}, dimensions={0}, use_global_device_ids=true | all-gather | bytes 616104 | tf_op jit(solution)/shard_map/all_gather | solution.py:21
  84.9 6.4 scatter_custom_fusion
  91.3 4.1 all-to-all-start
  108.2 14.5 %all-gather = bf16[576,768]{1,0:T(8,128)(2,1)S(1)} all-gather(bf16[144,768]{1,0:T(8,128)(2,1)S(1)} %convolution_convert_fusion.11), channel_id=2, replica_groups=mesh['tok'=32,'exp'=4] {'exp'}, dimensions={0}, use_global_device_ids=true | all-gather | bytes 1105920 | tf_op jit(solution)/shard_map/all_gather | solution.py:220
  128.5 3.5 fusion.323
  143.5 6.1 fusion.68
  155.5 5.0 all-to-all-start.1
  160.5 6.2 slice.228
  174.2 6.4 scatter_custom_fusion.2
  180.6 4.1 all-to-all-start.4
  184.8 17.5 %all-gather.1 = bf16[576,768]{1,0:T(8,128)(2,1)S(1)} all-gather(bf16[144,768]{1,0:T(8,128)(2,1)S(1)} %convolution_convert_fusion.10), channel_id=3, replica_groups=mesh['tok'=32,'exp'=4] {'exp'}, dimensions={0}, use_global_device_ids=true | all-gather | bytes 1105920 | tf_op jit(solution)/shard_map/all_gather | solution.py:220
  219.2 6.1 fusion.69
  231.2 3.6 all-to-all-start.5
  235.5 7.7 all-to-all-done.5
  248.9 6.4 scatter_custom_fusion.3
  255.3 3.5 all-to-all-start.6
  259.3 6.4 scatter_custom_fusion.1
  267.1 3.7 all-to-all-start.2
  270.9 6.2 fusion.147
  277.1 13.3 %fusion.118 = bf16[4,1,3,64,384]{4,3,0,2,1:T(8,128)(2,1)S(1)} fusion(bf16[3,1536,384]{2,1,0:T(8,128)(2,1)} %all-gather.8.cloned.1.call-done, f32[3,1536,4,64]{1,3,2,0:T(8,128)} %fusion.147), kind=kOutput, calls=%fused_computation.160 | convolution fusion | flops 982941696 | bytes 8847360 | tf_op jit(solution)/shard_map/siecf,efd->siecd/dot_general | solution.py:286
  291.3 4.8 all-to-all-start.7
  296.0 4.1 fusion.152
  300.2 11.7 %fusion.121 = bf16[4,1,3,64,384]{4,3,0,2,1:T(8,128)(2,1)S(1)} fusion(bf16[3,1536,384]{2,1,0:T(8,128)(2,1)S(1)} %copy-done.143, f32[3,1536,4,64]{1,3,2,0:T(8,128)S(1)} %fusion.152), kind=kOutput, calls=%fused_computation.161 | convolution fusion | flops 982941696 | bytes 8847360 | tf_op jit(solution)/shard_map/siecf,efd->siecd/dot_general | solution.py:286
  312.8 5.3 all-to-all-start.3
  322.8 8.2 scatter_custom_fusion.6
  331.0 4.8 all-to-all-start.12
  340.5 8.2 scatter_custom_fusion.4
  348.8 5.0 all-to-all-start.8
  353.8 13.7 %fusion.61 = bf16[4,3,64,1536]{3,2,0,1:T(8,128)(2,1)S(1)} fusion(f32[3,1536,4,64]{1,3,2,0:T(8,128)} %fusion.147, bf16[3,1536,384]{2,1,0:T(8,128)(2,1)} %all-gather.8.cloned.1.call-done, bf16[4,1,3,64,384]{4,3,2,1,0:T(8,128)(2,1)} %all-to-all-done.12), kind=kOutput, calls=%fused_computation.112 | convolution fusion | flops 990904320 | bytes 11206656 | tf_op jit(solution)/shard_map/siecd,efd->siecf/dot_general | solution.py:308
  367.6 14.3 %bitcast_convert_fusion = bf16[3,1536,384]{2,1,0:T(8,128)(2,1)} fusion(bf16[4,1,3,64,384]{4,3,2,1,0:T(8,128)(2,1)} %all-to-all-done.12, f32[3,1536,4,64]{1,3,2,0:T(8,128)} %fusion.147), kind=kOutput, calls=%fused_computation.34 | convolution fusion | flops 984416256 | bytes 8847360 | tf_op jit(solution)/shard_map/siecf,siecd->efd/dot_general | solution.py:305
  384.2 4.8 all-to-all-start.13
  389.0 13.7 %fusion.58 = bf16[4,3,64,1536]{3,2,0,1:T(8,128)(2,1)S(1)} fusion(f32[3,1536,4,64]{1,3,2,0:T(8,128)} %copy-done.14, bf16[3,1536,384]{2,1,0:T(8,128)(2,1)} %all-gather.8.cloned.1.call-done, bf16[4,1,3,64,384]{4,3,2,1,0:T(8,128)(2,1)S(1)} %all-to-all-done.8), kind=kOutput, calls=%fused_computation.111 | convolution fusion | flops 990904320 | bytes 11206656 | tf_op jit(solution)/shard_map/siecd,efd->siecf/dot_general | solution.py:308
  405.1 5.2 all-to-all-start.9
  410.4 13.5 %bitcast_convert_fusion.2 = bf16[3,1536,384]{2,1,0:T(8,128)(2,1)} fusion(bf16[4,1,3,64,384]{4,3,2,1,0:T(8,128)(2,1)S(1)} %all-to-all-done.8, f32[3,1536,4,64]{1,3,2,0:T(8,128)} %copy-done.14), kind=kOutput, calls=%fused_computation.36 | convolution fusion | flops 984416256 | bytes 8847360 | tf_op jit(solution)/shard_map/siecf,siecd->efd/dot_general | solution.py:305
  442.6 7.7 scatter_custom_fusion.5
  450.3 5.0 all-to-all-start.10
  458.3 3.4 reshape.3389
  461.7 4.9 copy.605
  466.6 6.2 reshape.3390
  476.9 3.4 reshape.3380
  480.3 4.9 copy.599
  485.2 6.2 reshape.3381
  491.9 8.3 scatter_custom_fusion.7
  500.3 4.8 all-to-all-start.14
  507.6 3.6 reshape_squeeze.20
  511.2 7.2 multiply_reduce_fusion.1
  518.6 6.1 fusion.2
  524.7 4.6 fusion.96
  532.9 7.2 fusion.70
  545.3 4.6 fusion.105
  563.4 4.3 copy.631
  568.9 7.1 multiply_reduce_fusion
  576.0 6.7 fusion.3
  587.5 5.4 copy.633
  595.6 13.8 %pad_maximum_fusion = bf16[32,138240]{1,0:T(8,128)(2,1)} fusion(bf16[32,55296]{1,0:T(8,128)(2,1)S(1)} %bitcast.828, bf16[32,55296]{1,0:T(8,128)(2,1)} %reshape.3381, bf16[32,13824]{1,0:T(8,128)(2,1)} %reshape.3379, bf16[32,13824]{1,0:T(8,128)(2,1)} %reshape.3377), kind=kLoop, calls=%fused_computation.32 | loop fusion | flops 35389440 | bytes 17694720 | tf_op jit(solution)/shard_map/concatenate | solution.py:46
  612.8 6.2 fusion.71
  630.7 11.0 %pad_maximum_fusion.1 = bf16[32,138240]{1,0:T(8,128)(2,1)} fusion(bf16[32,55296]{1,0:T(8,128)(2,1)} %bitcast.827, bf16[32,55296]{1,0:T(8,128)(2,1)} %reshape.3390, bf16[32,13824]{1,0:T(8,128)(2,1)S(1)} %copy-done.43, bf16[32,13824]{1,0:T(8,128)(2,1)} %reshape.3386), kind=kLoop, calls=%fused_computation.33 | loop fusion | flops 35389440 | bytes 17694720 | tf_op jit(solution)/shard_map/concatenate | solution.py:46
  641.7 9.3 reshape.3384
  651.0 9.2 reshape.3393
  677.4 4.7 all-to-all-start.11
  687.4 5.8 all-to-all-done.11
  693.1 3.7 all-to-all-start.15
  713.9 72.2 %all-reduce.13 = (f32[384]{0:T(512)S(1)}, f32[384]{0:T(512)S(1)}, f32[384]{0:T(512)S(1)}, f32[384]{0:T(512)S(1)}, f32[384,12]{1,0:T(8,128)S(1)}, /*index=5*/f32[384,12]{1,0:T(8,128)S(1)}) all-reduce(f32[384]{0:T(512)S(1)} %add.629, f32[384]{0:T(512)S(1)} %add.630, ...), channel_id=13, replica_groups=mesh['tok'=32,'exp'=4] {'tok','exp'}, use_global_device_ids=true, to_apply=%region_77.78.clone | all-reduce | flops 10752 | bytes 86016
  792.0 173.1 %all-reduce.20.cloned.1.call-done = (bf16[34560,128]{1,0:T(8,128)(2,1)}, bf16[34560,128]{1,0:T(8,128)(2,1)}) async-done(((bf16[34560,128]{1,0:T(8,128)(2,1)}, bf16[34560,128]{1,0:T(8,128)(2,1)}), (bf16[34560,128]{1,0:T(8,128)(2,1)}, bf16[34560,128]{1,0:T(8,128)(2,1)})) %all-reduce.20.cloned.1.call-update) | async-done | bytes 17694736
  (696 shorter events, 226.5 us)
Async XLA Ops:
  7.2 76.3 %copy-start.3 = (bf16[2,1,144,384]{3,2,1,0:T(8,128)(2,1)S(1)}, bf16[2,1,144,384]{3,2,1,0:T(8,128)(2,1)}, u32[]{:S(2)}) copy-start(bf16[2,1,144,384]{3,2,1,0:T(8,128)(2,1)} %param.16) | copy-start | bytes 663556
  7.2 89.0 %copy-start.102 = (s32[2,1,144,4]{2,3,1,0:T(4,128)S(1)}, s32[2,1,144,4]{2,3,1,0:T(4,128)}, u32[]{:S(2)}) copy-start(s32[2,1,144,4]{2,3,1,0:T(4,128)} %param.19) | copy-start | bytes 13828
  7.2 121.3 %all-gather.6.cloned.1.call-start = ((), (), s32[]{:S(2)}) async-start(), calls=%async_computation.18 | async-start | bytes 7299072 | tf_op jit(solution)/shard_map/all_gather | solution.py:31
  15.4 92.7 %copy-start.94 = (s32[144,4]{0,1:T(4,128)}, s32[144,4]{0,1:T(4,128)S(1)}, u32[]{:S(2)}) copy-start(s32[144,4]{0,1:T(4,128)S(1)} %get-tuple-element.88) | copy-start | bytes 6916
  15.4 158.4 %copy-start.96 = (s32[144,4]{0,1:T(4,128)}, s32[144,4]{0,1:T(4,128)S(1)}, u32[]{:S(2)}) copy-start(s32[144,4]{0,1:T(4,128)S(1)} %get-tuple-element.87) | copy-start | bytes 6916
  82.8 20.5 %copy-start.142 = (s32[2,1]{0,1:T(1,128)S(1)}, s32[2,1]{0,1:T(1,128)}, u32[]{:S(2)}) copy-start(s32[2,1]{0,1:T(1,128)} %param.17) | copy-start | bytes 28
  83.5 175.3 %copy-start.6 = (bf16[384,796]{1,0:T(8,128)(2,1)}, bf16[384,796]{1,0:T(8,128)(2,1)S(1)}, u32[]{:S(2)}) copy-start(bf16[384,796]{1,0:T(8,128)(2,1)S(1)} %reshape.3551) | copy-start | bytes 1833988
  83.7 24.2 %copy-start.110 = (f32[144]{0:T(256)}, f32[144]{0:T(256)S(1)}, u32[]{:S(2)}) copy-start(f32[144]{0:T(256)S(1)} %broadcast_multiply_fusion.11) | copy-start | bytes 1732
  83.9 24.1 %copy-start.66 = (bf16[2,1,144,384]{3,2,1,0:T(8,128)(2,1)S(1)}, bf16[2,1,144,384]{3,2,1,0:T(8,128)(2,1)}, u32[]{:S(2)}) copy-start(bf16[2,1,144,384]{3,2,1,0:T(8,128)(2,1)} %param.31) | copy-start | bytes 663556
  84.2 88.8 %copy-start.83 = (f32[384]{0:T(512)}, f32[384]{0:T(512)S(1)}, u32[]{:S(2)}) copy-start(f32[384]{0:T(512)S(1)} %get-tuple-element.13) | copy-start | bytes 4612
  84.2 88.8 %copy-start.88 = (f32[384]{0:T(512)}, f32[384]{0:T(512)S(1)}, u32[]{:S(2)}) copy-start(f32[384]{0:T(512)S(1)} %get-tuple-element.16) | copy-start | bytes 4612
  84.2 163.8 %copy-start.113 = (f32[384]{0:T(512)}, f32[384]{0:T(512)S(1)}, u32[]{:S(2)}) copy-start(f32[384]{0:T(512)S(1)} %get-tuple-element.15) | copy-start | bytes 4612
  84.3 23.7 %copy-start.51 = (bf16[144,384]{1,0:T(8,128)(2,1)}, bf16[144,384]{1,0:T(8,128)(2,1)S(1)}, u32[]{:S(2)}) copy-start(bf16[144,384]{1,0:T(8,128)(2,1)S(1)} %fusion.233) | copy-start | bytes 331780
  84.9 37.9 %copy-start.123 = (s32[576]{0:T(1024)}, s32[576]{0:T(1024)S(1)}, u32[]{:S(2)}) copy-start(s32[576]{0:T(1024)S(1)} %fusion.307) | copy-start | bytes 6916
  91.3 40.7 %all-to-all-start = ((bf16[4,1,3,64,384]{4,3,2,1,0:T(8,128)(2,1)}), bf16[4,1,3,64,384]{4,3,2,1,0:T(8,128)(2,1)}, u32[]{:S(2)}, u32[]{:S(2)}) async-start(bf16[4,1,3,64,384]{4,3,2,1,0:T(8,128)(2,1)} %bitcast.20), calls=%async_computation | async-start | bytes 1179648 | tf_op jit(solution)/shard_map/all_to_all | solution.py:231
  95.5 181.6 %all-gather.8.cloned.1.call-start = ((), (), s32[]{:S(2)}) async-start(), calls=%async_computation.19 | async-start | bytes 3649536 | tf_op jit(solution)/shard_map/all_gather | solution.py:161
  102.6 66.3 %copy-start.90 = (s32[1024]{0:T(1024)}, s32[1024]{0:T(1024)S(1)}, u32[]{:S(2)}) copy-start(s32[1024]{0:T(1024)S(1)} %pad_clamp_fusion.3) | copy-start | bytes 12292
  104.6 113.2 %copy-start.98 = (pred[576]{0:T(1024)(128)(4,1)}, pred[576]{0:T(1024)(128)(4,1)S(1)}, u32[]{:S(2)}) copy-start(pred[576]{0:T(1024)(128)(4,1)S(1)} %iota_compare_fusion.4) | copy-start | bytes 1732
  108.1 19.3 %copy-start.79 = (f32[144,4]{0,1:T(4,128)}, f32[144,4]{0,1:T(4,128)S(1)}, u32[]{:S(2)}) copy-start(f32[144,4]{0,1:T(4,128)S(1)} %select_reduce_fusion.7) | copy-start | bytes 6916
  122.9 51.3 %copy-start.124 = (s32[576]{0:T(1024)}, s32[576]{0:T(1024)S(1)}, u32[]{:S(2)}) copy-start(s32[576]{0:T(1024)S(1)} %fusion.309) | copy-start | bytes 6916
  128.5 114.7 %copy-start.92 = (s32[1024]{0:T(1024)}, s32[1024]{0:T(1024)S(1)}, u32[]{:S(2)}) copy-start(s32[1024]{0:T(1024)S(1)} %pad_clamp_fusion.1) | copy-start | bytes 12292
  155.5 13.4 %all-to-all-start.1 = ((bf16[4,1,3,64,384]{4,3,2,1,0:T(8,128)(2,1)}), bf16[4,1,3,64,384]{4,3,2,1,0:T(8,128)(2,1)S(1)}, u32[]{:S(2)}, u32[]{:S(2)}) async-start(bf16[4,1,3,64,384]{4,3,2,1,0:T(8,128)(2,1)} %copy.511), calls=%async_computation.1 | async-start | bytes 1179648 | tf_op jit(solution)/shard_map/all_to_all | solution.py:261
  171.7 32.5 %copy-start.25 = (bf16[576,384]{1,0:T(8,128)(2,1)}, bf16[576,384]{1,0:T(8,128)(2,1)S(1)}, u32[]{:S(2)}) copy-start(bf16[576,384]{1,0:T(8,128)(2,1)S(1)} %gather_fusion) | copy-start | bytes 1327108
  172.5 75.5 %copy-start.15 = (f32[144,384]{1,0:T(8,128)}, f32[144,384]{1,0:T(8,128)S(1)}, u32[]{:S(2)}) copy-start(f32[144,384]{1,0:T(8,128)S(1)} %multiply_reduce_fusion.9) | copy-start | bytes 663556
  172.6 75.3 %copy-start.118 = (f32[144]{0:T(256)}, f32[144]{0:T(256)S(1)}, u32[]{:S(2)}) copy-start(f32[144]{0:T(256)S(1)} %broadcast_multiply_fusion.10) | copy-start | bytes 1732
  173.0 29.3 %copy-start.115 = (f32[144]{0:T(256)}, f32[144]{0:T(256)S(1)}, u32[]{:S(2)}) copy-start(f32[144]{0:T(256)S(1)} %add_rsqrt_fusion.1) | copy-start | bytes 1732
  173.1 31.1 %copy-start.53 = (bf16[144,384]{1,0:T(8,128)(2,1)}, bf16[144,384]{1,0:T(8,128)(2,1)S(1)}, u32[]{:S(2)}) copy-start(bf16[144,384]{1,0:T(8,128)(2,1)S(1)} %fusion.215) | copy-start | bytes 331780
  173.8 35.7 %copy-start.81 = (f32[144,4]{0,1:T(4,128)}, f32[144,4]{0,1:T(4,128)S(1)}, u32[]{:S(2)}) copy-start(f32[144,4]{0,1:T(4,128)S(1)} %select_reduce_fusion.5) | copy-start | bytes 6916
  173.9 35.7 %copy-start.108 = (f32[144]{0:T(256)}, f32[144]{0:T(256)S(1)}, u32[]{:S(2)}) copy-start(f32[144]{0:T(256)S(1)} %reduce_max.57) | copy-start | bytes 1732
  173.9 35.7 %copy-start.127 = (f32[144]{0:T(256)}, f32[144]{0:T(256)S(1)}, u32[]{:S(2)}) copy-start(f32[144]{0:T(256)S(1)} %fusion.300) | copy-start | bytes 1732
  180.6 27.0 %all-to-all-start.4 = ((bf16[4,1,3,64,384]{4,3,2,1,0:T(8,128)(2,1)}), bf16[4,1,3,64,384]{4,3,2,1,0:T(8,128)(2,1)}, u32[]{:S(2)}, u32[]{:S(2)}) async-start(bf16[4,1,3,64,384]{4,3,2,1,0:T(8,128)(2,1)} %bitcast.68), calls=%async_computation.4 | async-start | bytes 1179648 | tf_op jit(solution)/shard_map/all_to_all | solution.py:231
  231.2 12.0 %all-to-all-start.5 = ((bf16[4,1,3,64,384]{4,3,2,1,0:T(8,128)(2,1)}), bf16[4,1,3,64,384]{4,3,2,1,0:T(8,128)(2,1)S(1)}, u32[]{:S(2)}, u32[]{:S(2)}) async-start(bf16[4,1,3,64,384]{4,3,2,1,0:T(8,128)(2,1)} %copy.542), calls=%async_computation.5 | async-start | bytes 1179648 | tf_op jit(solution)/shard_map/all_to_all | solution.py:261
  247.6 29.4 %copy-start.18 = (f32[144,384]{1,0:T(8,128)}, f32[144,384]{1,0:T(8,128)S(1)}, u32[]{:S(2)}) copy-start(f32[144,384]{1,0:T(8,128)S(1)} %multiply_reduce_fusion.7) | copy-start | bytes 663556
  247.9 29.1 %copy-start.134 = (f32[144]{0:T(256)}, f32[144]{0:T(256)S(1)}, u32[]{:S(2)}) copy-start(f32[144]{0:T(256)S(1)} %add_rsqrt_fusion) | copy-start | bytes 1732
  248.3 28.7 %copy-start.60 = (bf16[144,384]{1,0:T(8,128)(2,1)}, bf16[144,384]{1,0:T(8,128)(2,1)S(1)}, u32[]{:S(2)}) copy-start(bf16[144,384]{1,0:T(8,128)(2,1)S(1)} %get-tuple-element.70) | copy-start | bytes 331780
  255.3 11.9 %all-to-all-start.6 = ((bf16[4,1,3,64,384]{4,3,2,1,0:T(8,128)(2,1)}), bf16[4,1,3,64,384]{4,3,2,1,0:T(8,128)(2,1)S(1)}, u32[]{:S(2)}, u32[]{:S(2)}) async-start(bf16[4,1,3,64,384]{4,3,2,1,0:T(8,128)(2,1)} %bitcast.87), calls=%async_computation.6 | async-start | bytes 1179648 | tf_op jit(solution)/shard_map/all_to_all | solution.py:279
  267.1 24.1 %all-to-all-start.2 = ((bf16[4,1,3,64,384]{4,3,2,1,0:T(8,128)(2,1)}), bf16[4,1,3,64,384]{4,3,2,1,0:T(8,128)(2,1)S(1)}, u32[]{:S(2)}, u32[]{:S(2)}) async-start(bf16[4,1,3,64,384]{4,3,2,1,0:T(8,128)(2,1)} %bitcast.40), calls=%async_computation.2 | async-start | bytes 1179648 | tf_op jit(solution)/shard_map/all_to_all | solution.py:279
  291.3 21.6 %all-to-all-start.7 = ((bf16[4,1,3,64,384]{4,3,2,1,0:T(8,128)(2,1)}), bf16[4,1,3,64,384]{4,3,2,1,0:T(8,128)(2,1)S(1)}, u32[]{:S(2)}, u32[]{:S(2)}) async-start(bf16[4,1,3,64,384]{4,3,2,1,0:T(8,128)(2,1)} %copy.554), calls=%async_computation.7 | async-start | bytes 1179648 | tf_op jit(solution)/shard_map/all_to_all | solution.py:290
  312.8 18.1 %all-to-all-start.3 = ((bf16[4,1,3,64,384]{4,3,2,1,0:T(8,128)(2,1)}), bf16[4,1,3,64,384]{4,3,2,1,0:T(8,128)(2,1)S(1)}, u32[]{:S(2)}, u32[]{:S(2)}) async-start(bf16[4,1,3,64,384]{4,3,2,1,0:T(8,128)(2,1)} %copy.524), calls=%async_computation.3 | async-start | bytes 1179648 | tf_op jit(solution)/shard_map/all_to_all | solution.py:290
  331.0 17.8 %all-to-all-start.12 = ((bf16[4,1,3,64,384]{4,3,2,1,0:T(8,128)(2,1)}), bf16[4,1,3,64,384]{4,3,2,1,0:T(8,128)(2,1)}, u32[]{:S(2)}, u32[]{:S(2)}) async-start(bf16[4,1,3,64,384]{4,3,2,1,0:T(8,128)(2,1)} %bitcast.143), calls=%async_computation.12 | async-start | bytes 1179648 | tf_op jit(solution)/shard_map/all_to_all | solution.py:302
  338.5 29.0 %copy-start.31 = (bf16[576,384]{1,0:T(8,128)(2,1)}, bf16[576,384]{1,0:T(8,128)(2,1)S(1)}, u32[]{:S(2)}) copy-start(bf16[576,384]{1,0:T(8,128)(2,1)S(1)} %gather_fusion.1) | copy-start | bytes 1327108
  338.6 43.3 %slice-start.3 = ((s8[4718592]{0:T(1024)(128)(4,1)}), s8[524288]{0:T(1024)(128)(4,1)S(1)}, s32[]{:S(2)}) async-start(s8[4718592]{0:T(1024)(128)(4,1)} %bitcast.811), calls=%async_computation.27 | async-start | bytes 1048576
  340.4 27.2 %copy-start.70 = (f32[144,4]{1,0:T(8,128)}, f32[144,4]{1,0:T(8,128)S(1)}, u32[]{:S(2)}) copy-start(f32[144,4]{1,0:T(8,128)S(1)} %copy.512) | copy-start | bytes 6916
  348.8 86.4 %copy-start.86 = (f32[144,12]{0,1:T(8,128)}, f32[144,12]{0,1:T(8,128)S(1)}, u32[]{:S(2)}) copy-start(f32[144,12]{0,1:T(8,128)S(1)} %get-tuple-element.110) | copy-start | bytes 20740
  348.8 35.4 %all-to-all-start.8 = ((bf16[4,1,3,64,384]{4,3,2,1,0:T(8,128)(2,1)}), bf16[4,1,3,64,384]{4,3,2,1,0:T(8,128)(2,1)S(1)}, u32[]{:S(2)}, u32[]{:S(2)}) async-start(bf16[4,1,3,64,384]{4,3,2,1,0:T(8,128)(2,1)} %bitcast.105), calls=%async_computation.8 | async-start | bytes 1179648 | tf_op jit(solution)/shard_map/all_to_all | solution.py:302
  353.8 28.1 %slice-start.4 = ((s8[4718592]{0:T(1024)(128)(4,1)}), s8[4194304]{0:T(1024)(128)(4,1)S(1)}, s32[]{:S(2)}) async-start(s8[4718592]{0:T(1024)(128)(4,1)} %bitcast.811), calls=%async_computation.28 | async-start | bytes 8388608
  381.9 20.8 %slice-start.5 = ((s8[4718592]{0:T(1024)(128)(4,1)}), s8[524288]{0:T(1024)(128)(4,1)S(1)}, s32[]{:S(2)}) async-start(s8[4718592]{0:T(1024)(128)(4,1)} %bitcast.813), calls=%async_computation.29 | async-start | bytes 1048576
  384.2 20.9 %all-to-all-start.13 = ((bf16[4,1,3,64,384]{4,3,2,1,0:T(8,128)(2,1)}), bf16[4,1,3,64,384]{4,3,2,1,0:T(8,128)(2,1)S(1)}, u32[]{:S(2)}, u32[]{:S(2)}) async-start(bf16[4,1,3,64,384]{4,3,2,1,0:T(8,128)(2,1)} %copy.578), calls=%async_computation.13 | async-start | bytes 1179648 | tf_op jit(solution)/shard_map/all_to_all | solution.py:320
  405.1 24.7 %all-to-all-start.9 = ((bf16[4,1,3,64,384]{4,3,2,1,0:T(8,128)(2,1)}), bf16[4,1,3,64,384]{4,3,2,1,0:T(8,128)(2,1)S(1)}, u32[]{:S(2)}, u32[]{:S(2)}) async-start(bf16[4,1,3,64,384]{4,3,2,1,0:T(8,128)(2,1)} %copy.558), calls=%async_computation.9 | async-start | bytes 1179648 | tf_op jit(solution)/shard_map/all_to_all | solution.py:320
  450.3 50.0 %all-to-all-start.10 = ((bf16[4,1,3,64,384]{4,3,2,1,0:T(8,128)(2,1)}), bf16[4,1,3,64,384]{4,3,2,1,0:T(8,128)(2,1)}, u32[]{:S(2)}, u32[]{:S(2)}) async-start(bf16[4,1,3,64,384]{4,3,2,1,0:T(8,128)(2,1)} %bitcast.847), calls=%async_computation.10 | async-start | bytes 1179648 | tf_op jit(solution)/shard_map/all_to_all | solution.py:337
  491.6 19.6 %copy-start.72 = (f32[6,4,3,64]{3,2,1,0:T(4,128)S(1)}, f32[6,4,3,64]{3,2,1,0:T(4,128)}, u32[]{:S(2)}) copy-start(f32[6,4,3,64]{3,2,1,0:T(4,128)} %log_add_fusion.1) | copy-start | bytes 55300
  491.6 19.6 %copy-start.101 = (pred[576]{0:T(1024)(128)(4,1)S(1)}, pred[576]{0:T(1024)(128)(4,1)}, u32[]{:S(2)}) copy-start(pred[576]{0:T(1024)(128)(4,1)} %copy-done.100) | copy-start | bytes 1732
  500.3 39.8 %all-to-all-start.14 = ((bf16[4,1,3,64,384]{4,3,2,1,0:T(8,128)(2,1)}), bf16[4,1,3,64,384]{4,3,2,1,0:T(8,128)(2,1)}, u32[]{:S(2)}, u32[]{:S(2)}) async-start(bf16[4,1,3,64,384]{4,3,2,1,0:T(8,128)(2,1)} %bitcast.157), calls=%async_computation.14 | async-start | bytes 1179648 | tf_op jit(solution)/shard_map/all_to_all | solution.py:337
  505.1 119.8 %reduce-scatter.7.cloned.1.call-start = ((), (), s32[]{:S(2)}) async-start(), calls=%async_computation.20 | async-start | bytes 1105920
  568.8 58.5 %reduce-scatter.9.cloned.1.call-start = ((), (), s32[]{:S(2)}) async-start(), calls=%async_computation.21 | async-start | bytes 1105920
  595.5 195.2 %all-reduce.18.cloned.1.call-start = ((), (), s32[]{:S(2)}) async-start(), calls=%async_computation.22 | async-start | bytes 2359296
  630.6 334.5 %all-reduce.20.cloned.1.call-start = ((), (), s32[]{:S(2)}) async-start(), calls=%async_computation.23 | async-start | bytes 35389440
  674.5 22.3 %copy-start.52 = (bf16[144,384]{1,0:T(8,128)(2,1)S(1)}, bf16[144,384]{1,0:T(8,128)(2,1)}, u32[]{:S(2)}) copy-start(bf16[144,384]{1,0:T(8,128)(2,1)} %copy-done.51) | copy-start | bytes 331780
  674.5 22.7 %copy-start.54 = (bf16[144,384]{1,0:T(8,128)(2,1)S(1)}, bf16[144,384]{1,0:T(8,128)(2,1)}, u32[]{:S(2)}) copy-start(bf16[144,384]{1,0:T(8,128)(2,1)} %copy-done.53) | copy-start | bytes 331780
  674.5 23.9 %copy-start.91 = (s32[1024]{0:T(1024)S(1)}, s32[1024]{0:T(1024)}, u32[]{:S(2)}) copy-start(s32[1024]{0:T(1024)} %copy-done.90) | copy-start | bytes 12292
  677.4 15.7 %all-to-all-start.11 = ((bf16[4,1,3,64,384]{4,3,2,1,0:T(8,128)(2,1)}), bf16[4,1,3,64,384]{4,3,2,1,0:T(8,128)(2,1)S(1)}, u32[]{:S(2)}, u32[]{:S(2)}) async-start(bf16[4,1,3,64,384]{4,3,2,1,0:T(8,128)(2,1)} %copy.568), calls=%async_computation.11 | async-start | bytes 1179648 | tf_op jit(solution)/shard_map/all_to_all | solution.py:400
  693.1 12.2 %all-to-all-start.15 = ((bf16[4,1,3,64,384]{4,3,2,1,0:T(8,128)(2,1)}), bf16[4,1,3,64,384]{4,3,2,1,0:T(8,128)(2,1)S(1)}, u32[]{:S(2)}, u32[]{:S(2)}) async-start(bf16[4,1,3,64,384]{4,3,2,1,0:T(8,128)(2,1)} %copy.588), calls=%async_computation.15 | async-start | bytes 1179648 | tf_op jit(solution)/shard_map/all_to_all | solution.py:400
  705.3 84.4 %copy-start.48 = (f32[144,384]{1,0:T(8,128)S(1)}, f32[144,384]{1,0:T(8,128)}, u32[]{:S(2)}) copy-start(f32[144,384]{1,0:T(8,128)} %get-tuple-element.68) | copy-start | bytes 663556
  708.5 81.2 %copy-start.131 = (f32[144]{0:T(256)S(1)}, f32[144]{0:T(256)}, u32[]{:S(2)}) copy-start(f32[144]{0:T(256)} %copy-done.129) | copy-start | bytes 1732
  (114 other events, 886.9 us)
Sparse Core Ops, SparseCore 0:
  10.9 53.6 all-gather.5
  98.7 45.1 all-gather.7
  569.0 25.0 reduce-scatter.6
  596.4 24.2 reduce-scatter.8
  630.7 150.4 all-reduce.17
  785.5 179.5 all-reduce.19
where the time goes:
time: 989 us; the launch traced here: 977 us
  local copies, waits for them, and re-layouts  225 us (23%)
  matrix products  192 us (19%)
  waiting for transfers between devices  191 us (19%)
  blocking collectives  168 us (17%)
  other arithmetic  111 us (11%)
  starting transfers between devices  72.3 us (7%)
  between operations  18.5 us (2%)
    unnamed x10, waiting for transfers between devices  174 us
    unnamed x1, blocking collectives  72.2 us
    all_gather x1, blocking collectives, rows_first(): out, at, finished = (lax.all_gather(both, axis, axis=0, tiled=True), 0, [])  63.7 us
    unnamed x334, local copies, waits for them, and re-layouts  38.3 us
    scatter x4, other arithmetic, dispatch(): buffer.at[target].set(flat_rows)  32.5 us
    all_gather x2, blocking collectives, micro_step(): lax.all_gather(key_values.reshape(image_count, slots_here, 2 * att_width)...  32 us
    dot_general x2, matrix products, micro_step(): jnp.einsum('siecf,siecd->efd', hidden, arrived_grad_mlp, preferred_elemen...  27.8 us
    dot_general x2, matrix products, micro_step(): jnp.einsum('siecd,efd->siecf', arrived_grad_mlp, down_full, preferred_ele...  27.4 us
  transfers between devices with their start and end apart: 22, of which 6 were waited for; matrix products, arithmetic and copies ran while one was open for 47% of the time, Pallas kernels for 0%

commit v1 on v0

v1 whole, which is shorter than its diff:
```python
import jax
import jax.numpy as jnp
from jax import lax
from jax.experimental import pallas as pl
from jax.experimental.pallas import tpu as pltpu
from jax.sharding import Mesh, PartitionSpec as P

BF = jnp.bfloat16
F32 = jnp.float32
EPSILON = 1e-06
MASKED = -1e30
MB, NX, SQ, SLOTS, D = 2, 4, 144, 576, 384
EXP, CAP, HEADS, FF = 3, 256, 6, 1536
PACK = 160
TOKS = ("z", "y", "c")
VMEM = 62 * 1024 * 1024


def params(n):
    return pltpu.CompilerParams(
        dimension_semantics=("arbitrary",) * n, vmem_limit_bytes=VMEM
    )


def dot(a, b):
    return jnp.dot(a, b, preferred_element_type=F32)


def dot_nt(a, b):
    return lax.dot_general(a, b, (((1,), (1,)), ((), ())), preferred_element_type=F32)


def dot_tn(a, b):
    return lax.dot_general(a, b, (((0,), (0,)), ((), ())), preferred_element_type=F32)


def iota(shape, dim):
    return lax.broadcasted_iota(jnp.int32, shape, dim)


def hot(cond):
    return jnp.where(cond, 1.0, 0.0).astype(BF)


def eye(n):
    return hot(iota((n, n), 0) == iota((n, n), 1))


def flip(a):
    return dot_nt(eye(a.shape[1]), a)


def tok_of(place, sc):
    z = (sc[2] + (place & 3)) & 3
    y = (sc[3] + ((place >> 2) & 3)) & 3
    c = (sc[1] + (place >> 4)) & 1
    return z * 8 + y * 2 + c


def third(v):
    return (v * 11) >> 5


def padded_feature(col, sc):
    r = col & 15
    feature = tok_of(col >> 4, sc) * 12 + r
    return jnp.where(r < 12, feature, -1)


def canonical_feature(col):
    r = col & 15
    return jnp.where(r < 12, (col >> 4) * 12 + r, -1)


def native_lane(sc):
    j = iota((1, 128), 1)
    n = j + 3 * sc[0]
    n = jnp.where(n >= 12, n - 12, n)
    return jnp.where(j < 12, n, -1)


def router_turn(sc, offset):
    n = native_lane(sc)
    return hot((iota((128, 128), 0) == n + offset) & (n >= 0))


def norm_parts(x):
    mu = jnp.mean(x, -1, keepdims=True)
    c = x - mu
    var = jnp.mean(c * c, -1, keepdims=True)
    inv = lax.rsqrt(var + EPSILON)
    return c * inv, inv


def norm_back(grad, normed, inv, gain):
    u = grad * gain
    a = jnp.mean(u, -1, keepdims=True)
    b = jnp.mean(u * normed, -1, keepdims=True)
    return (u - a - normed * b) * inv


def routing(rcol, first, x, router, sc):
    nat = native_lane(sc).astype(F32)
    member = jnp.zeros((SLOTS, 128), F32)
    for k in range(4):
        member = member + jnp.where(rcol[:, first + k : first + k + 1] == nat, 1.0, 0.0)
    inside = member > 0.5
    logits = jnp.where(inside, dot(x, router), MASKED)
    top = jnp.max(logits, -1, keepdims=True)
    ex = jnp.where(inside, jnp.exp(logits - top), 0.0)
    gates = ex / jnp.sum(ex, -1, keepdims=True)
    mb = member.astype(BF)
    lower = hot(iota((SLOTS, SLOTS), 1) < iota((SLOTS, SLOTS), 0))
    mt = dot_nt(hot(iota((16, 128), 0) == iota((16, 128), 1)), mb)
    posc = jnp.where(inside, dot(lower, mb), -1.0)
    posr = jnp.where(mt > 0.5, dot_nt(mt.astype(BF), lower), -1.0)
    return gates, posc, posr


def route_columns(refs, m):
    unit = hot(iota((SQ, 256), 0) == iota((SQ, 256), 1))
    return jnp.concatenate([dot_nt(unit, r[m, SQ:PACK, 0:256]) for r in refs], 0)


def gate_lanes(gates):
    hi = gates.astype(BF).astype(F32)
    lo = pltpu.roll(gates - hi, 64, 1)
    return jnp.where(iota(gates.shape, 1) < 64, hi, lo).astype(BF)


def pick(ext, e):
    lane = iota(ext.shape, 1)
    return jnp.sum(jnp.where((lane == e) | (lane == 64 + e), ext, 0.0), -1, keepdims=True)


def split_lanes(col, e):
    hi = col.astype(BF).astype(F32)
    lane = iota((col.shape[0], 128), 1)
    both = jnp.where(lane == e, hi, 0.0) + jnp.where(lane == 64 + e, col - hi, 0.0)
    return both.astype(BF)


def gather_matrix(row):
    return hot(row == iota((CAP, SLOTS), 0).astype(F32))


def scatter_matrix(posc, e):
    col = jnp.sum(jnp.where(iota(posc.shape, 1) == e, posc, 0.0), -1, keepdims=True)
    return hot(col == iota((SLOTS, CAP), 1).astype(F32))


def router_grad(gates, lanes):
    t = lanes + pltpu.roll(lanes, 64, 1)
    inner = jnp.sum(gates * t, -1, keepdims=True)
    return (gates * (t - inner)).astype(BF)


def smem():
    return pl.BlockSpec(memory_space=pltpu.SMEM)


def full(shape):
    return pl.BlockSpec(shape, lambda *_: (0,) * len(shape))


def sds(shape, dtype):
    return jax.ShapeDtypeStruct(shape, dtype)


def prep_kernel(sc, w0, w1, wq, wo, wkv, wkvt, sm, vec):
    col = iota((1, 512), 1)
    take = hot(iota((D, 512), 0) == padded_feature(col, sc))
    for e in range(EXP):
        rows = jnp.concatenate(
            [w[:, 16 * e : 16 * e + 16, 0:768].reshape(256, 768) for w in (w0, w1)], 0
        )
        nat = dot(take, rows).astype(BF)
        wq[e] = nat[:, :D]
        wo[e] = nat[:, D:]
    k = iota((1, 1536), 1)
    place = (k * 1366) >> 16
    r48 = k - place * 48
    base = tok_of(place, sc) * 12

    def feature(idx, ok):
        s = third(idx)
        return jnp.where(ok, base + ((sc[0] + s) & 3) * 3 + idx - 3 * s, -1)

    r16 = r48 & 15
    kv_feature = feature((r48 >> 4) * 4 + r16 - 12, r16 >= 12)
    sm_feature = feature(r48, r48 < 12)
    everything = jnp.concatenate([w[...].reshape(768, 896) for w in (w0, w1)], 0)
    d = iota((D, 1536), 0)
    kv = dot(hot(d == kv_feature), everything[:, :768]).astype(BF)
    wkv[...] = kv
    wkvt[...] = flip(kv).astype(BF)
    small = dot(hot(d == sm_feature), everything[:, 768:]).astype(BF)
    sm[...] = small
    vec[...] = dot_nt(hot(iota((8, 128), 1) == iota((8, 128), 0) + 24), small)


def prep(sc, w0, w1):
    return pl.pallas_call(
        prep_kernel,
        grid=(1,),
        in_specs=[smem(), full((16, 48, 896)), full((16, 48, 896))],
        out_specs=[
            full((EXP, D, D)),
            full((EXP, D, D)),
            full((D, 768)),
            full((768, D)),
            full((D, 128)),
            full((8, D)),
        ],
        out_shape=[
            sds((EXP, D, D), BF),
            sds((EXP, D, D), BF),
            sds((D, 768), BF),
            sds((768, D), BF),
            sds((D, 128), BF),
            sds((8, D), F32),
        ],
        compiler_params=params(1),
        name="prep",
    )(sc, w0, w1)


def attend_kernel(
    sc, t0, t1, t2, t3, wq, wo, wkv, wkvt, sm, vec,
    o0, o1, o2, o3, xo, kvo, kto, gateo, poso, posco, rowso, qo, atto, bro, grow, pro,
    xe, acc,
):
    m, e = pl.program_id(0), pl.program_id(1)
    toks = (t0, t1, t2, t3)

    @pl.when(e == 0)
    def _():
        x = jnp.concatenate([t[0, 0:SQ, :].astype(F32) for t in toks], 0)
        n, _ = norm_parts(x)
        a = (n * vec[0:1, :] + vec[1:2, :]).astype(BF)
        xo[0] = a
        router = dot(sm[...], router_turn(sc, 0)).astype(BF)
        gates, posc, posr = routing(route_columns(toks, 0), 0, a, router, sc)
        gateo[0] = gates
        posco[0] = posc
        poso[0] = posr
        xe[:, 0:D] = a
        xe[:, D:512] = gate_lanes(gates)
        kvo[0] = dot(a, wkv[...]).astype(BF)
        kto[0] = dot_nt(wkvt[...], a).astype(BF)
        acc[...] = jnp.zeros_like(acc)

    g = gather_matrix(poso[0, pl.ds(e, 1), :])
    ext = dot(g, xe[...])
    rows = ext[:, 0:D].astype(BF)
    gate = pick(ext[:, D:512], e)
    rowso[0, 0] = rows
    grow[0, 0] = jnp.broadcast_to(gate, (CAP, 128))
    q = dot(rows, wq[0]).astype(BF)
    qo[0, 0] = q
    qs = q * jnp.asarray(0.125, BF)
    slot = iota((1, SLOTS), 1) + SQ * sc[0]
    slot = jnp.where(slot >= SLOTS, slot - SLOTS, slot)
    bias = jnp.where(slot < sc[4 + m], 0.0, MASKED)
    half = iota((CAP, 128), 1) < 64
    zero = jnp.zeros((CAP, 128), BF)
    for hp in range(3):
        span = slice(128 * hp, 128 * hp + 128)
        qp = qs[:, span]
        kt = kto[0, 128 * hp : 128 * hp + 128, :]
        v = kvo[0, :, D + 128 * hp : D + 128 * hp + 128]
        outs = []
        for side in range(2):
            mine = half if side == 0 else ~half
            s = dot(jnp.where(mine, qp, zero), kt) + bias
            ex = jnp.exp(s - jnp.max(s, -1, keepdims=True))
            p = (ex * (1.0 / jnp.sum(ex, -1, keepdims=True))).astype(BF)
            pro[0, 0, 2 * hp + side] = p
            outs.append(dot(p, v))
        atto[0, 0, :, span] = jnp.where(half, outs[0], outs[1]).astype(BF)
    br = dot(atto[0, 0], wo[0]).astype(BF)
    bro[0, 0] = br
    acc[...] += dot(scatter_matrix(posco[0], e), (gate * br.astype(F32)).astype(BF))

    @pl.when(e == EXP - 1)
    def _():
        for s, o in enumerate((o0, o1, o2, o3)):
            o[0] = acc[SQ * s : SQ * s + SQ, :].astype(BF)


def per_m(*shape):
    return pl.BlockSpec((1,) + shape, lambda m, e: (m,) + (0,) * len(shape))


def per_me(*shape):
    return pl.BlockSpec((1, 1) + shape, lambda m, e: (m, e) + (0,) * len(shape))


def per_e(*shape):
    return pl.BlockSpec((1,) + shape, lambda m, e: (e,) + (0,) * len(shape))


def attend(sc, toks, weights):
    saved = [
        (per_m(SLOTS, D), sds((MB, SLOTS, D), BF)),
        (per_m(SLOTS, 768), sds((MB, SLOTS, 768), BF)),
        (per_m(768, SLOTS), sds((MB, 768, SLOTS), BF)),
        (per_m(SLOTS, 128), sds((MB, SLOTS, 128), F32)),
        (per_m(16, SLOTS), sds((MB, 16, SLOTS), F32)),
        (per_m(SLOTS, 128), sds((MB, SLOTS, 128), F32)),
        (per_me(CAP, D), sds((MB, EXP, CAP, D), BF)),
        (per_me(CAP, D), sds((MB, EXP, CAP, D), BF)),
        (per_me(CAP, D), sds((MB, EXP, CAP, D), BF)),
        (per_me(CAP, D), sds((MB, EXP, CAP, D), BF)),
        (per_me(CAP, 128), sds((MB, EXP, CAP, 128), F32)),
        (per_me(HEADS, CAP, SLOTS), sds((MB, EXP, HEADS, CAP, SLOTS), BF)),
    ]
    piece = [(per_m(SQ, D), sds((MB, SQ, D), BF))] * 4
    out = pl.pallas_call(
        attend_kernel,
        grid=(MB, EXP),
        in_specs=[smem()]
        + [per_m(PACK, D)] * 4
        + [per_e(D, D), per_e(D, D), full((D, 768)), full((768, D)), full((D, 128)), full((8, D))],
        out_specs=[p[0] for p in piece + saved],
        out_shape=[p[1] for p in piece + saved],
        scratch_shapes=[pltpu.VMEM((SLOTS, 512), BF), pltpu.VMEM((SLOTS, D), F32)],
        compiler_params=params(2),
        name="attend",
    )(sc, *toks, *weights)
    return out[:4], out[4:]


def mix_kernel(t, p0, p1, p2, p3, vec, mixed, mlp_in):
    for m in range(MB):
        x = t[m].astype(F32)
        for p in (p0, p1, p2, p3):
            x = x + p[m].astype(F32)
        mixed[m] = x
        n, _ = norm_parts(x)
        mlp_in[m] = (n * vec[2:3, :] + vec[3:4, :]).astype(BF)


def mix(tokens, parts, vec):
    shape = (MB, SQ, D)
    return pl.pallas_call(
        mix_kernel,
        grid=(1,),
        in_specs=[full(shape)] * 5 + [full((8, D))],
        out_specs=[full(shape)] * 2,
        out_shape=[sds(shape, F32), sds(shape, BF)],
        compiler_params=params(1),
        name="mix",
    )(tokens, *parts, vec)


def gelu_both(v):
    a = jnp.abs(v)
    t = 1.0 / (1.0 + (0.3275911 * 0.7071067811865476) * a)
    ex = jnp.exp(-0.5 * (v * v))
    poly = 0.5 * 1.061405429
    for c in (-1.453152027, 1.421413741, -0.284496736, 0.254829592):
        poly = poly * t + 0.5 * c
    tail = poly * t * ex
    phi = jnp.where(v < 0, tail, 1.0 - tail)
    return v * phi, phi + v * (ex * 0.3989422804014327)


FC = 256


def experts_kernel(
    sc, x0, x1, x2, x3, g0, g1, g2, g3, t0, t1, t2, t3, sm, up, down,
    oo0, oo1, oo2, oo3, og0, og1, og2, og3, rmlp, rowso, gbo, hido, gpo,
    xe, gin, gates, posr, posc, acco, accg,
):
    e = pl.program_id(0)
    router = None

    @pl.when(e == 0)
    def _():
        turn = dot(sm[...], router_turn(sc, 12)).astype(BF)
        pad = hot(iota((D, 512), 0) == canonical_feature(iota((1, 512), 1)))
        for m in range(MB):
            a = jnp.concatenate([x[m] for x in (x0, x1, x2, x3)], 0)
            gt, pc, pr = routing(route_columns((t0, t1, t2, t3), m), 4, a, turn, sc)
            gates[m] = gt
            posc[m] = pc
            posr[m] = pr
            xe[m, :, 0:512] = dot(a, pad).astype(BF)
            xe[m, :, 512:640] = gate_lanes(gt)
            gin[m] = jnp.concatenate([g[m] for g in (g0, g1, g2, g3)], 0)
        acco[...] = jnp.zeros_like(acco)
        accg[...] = jnp.zeros_like(accg)

    exts, grs = [], []
    for m in range(MB):
        g = gather_matrix(posr[m, pl.ds(e, 1), :])
        exts.append(dot(g, xe[m]))
        grs.append(dot(g, gin[m]))
    ext = jnp.concatenate(exts, 0)
    gr = jnp.concatenate(grs, 0)
    rows = ext[:, 0:512].astype(BF)
    gate = pick(ext[:, 512:640], e)
    gb = (gate * gr).astype(BF)
    rowso[0] = rows
    gbo[0] = gb
    branch = jnp.zeros((512, D), F32)
    back = jnp.zeros((512, 512), F32)
    for c in range(FF // FC):
        span = slice(c * FC, c * FC + FC)
        w = up[:, :, span].reshape(512, FC)
        wd = down[...].reshape(FF, D)[span, :]
        act, slope = gelu_both(dot(rows, w))
        hid = act.astype(BF)
        gp = (dot_nt(gb, wd) * slope).astype(BF)
        hido[0, :, span] = hid
        gpo[0, :, span] = gp
        branch = branch + dot(hid, wd)
        back = back + dot_nt(gp, w)
    br = branch.astype(BF).astype(F32)
    t = jnp.sum(gr * br, -1, keepdims=True)
    scaled = (gate * br).astype(BF)
    lanes = split_lanes(t, e)
    backb = back.astype(BF)
    for m in range(MB):
        r = slice(CAP * m, CAP * m + CAP)
        sca = scatter_matrix(posc[m], e)
        acco[m] += dot(sca, jnp.concatenate([scaled[r], lanes[r]], 1))
        accg[m] += dot(sca, backb[r])

    @pl.when(e == EXP - 1)
    def _():
        turn = dot(sm[...], router_turn(sc, 12)).astype(BF)
        pad = hot(iota((D, 512), 0) == canonical_feature(iota((1, 512), 1)))
        total = jnp.zeros((D, 128), F32)
        for m in range(MB):
            dl = router_grad(gates[m], acco[m, :, D:512])
            a = jnp.concatenate([x[m] for x in (x0, x1, x2, x3)], 0)
            total = total + dot(flip(a).astype(BF), dl)
            part = dot_nt(accg[m].astype(BF), pad) + dot_nt(dl, turn)
            for s, (o, og) in enumerate(zip((oo0, oo1, oo2, oo3), (og0, og1, og2, og3))):
                r = slice(SQ * s, SQ * s + SQ)
                o[m] = acco[m, r, 0:D].astype(BF)
                og[m] = part[r].astype(BF)
        rmlp[...] = total


def experts(sc, xs, gs, toks, sm, wmlp):
    piece = (full((MB, SQ, D)), sds((MB, SQ, D), BF))

    def by_e(*shape):
        return pl.BlockSpec((1,) + shape, lambda e: (e,) + (0,) * len(shape))

    saved = [
        (full((D, 128)), sds((D, 128), F32)),
        (by_e(512, 512), sds((EXP, 512, 512), BF)),
        (by_e(512, D), sds((EXP, 512, D), BF)),
        (by_e(512, FF), sds((EXP, 512, FF), BF)),
        (by_e(512, FF), sds((EXP, 512, FF), BF)),
    ]
    outs = [piece] * 8 + saved
    got = pl.pallas_call(
        experts_kernel,
        grid=(EXP,),
        in_specs=[smem()]
        + [full((MB, SQ, D))] * 8
        + [full((MB, PACK, D))] * 4
        + [
            full((D, 128)),
            pl.BlockSpec((32, 16, FF), lambda e: (0, e, 0)),
            pl.BlockSpec((32, 48, D), lambda e: (0, 0, 4 + e)),
        ],
        out_specs=[o[0] for o in outs],
        out_shape=[o[1] for o in outs],
        scratch_shapes=[
            pltpu.VMEM((MB, SLOTS, 640), BF),
            pltpu.VMEM((MB, SLOTS, D), BF),
            pltpu.VMEM((MB, SLOTS, 128), F32),
            pltpu.VMEM((MB, 16, SLOTS), F32),
            pltpu.VMEM((MB, SLOTS, 128), F32),
            pltpu.VMEM((MB, SLOTS, 512), F32),
            pltpu.VMEM((MB, SLOTS, 512), F32),
        ],
        compiler_params=params(1),
        name="experts",
    )(sc, *xs, *gs, *toks, sm, wmlp, wmlp)
    return got[:4], got[4:8], got[8], got[9:]


def expert_grads_kernel(rows, gb, hid, gp, out):
    e = pl.program_id(0)
    du = dot_tn(rows[0], gp[0]).astype(BF)
    out[:, pl.ds(pl.multiple_of(16 * e, 16), 16), 0:FF] = du.reshape(32, 16, FF)
    dd = dot_tn(hid[0], gb[0]).astype(BF)
    out[:, :, pl.ds(pl.multiple_of(FF + D * e, 128), D)] = dd.reshape(32, 48, D)


def expert_grads(saved):
    def by_e(*shape):
        return pl.BlockSpec((1,) + shape, lambda e: (e,) + (0,) * len(shape))

    return pl.pallas_call(
        expert_grads_kernel,
        grid=(EXP,),
        in_specs=[by_e(512, 512), by_e(512, D), by_e(512, FF), by_e(512, FF)],
        out_specs=full((32, 48, 2688)),
        out_shape=sds((32, 48, 2688), BF),
        compiler_params=params(1),
        name="expert_grads",
    )(*saved)


def turn_kernel(mixed, cot, p0, p1, p2, p3, vec, gmix, gmixb, gv):
    rows = [jnp.zeros((1, D), F32)] * 2
    for m in range(MB):
        n, inv = norm_parts(mixed[m])
        grad = jnp.zeros((SQ, D), F32)
        for p in (p0, p1, p2, p3):
            grad = grad + p[m].astype(F32)
        gm = cot[m].astype(F32) + norm_back(grad, n, inv, vec[2:3, :])
        gmix[m] = gm
        gmixb[m] = gm.astype(BF)
        rows[0] = rows[0] + jnp.sum(grad * n, 0, keepdims=True)
        rows[1] = rows[1] + jnp.sum(grad, 0, keepdims=True)
    gv[...] = jnp.concatenate(rows + [jnp.zeros((6, D), F32)], 0)


def turn(mixed, cot, parts, vec):
    shape = (MB, SQ, D)
    return pl.pallas_call(
        turn_kernel,
        grid=(1,),
        in_specs=[full(shape)] * 6 + [full((8, D))],
        out_specs=[full(shape), full(shape), full((8, D))],
        out_shape=[sds(shape, F32), sds(shape, BF), sds((8, D), F32)],
        compiler_params=params(1),
        name="turn",
    )(mixed, cot, *parts, vec)


def attend_back_kernel(
    sc, g0, g1, g2, g3, t0, t1, t2, t3, x, kv, kt, gates, posr, posc, rows, q, att, br, grow, pro,
    wq, wo, wkvt, sm, vec, gv, rmlp,
    o0, o1, o2, o3, kvs, dqo0, dqo1,
    gin, acc, dkvt, dwq, dwo, dwkvt, dsm, dvec,
):
    m, e = pl.program_id(0), pl.program_id(1)

    @pl.when((m == 0) & (e == 0))
    def _():
        dwq[...] = jnp.zeros_like(dwq)
        dwo[...] = jnp.zeros_like(dwo)
        dwkvt[...] = jnp.zeros_like(dwkvt)
        dsm[...] = jnp.zeros_like(dsm)
        dvec[...] = jnp.zeros_like(dvec)

    @pl.when(e == 0)
    def _():
        gin[...] = jnp.concatenate([g[0] for g in (g0, g1, g2, g3)], 0)
        acc[...] = jnp.zeros_like(acc)
        dkvt[...] = jnp.zeros_like(dkvt)

    gr = dot(gather_matrix(posr[0, pl.ds(e, 1), :]), gin[...])
    gb = (grow[0, 0][:, 0:1] * gr).astype(BF)
    t = jnp.sum(gr * br[0, 0].astype(F32), -1, keepdims=True)
    dwo[e] += dot_tn(att[0, 0], gb)
    ga = dot_nt(gb, wo[0]).astype(BF)
    gat = flip(ga).astype(BF)
    qt = flip(q[0, 0] * jnp.asarray(0.125, BF)).astype(BF)
    half = iota((CAP, 128), 1) < 64
    zero = jnp.zeros((CAP, 128), BF)
    dqs = []
    for hp in range(3):
        span = slice(128 * hp, 128 * hp + 128)
        vt = kt[0, D + 128 * hp : D + 128 * hp + 128, :]
        k = kv[0, :, span]
        gap = ga[:, span]
        inner = gap.astype(F32) * att[0, 0, :, span].astype(F32)
        outs = []
        for side in range(2):
            h = 2 * hp + side
            mine = half if side == 0 else ~half
            p = pro[0, 0, h]
            dp = dot(jnp.where(mine, gap, zero), vt)
            ri = jnp.sum(jnp.where(mine, inner, 0.0), -1, keepdims=True)
            ds = (p.astype(F32) * (dp - ri)).astype(BF)
            outs.append(dot(ds, k))
            hs = slice(64 * h, 64 * h + 64)
            dkvt[hs, :] += dot(qt[hs, :], ds)
            vs = slice(D + 64 * h, D + 64 * h + 64)
            dkvt[vs, :] += dot(gat[hs, :], p)
        dqs.append((jnp.where(half, outs[0], outs[1]) * 0.125).astype(BF))
    dq = jnp.concatenate(dqs, 1)
    dwq[e] += dot_tn(rows[0, 0], dq)
    back = dot_nt(dq, wq[0]).astype(BF)
    acc[...] += dot(scatter_matrix(posc[0], e), jnp.concatenate([back, split_lanes(t, e)], 1))

    @pl.when(e == EXP - 1)
    def _():
        dl = router_grad(gates[0], acc[:, D:512])
        router = dot(sm[...], router_turn(sc, 0)).astype(BF)
        dkvb = dkvt[...].astype(BF)
        part = acc[:, 0:D] + dot_nt(dl, router) + dot(flip(dkvb).astype(BF), wkvt[...])
        tk = jnp.concatenate([r[0, 0:SQ, :].astype(F32) for r in (t0, t1, t2, t3)], 0)
        n, _ = norm_parts(tk)
        dvec[0:1, :] += jnp.sum(part * n, 0, keepdims=True)
        dvec[1:2, :] += jnp.sum(part, 0, keepdims=True)
        dsm[...] += dot(flip(x[0]).astype(BF), dl)
        dwkvt[...] += dot(dkvb, x[0])
        for s, o in enumerate((o0, o1, o2, o3)):
            o[0] = part[SQ * s : SQ * s + SQ].astype(BF)

    @pl.when((m == MB - 1) & (e == EXP - 1))
    def _():
        small = dot_nt(dsm[...].astype(BF), router_turn(sc, 0))
        small = small + dot_nt(rmlp[...].astype(BF), router_turn(sc, 12))
        vecs = jnp.concatenate(
            [jnp.zeros((24, D), F32), dvec[0:2, :], gv[0:2, :], jnp.zeros((100, D), F32)], 0
        ).astype(BF)
        small = (small + dot_nt(eye(D), vecs)).astype(BF)
        k = iota((D, 1), 0)
        s = (k >= 96).astype(jnp.int32) + (k >= 192).astype(jnp.int32) + (k >= 288).astype(jnp.int32)
        j = k - 96 * s
        place = (j * 171) >> 9
        feature = tok_of(place, sc) * 12 + ((sc[0] + s) & 3) * 3 + j - 3 * place
        perm = hot(feature == iota((D, D), 1))
        both = jnp.concatenate([dot_nt(perm, dwkvt[...].astype(BF)), dot(perm, small)], 1)
        kvs[...] = both.astype(BF).reshape(4, 96, 896)
        back_pad = hot(padded_feature(iota((512, 1), 0), sc) == iota((512, D), 1))
        for i in range(EXP):
            both = jnp.concatenate([dwq[i], dwo[i]], 1).astype(BF)
            wide = dot(back_pad, both).astype(BF).reshape(32, 16, 768)
            dqo0[:, 16 * i : 16 * i + 16, :] = wide[0:16]
            dqo1[:, 16 * i : 16 * i + 16, :] = wide[16:32]


def attend_back(sc, gs, toks, saved, wq, wo, wkvt, sm, vec, gv, rmlp):
    piece = [(per_m(SQ, D), sds((MB, SQ, D), BF))] * 4
    outs = piece + [
        (full((4, 96, 896)), sds((4, 96, 896), BF)),
        (full((16, 48, 768)), sds((16, 48, 768), BF)),
        (full((16, 48, 768)), sds((16, 48, 768), BF)),
    ]
    got = pl.pallas_call(
        attend_back_kernel,
        grid=(MB, EXP),
        in_specs=[smem()]
        + [per_m(SQ, D)] * 4
        + [per_m(PACK, D)] * 4
        + [
            per_m(SLOTS, D), per_m(SLOTS, 768), per_m(768, SLOTS), per_m(SLOTS, 128),
            per_m(16, SLOTS), per_m(SLOTS, 128), per_me(CAP, D), per_me(CAP, D), per_me(CAP, D),
            per_me(CAP, D), per_me(CAP, 128), per_me(HEADS, CAP, SLOTS),
            per_e(D, D), per_e(D, D), full((768, D)), full((D, 128)), full((8, D)), full((8, D)),
            full((D, 128)),
        ],
        out_specs=[o[0] for o in outs],
        out_shape=[o[1] for o in outs],
        scratch_shapes=[
            pltpu.VMEM((SLOTS, D), BF),
            pltpu.VMEM((SLOTS, 512), F32),
            pltpu.VMEM((768, SLOTS), F32),
            pltpu.VMEM((EXP, D, D), F32),
            pltpu.VMEM((EXP, D, D), F32),
            pltpu.VMEM((768, D), F32),
            pltpu.VMEM((D, 128), F32),
            pltpu.VMEM((8, D), F32),
        ],
        compiler_params=params(2),
        name="attend_back",
    )(sc, *gs, *toks, *saved, wq, wo, wkvt, sm, vec, gv, rmlp)
    return got[:4], got[4], got[5], got[6]


def finish_kernel(gmix, tokens, p0, p1, p2, p3, vec, out):
    for m in range(MB):
        n, inv = norm_parts(tokens[m].astype(F32))
        grad = jnp.zeros((SQ, D), F32)
        for p in (p0, p1, p2, p3):
            grad = grad + p[m].astype(F32)
        out[m] = (gmix[m] + norm_back(grad, n, inv, vec[0:1, :])).astype(BF)


def finish(gmix, tokens, parts, vec):
    shape = (MB, SQ, D)
    return pl.pallas_call(
        finish_kernel,
        grid=(1,),
        in_specs=[full(shape)] * 6 + [full((8, D))],
        out_specs=full(shape),
        out_shape=sds(shape, BF),
        compiler_params=params(1),
        name="finish",
    )(gmix, tokens, *parts, vec)


def place_kernel(k0, k1, k2, k3, d0, d1, o0, o1):
    total = jnp.zeros((96, 896), F32)
    for k in (k0, k1, k2, k3):
        total = total + k[...].astype(F32)
    total = total.astype(BF)
    for half, (d, o) in enumerate(((d0, o0), (d1, o1))):
        mine = total[48 * half : 48 * half + 48]
        row = iota((768, 1), 0)
        place = (row * 1366) >> 16
        r = row - 48 * place
        col = iota((768, 48), 1)
        kv = hot((col == place * 3 + r - 12) & (r >= 12) & (r < 15))
        sm = hot((col == place * 3 + r - 28) & (r >= 28) & (r < 31))
        wide = dot(kv, mine[:, 0:768])
        small = dot(sm, mine[:, 768:896])
        both = jnp.concatenate([wide[:, 0:128] + small, wide[:, 128:]], 1).reshape(16, 48, 768)
        o[...] = (both + d[...].astype(F32)).astype(BF)


def place(pieces, d0, d1):
    return pl.pallas_call(
        place_kernel,
        grid=(1,),
        in_specs=[full((96, 896))] * 4 + [full((16, 48, 768))] * 2,
        out_specs=[full((16, 48, 768))] * 2,
        out_shape=[sds((16, 48, 768), BF)] * 2,
        compiler_params=params(1),
        name="place",
    )(*pieces, d0, d1)


def shift(a, axis, s):
    n = lax.axis_size(axis)
    return lax.ppermute(a, axis, [(i, (i + s) % n) for i in range(n)])


def fetch(a, axis):
    n = lax.axis_size(axis)
    return [a] + [shift(a, axis, n - s) for s in range(1, n)]


def send(parts, axis):
    return [parts[0]] + [shift(parts[s], axis, s) for s in range(1, len(parts))]


def local(
    tokens, patch_counts, attn_routes, mlp_routes, gain1, bias1, gain2, bias2, wkv, rattn, rmlp,
    wq, wo, wup, wdown, cotangent,
):
    tokens = tokens.reshape(MB, SQ, D)
    cot = cotangent.reshape(MB, SQ, D)
    index = [lax.axis_index(a) for a in ("x", "c", "z", "y")]
    sc = jnp.stack(index + [patch_counts[0, 0], patch_counts[1, 0], 0, 0]).astype(jnp.int32)

    mlp_shard = jnp.concatenate(
        [
            jnp.pad(wup, ((0, 0), (0, 4), (0, 0))).reshape(48, FF),
            jnp.moveaxis(wdown, 0, 1).reshape(48, EXP * D),
        ],
        1,
    )
    wmlp = lax.all_gather(mlp_shard, TOKS, axis=0).reshape(32, 48, 2688)

    routes = jnp.concatenate([attn_routes, mlp_routes], -1).reshape(MB, SQ, 8)
    routes = jnp.moveaxis(routes, 1, 2).astype(BF)
    packed = jnp.concatenate([tokens, jnp.pad(routes, ((0, 0), (0, 8), (0, D - SQ)))], 1)
    vecs = jnp.stack([gain1, bias1, gain2, bias2], 1)
    shared = jnp.concatenate(
        [wkv, rattn, rmlp, vecs, jnp.zeros((3, 100), BF)], 1
    )
    kv12 = jnp.concatenate(fetch(shared, "x"), 0)
    toks = fetch(packed, "x")
    qo = jnp.concatenate([wq, wo], -1)
    qo = jnp.concatenate([qo, kv12[:, :768].reshape(3, 4, 768)], 1).reshape(48, 768)
    side = jnp.pad(kv12[:, 768:], ((0, 36), (0, 0)))
    shard = jnp.concatenate([qo, side], 1)
    zs = jnp.stack(fetch(shard, "z"))
    w0 = jnp.stack(fetch(zs, "y")).reshape(16, 48, 896)
    w1 = shift(w0, "c", 1)
    fq, fo, fkv, fkvt, sm, vec = prep(sc, w0, w1)

    parts, saved = attend(sc, toks, (fq, fo, fkv, fkvt, sm, vec))
    gs = fetch(cot, "x")
    mixed, mlp_in = mix(tokens, send(parts, "x"), vec)
    xs = fetch(mlp_in, "x")
    outp, gradp, rm, kept = experts(sc, xs, gs, toks, sm, wmlp)
    gradp = send(gradp, "x")
    outp = send(outp, "x")
    dmlp = expert_grads(kept)
    dmlp = lax.psum_scatter(dmlp, TOKS, scatter_dimension=0, tiled=True).reshape(48, 2688)
    gmix, gmixb, gv = turn(mixed, cot, gradp, vec)
    result = mixed
    for o in outp:
        result = result + o.astype(F32)
    result = result.astype(BF)
    gms = fetch(gmixb, "x")
    back, kvs, d0, d1 = attend_back(sc, gms, toks, saved, fq, fo, fkvt, sm, vec, gv, rm)
    kvp = send([kvs[s] for s in range(4)], "x")
    tokens_grad = finish(gmix, tokens, send(back, "x"), vec)
    e0, e1 = place(kvp, d0, d1)
    other = shift(e1, "c", 1)
    h = (e0.astype(F32) + other.astype(F32)).astype(BF).reshape(4, 4, 48, 768)
    h = sum(p.astype(F32) for p in send([h[s] for s in range(4)], "y")).astype(BF)
    tail = sum(p.astype(F32) for p in send([h[s] for s in range(4)], "z"))

    t3 = tail.reshape(3, 16, 768)
    small = tail[28:31]
    mlp = dmlp.astype(F32)
    dup = mlp[:, :FF].reshape(3, 16, FF)[:, :12]
    ddown = jnp.moveaxis(mlp[:, FF:].reshape(48, EXP, D), 1, 0)
    shape = (MB, 1, SQ, D)
    return (
        result.reshape(shape),
        tokens_grad.reshape(shape),
        small[:, 24],
        small[:, 25],
        small[:, 26],
        small[:, 27],
        tail[12:15],
        small[:, 0:12],
        small[:, 12:24],
        t3[:, :12, :D],
        t3[:, :12, D:],
        dup,
        ddown,
    )


def solution(mesh):
    fine = Mesh(mesh.devices.reshape(4, 4, 2, 4), ("z", "y", "c", "x"))
    every = TOKS + ("x",)
    act = P(None, TOKS, "x", None)
    row, mat, own = P(every), P(every, None), P("x", TOKS, None)
    return jax.shard_map(
        local,
        mesh=fine,
        in_specs=(
            act, P(None, TOKS), act, act, row, row, row, row, mat, mat, mat, own, own, own, own, act,
        ),
        out_specs=(act, act, row, row, row, row, mat, mat, mat, own, own, own, own),
        check_vma=False,
    )
```

time: 989 us -> 326 us (0.33)
  local copies, waits for them, and re-layouts: 225 us -> 20.4 us
  matrix products: 192 us -> 0 us
  blocking collectives: 168 us -> 0 us
  Pallas kernels: 0 us -> 134 us
  other arithmetic: 111 us -> 4.7 us
  waiting for transfers between devices: 191 us -> 87.5 us
  starting transfers between devices: 72.3 us -> 60.4 us
    dot_general x54 -> x0, matrix products: 192 us -> none  [the longest x2 27.8 us: micro_step(): jnp.einsum('siecf,siecd->efd', hidden, arrived_grad_mlp, preferred_elemen...]
    unnamed x10 -> x2, waiting for transfers between devices: 174 us -> 0.03 us
    pallas_call x0 -> x9, Pallas kernels: none -> 134 us  [the longest x1 36.4 us: attend_back(): pl.pallas_call(attend_back_kernel, grid=(MB, EXP), in_specs=[smem()] + [p...]
    all_gather x3 -> x0, blocking collectives: 95.8 us -> none  [the longest x1 63.7 us: rows_first(): out, at, finished = (lax.all_gather(both, axis, axis=0, tiled=True), 0, [])]
    ppermute x0 -> x44, waiting for transfers between devices: none -> 87.4 us  [shift(): return lax.ppermute(a, axis, [(i, (i + s) % n) for i in range(n)])]
    unnamed x1 -> x0, blocking collectives: 72.2 us -> none
    all_to_all x16 -> x0, starting transfers between devices: 72.1 us -> none  [the longest x2 10 us: micro_step(): lax.all_to_all(branch_mlp, 'exp', split_axis=0, concat_axis=0, tiled=True)]
    ppermute x0 -> x44, starting transfers between devices: none -> 60.3 us  [shift(): return lax.ppermute(a, axis, [(i, (i + s) % n) for i in range(n)])]
  transfers between devices with their start and end apart: 22 -> 46, of which waited for: 6 -> 27; matrix products, arithmetic and copies ran while one was open for 47% -> 4% of each run, Pallas kernels for 0% -> 28%
where the time goes in v1:
time: 326 us; the launch traced here: 321 us
  Pallas kernels  134 us (41%)
  waiting for transfers between devices  87.5 us (27%)
  starting transfers between devices  60.4 us (19%)
  local copies, waits for them, and re-layouts  20.4 us (6%)
  between operations  14.7 us (5%)
  other arithmetic  4.7 us (1%)
    ppermute x44, waiting for transfers between devices, shift(): return lax.ppermute(a, axis, [(i, (i + s) % n) for i in range(n)])  87.4 us
    ppermute x44, starting transfers between devices, shift(): return lax.ppermute(a, axis, [(i, (i + s) % n) for i in range(n)])  60.3 us
    pallas_call x1, Pallas kernels, attend_back(): pl.pallas_call(attend_back_kernel, grid=(MB, EXP), in_specs=[smem()] + [p...  36.4 us
    pallas_call x1, Pallas kernels, attend(): pl.pallas_call(attend_kernel, grid=(MB, EXP), in_specs=[smem()] + [per_m(...  36.2 us
    pallas_call x1, Pallas kernels, experts(): pl.pallas_call(experts_kernel, grid=(EXP,), in_specs=[smem()] + [full((MB...  32.4 us
    pallas_call x1, Pallas kernels, expert_grads(): pl.pallas_call(expert_grads_kernel, grid=(EXP,), in_specs=[by_e(512, 512)...  11.2 us
    unnamed x85, local copies, waits for them, and re-layouts  6.78 us
  transfers between devices with their start and end apart: 46, of which 27 were waited for; matrix products, arithmetic and copies ran while one was open for 4% of the time, Pallas kernels for 28%

profile of v1, /device:TPU:0, one launch (start us, length us, event | category | flops | bytes accessed | tf_op | source)
XLA Modules:
  0.0 321.4 jit_solution(14066467601627471513)
XLA Ops:
  7.2 0.9 copy.48
  8.2 0.9 pad.14
  13.7 1.6 collective-permute-start.5
  15.3 2.7 collective-permute-start.4
  18.0 1.4 collective-permute-start.3
  19.5 1.0 collective-permute-done.4
  20.5 1.2 collective-permute-done.3
  21.8 4.0 %collective-permute-start.7 = (bf16[48,896]{1,0:T(8,128)(2,1)S(1)}, bf16[48,896]{1,0:T(8,128)(2,1)S(1)}, u32[]{:S(2)}, u32[]{:S(2)}) collective-permute-start(bf16[48,896]{1,0:T(8,128)(2,1)S(1)} %get-tuple-element.158), channel_id=1, source_target_pairs={{0,64},{32,96},{64,0},{96,32},{1,65},{33,97},{65,1},{97,33},{2,66}... | collective-permute-start | bytes 258056 | tf_op jit(solution)/shard_map/ppermute | solution.py:731
  26.5 1.3 collective-permute-start.8
  27.8 2.3 collective-permute-done.7
  30.2 1.1 collective-permute-done.6
  31.2 1.3 collective-permute-done.8
  32.6 4.0 %collective-permute-start.10 = (bf16[4,48,896]{2,1,0:T(8,128)(2,1)S(1)}, bf16[4,48,896]{2,1,0:T(8,128)(2,1)S(1)}, u32[]{:S(2)}, u32[]{:S(2)}) collective-permute-start(bf16[4,48,896]{2,1,0:T(8,128)(2,1)S(1)} %get-tuple-element.149), channel_id=1, source_target_pairs={{0,16},{8,24},{16,0},{24,8},{1,17},{9,25},{17,1},{25,9},{2,18},{10... | collective-permute-start | bytes 1032200 | tf_op jit(solution)/shard_map/ppermute | solution.py:731
  36.6 1.1 collective-permute-start.9
  37.6 1.0 collective-permute-start.11
  38.6 6.9 %collective-permute-done.10 = bf16[4,48,896]{2,1,0:T(8,128)(2,1)S(1)} collective-permute-done((bf16[4,48,896]{2,1,0:T(8,128)(2,1)S(1)}, bf16[4,48,896]{2,1,0:T(8,128)(2,1)S(1)}, u32[]{:S(2)}, u32[]{:S(2)}) %collective-permute-start.10) | collective-permute-done | bytes 344096 | tf_op jit(solution)/shard_map/ppermute | solution.py:731
  45.6 5.3 %collective-permute-done.9 = bf16[4,48,896]{2,1,0:T(8,128)(2,1)S(1)} collective-permute-done((bf16[4,48,896]{2,1,0:T(8,128)(2,1)S(1)}, bf16[4,48,896]{2,1,0:T(8,128)(2,1)S(1)}, u32[]{:S(2)}, u32[]{:S(2)}) %collective-permute-start.9) | collective-permute-done | bytes 344096 | tf_op jit(solution)/shard_map/ppermute | solution.py:731
  52.9 3.5 %collective-permute-start.1 = (bf16[2,160,384]{2,1,0:T(8,128)(2,1)S(1)}, bf16[2,160,384]{2,1,0:T(8,128)(2,1)}, u32[]{:S(2)}, u32[]{:S(2)}) collective-permute-start(bf16[2,160,384]{2,1,0:T(8,128)(2,1)S(1)} %fusion.1.t0), channel_id=1, source_target_pairs={{0,2},{1,3},{2,0},{3,1},{4,6},{5,7},{6,4},{7,5},{8,10},{9,11},{10,... | collective-permute-start | bytes 737288 | tf_op jit(solution)/shard_map/ppermute | solution.py:731
  57.6 1.9 stack.61.sc
  59.5 5.8 %prep.1 = (bf16[3,384,384]{2,1,0:T(8,128)(2,1)}, bf16[3,384,384]{2,1,0:T(8,128)(2,1)}, bf16[384,768]{1,0:T(8,128)(2,1)}, bf16[768,384]{1,0:T(8,128)(2,1)}, bf16[384,128]{1,0:T(8,128)(2,1)}, /*index=5*/f32[8,384]{1,0:T(8,128)}) custom-call(s32[8]{0:T(128)} %stack.61.sc, bf16[16,48,896]{2,1,0:T(8,128)(2,1)} %bitcast.73, ...), custom_call_target="tpu_custom_call" | custom-call | tf_op jit(solution)/shard_map/prep/pallas_call | solution.py:203
  65.2 2.1 collective-permute-done.1.t2
  67.4 36.2 %attend.1 = (bf16[2,144,384]{2,1,0:T(8,128)(2,1)}, bf16[2,144,384]{2,1,0:T(8,128)(2,1)}, bf16[2,144,384]{2,1,0:T(8,128)(2,1)}, bf16[2,144,384]{2,1,0:T(8,128)(2,...) custom-call(s32[8]{0:T(128)} %stack.61.sc, ...), custom_call_target="tpu_custom_call" | custom-call | tf_op jit(solution)/shard_map/attend/pallas_call | solution.py:319
  103.6 1.1 collective-permute-start.13
  104.7 2.8 collective-permute-start.14
  108.1 1.5 collective-permute-start.21
  110.3 3.4 %collective-permute-done.13.p1 = bf16[2,144,384]{2,1,0:T(8,128)(2,1)S(1)} collective-permute-done((bf16[2,144,384]{2,1,0:T(8,128)(2,1)}, bf16[2,144,384]{2,1,0:T(8,128)(2,1)S(1)}, u32[]{:S(2)}, u32[]{:S(2)}) %collective-permute-start.13) | collective-permute-done | bytes 221216 | tf_op jit(solution)/shard_map/ppermute | solution.py:731
  114.5 4.2 %collective-permute-done.14.p2 = bf16[2,144,384]{2,1,0:T(8,128)(2,1)S(1)} collective-permute-done((bf16[2,144,384]{2,1,0:T(8,128)(2,1)}, bf16[2,144,384]{2,1,0:T(8,128)(2,1)S(1)}, u32[]{:S(2)}, u32[]{:S(2)}) %collective-permute-start.14) | collective-permute-done | bytes 221216 | tf_op jit(solution)/shard_map/ppermute | solution.py:731
  119.7 2.4 mix.1
  122.1 1.3 collective-permute-start.18
  123.4 2.9 collective-permute-start.17
  127.8 5.0 %collective-permute-done.18.x3 = bf16[2,144,384]{2,1,0:T(8,128)(2,1)S(1)} collective-permute-done((bf16[2,144,384]{2,1,0:T(8,128)(2,1)}, bf16[2,144,384]{2,1,0:T(8,128)(2,1)S(1)}, u32[]{:S(2)}, u32[]{:S(2)}) %collective-permute-start.18) | collective-permute-done | bytes 221216 | tf_op jit(solution)/shard_map/ppermute | solution.py:731
  132.8 4.0 %collective-permute-done.17.x2 = bf16[2,144,384]{2,1,0:T(8,128)(2,1)S(1)} collective-permute-done((bf16[2,144,384]{2,1,0:T(8,128)(2,1)}, bf16[2,144,384]{2,1,0:T(8,128)(2,1)S(1)}, u32[]{:S(2)}, u32[]{:S(2)}) %collective-permute-start.17) | collective-permute-done | bytes 221216 | tf_op jit(solution)/shard_map/ppermute | solution.py:731
  137.6 32.4 %experts.1 = (bf16[2,144,384]{2,1,0:T(8,128)(2,1)}, bf16[2,144,384]{2,1,0:T(8,128)(2,1)}, bf16[2,144,384]{2,1,0:T(8,128)(2,1)}, bf16[2,144,384]{2,1,0:T(8,128)(2...) custom-call(s32[8]{0:T(128)} %stack.61.sc, ...), custom_call_target="tpu_custom_call" | custom-call | tf_op jit(solution)/shard_map/experts/pallas_call | solution.py:463
  169.9 11.2 %expert_grads.1 = bf16[32,48,2688]{2,1,0:T(8,128)(2,1)} custom-call(bf16[3,512,512]{2,1,0:T(8,128)(2,1)} %get-tuple-element.107.rows, bf16[3,512,384]{2,1,0:T(8,128)(2,1)} %get-tuple-element.108.gb, bf16[3,512,1536]{2,1,0:T(8,128)(2,1)} %get-tuple-element.109.hid, bf16[3,512,1536]{2,1,0:T(8,128)(2,1)} %get-tuple-element.110.gp), custom_call_target="tpu_custom_call" | custom-call | tf_op jit(solution)/shard_map/expert_grads/pallas_call | solution.py:503
  181.2 0.9 copy-done.41
  182.8 2.9 collective-permute-start.26
  186.2 3.8 %collective-permute-done.25.p1 = bf16[2,144,384]{2,1,0:T(8,128)(2,1)S(1)} collective-permute-done((bf16[2,144,384]{2,1,0:T(8,128)(2,1)S(1)}, bf16[2,144,384]{2,1,0:T(8,128)(2,1)S(1)}, u32[]{:S(2)}, u32[]{:S(2)}) %collective-permute-start.25) | collective-permute-done | bytes 221216 | tf_op jit(solution)/shard_map/ppermute | solution.py:731
  190.0 5.7 %collective-permute-done.26.p2 = bf16[2,144,384]{2,1,0:T(8,128)(2,1)S(1)} collective-permute-done((bf16[2,144,384]{2,1,0:T(8,128)(2,1)S(1)}, bf16[2,144,384]{2,1,0:T(8,128)(2,1)S(1)}, u32[]{:S(2)}, u32[]{:S(2)}) %collective-permute-start.26) | collective-permute-done | bytes 221216 | tf_op jit(solution)/shard_map/ppermute | solution.py:731
  196.5 2.8 turn.1
  199.9 3.1 collective-permute-start.29
  203.1 4.2 %collective-permute-done.30.g3 = bf16[2,144,384]{2,1,0:T(8,128)(2,1)S(1)} collective-permute-done((bf16[2,144,384]{2,1,0:T(8,128)(2,1)}, bf16[2,144,384]{2,1,0:T(8,128)(2,1)S(1)}, u32[]{:S(2)}, u32[]{:S(2)}) %collective-permute-start.30) | collective-permute-done | bytes 221216 | tf_op jit(solution)/shard_map/ppermute | solution.py:731
  207.3 5.9 %collective-permute-done.29.g2 = bf16[2,144,384]{2,1,0:T(8,128)(2,1)S(1)} collective-permute-done((bf16[2,144,384]{2,1,0:T(8,128)(2,1)}, bf16[2,144,384]{2,1,0:T(8,128)(2,1)S(1)}, u32[]{:S(2)}, u32[]{:S(2)}) %collective-permute-start.29) | collective-permute-done | bytes 221216 | tf_op jit(solution)/shard_map/ppermute | solution.py:731
  214.0 36.4 %attend_back.1 = (bf16[2,144,384]{2,1,0:T(8,128)(2,1)}, bf16[2,144,384]{2,1,0:T(8,128)(2,1)}, bf16[2,144,384]{2,1,0:T(8,128)(2,1)}, bf16[2,144,384]{2,1,0:T(8,12...) custom-call(s32[8]{0:T(128)} %stack.61.sc, ...), custom_call_target="tpu_custom_call" | custom-call | tf_op jit(solution)/shard_map/attend_back/pallas_call | solution.py:645
  250.4 1.9 slice_bitcast_fusion
  252.2 2.2 collective-permute-start.36
  255.3 6.6 %collective-permute-done.36.k3 = bf16[96,896]{1,0:T(8,128)(2,1)S(1)} collective-permute-done((bf16[96,896]{1,0:T(8,128)(2,1)S(1)}, bf16[96,896]{1,0:T(8,128)(2,1)S(1)}, u32[]{:S(2)}, u32[]{:S(2)}) %collective-permute-start.36) | collective-permute-done | bytes 172064 | tf_op jit(solution)/shard_map/ppermute | solution.py:731
  261.9 1.3 collective-permute-done.35.k2
  263.2 2.3 collective-permute-done.34.k1
  266.2 4.1 %place.1 = (bf16[16,48,768]{2,1,0:T(8,128)(2,1)}, bf16[16,48,768]{2,1,0:T(8,128)(2,1)}) custom-call(bf16[96,896]{1,0:T(8,128)(2,1)} %get-tuple-element.147.k0, bf16[96,896]{1,0:T(8,128)(2,1)} %copy-done.27, bf16[96,896]{1,0:T(8,128)(2,1)} %copy-done.26, bf16[96,896]{1,0:T(8,128)(2,1)} %copy-done.25, bf16[16,48,768]{2,1,0:T(8,128)(2,1)} %get-tuple-element.103.d0, ...), custom_call_target="tpu_custom_call" | custom-call | tf_op jit(solution)/shard_map/place/pallas_call | solution.py:718
  270.2 3.1 collective-permute-done.37
  273.3 1.6 add_convert_fusion
  275.0 0.9 collective-permute-start.38
  275.9 2.4 collective-permute-start.40
  278.3 0.9 collective-permute-start.39
  279.4 2.2 collective-permute-start.23
  281.6 3.9 %collective-permute-done.38 = bf16[4,48,768]{2,1,0:T(8,128)(2,1)S(1)} collective-permute-done((bf16[4,48,768]{2,1,0:T(8,128)(2,1)S(1)}, bf16[4,48,768]{2,1,0:T(8,128)(2,1)S(1)}, u32[]{:S(2)}, u32[]{:S(2)}) %collective-permute-start.38) | collective-permute-done | bytes 294944 | tf_op jit(solution)/shard_map/ppermute | solution.py:731
  286.0 5.0 %collective-permute-done.40 = bf16[4,48,768]{2,1,0:T(8,128)(2,1)S(1)} collective-permute-done((bf16[4,48,768]{2,1,0:T(8,128)(2,1)S(1)}, bf16[4,48,768]{2,1,0:T(8,128)(2,1)S(1)}, u32[]{:S(2)}, u32[]{:S(2)}) %collective-permute-start.40) | collective-permute-done | bytes 294944 | tf_op jit(solution)/shard_map/ppermute | solution.py:731
  291.0 1.3 collective-permute-done.39
  293.3 1.2 collective-permute-start.33
  295.2 2.6 collective-permute-start.43
  297.7 5.1 %collective-permute-done.31.p1 = bf16[2,144,384]{2,1,0:T(8,128)(2,1)S(1)} collective-permute-done((bf16[2,144,384]{2,1,0:T(8,128)(2,1)S(1)}, bf16[2,144,384]{2,1,0:T(8,128)(2,1)S(1)}, u32[]{:S(2)}, u32[]{:S(2)}) %collective-permute-start.31) | collective-permute-done | bytes 221216 | tf_op jit(solution)/shard_map/ppermute | solution.py:731
  302.8 2.1 collective-permute-start.42
  306.5 2.5 finish.1
  311.7 1.0 bitcast_convert_fusion
  (162 shorter events, 27.3 us)
Async XLA Ops:
  7.2 14.6 %copy-start.28 = (bf16[3,12,384]{2,1,0:T(8,128)(2,1)S(1)}, bf16[3,12,384]{2,1,0:T(8,128)(2,1)}, u32[]{:S(2)}) copy-start(bf16[3,12,384]{2,1,0:T(8,128)(2,1)} %param.28) | copy-start | bytes 82948
  7.2 14.6 %copy-start.29 = (bf16[3,12,384]{2,1,0:T(8,128)(2,1)S(1)}, bf16[3,12,384]{2,1,0:T(8,128)(2,1)}, u32[]{:S(2)}) copy-start(bf16[3,12,384]{2,1,0:T(8,128)(2,1)} %param.27) | copy-start | bytes 82948
  7.2 129.6 %all-gather.3.cloned.1.call-start = ((), (), s32[]{:S(2)}) async-start(), calls=%async_computation.2 | async-start | bytes 8515584 | tf_op jit(solution)/shard_map/all_gather | solution.py:759
  9.8 301.9 %reduce-scatter.2.cloned.1.call-start = ((), (), s32[]{:S(2)}) async-start(), calls=%async_computation.1 | async-start | bytes 8515584 | tf_op jit(solution)/shard_map/reduce_scatter | solution.py:787
  13.7 5.8 %collective-permute-start.5 = (bf16[3,896]{1,0:T(4,128)(2,1)S(1)}, bf16[3,896]{1,0:T(4,128)(2,1)S(1)}, u32[]{:S(2)}, u32[]{:S(2)}) collective-permute-start(bf16[3,896]{1,0:T(4,128)(2,1)S(1)} %concatenate.28), channel_id=1, source_target_pairs={{0,1},{1,2},{2,3},{3,0},{4,5},{5,6},{6,7},{7,4},{8,9},{9,10},{10,1... | collective-permute-start | bytes 16136 | tf_op jit(solution)/shard_map/ppermute | solution.py:731
  15.3 5.1 %collective-permute-start.4 = (bf16[3,896]{1,0:T(4,128)(2,1)S(1)}, bf16[3,896]{1,0:T(4,128)(2,1)S(1)}, u32[]{:S(2)}, u32[]{:S(2)}) collective-permute-start(bf16[3,896]{1,0:T(4,128)(2,1)S(1)} %concatenate.28), channel_id=1, source_target_pairs={{0,2},{1,3},{2,0},{3,1},{4,6},{5,7},{6,4},{7,5},{8,10},{9,11},{10,... | collective-permute-start | bytes 16136 | tf_op jit(solution)/shard_map/ppermute | solution.py:731
  18.0 3.6 %collective-permute-start.3 = (bf16[3,896]{1,0:T(4,128)(2,1)S(1)}, bf16[3,896]{1,0:T(4,128)(2,1)S(1)}, u32[]{:S(2)}, u32[]{:S(2)}) collective-permute-start(bf16[3,896]{1,0:T(4,128)(2,1)S(1)} %concatenate.28), channel_id=1, source_target_pairs={{0,3},{1,0},{2,1},{3,2},{4,7},{5,4},{6,5},{7,6},{8,11},{9,8},{10,9... | collective-permute-start | bytes 16136 | tf_op jit(solution)/shard_map/ppermute | solution.py:731
  21.8 8.3 %collective-permute-start.7 = (bf16[48,896]{1,0:T(8,128)(2,1)S(1)}, bf16[48,896]{1,0:T(8,128)(2,1)S(1)}, u32[]{:S(2)}, u32[]{:S(2)}) collective-permute-start(bf16[48,896]{1,0:T(8,128)(2,1)S(1)} %get-tuple-element.158), channel_id=1, source_target_pairs={{0,64},{32,96},{64,0},{96,32},{1,65},{33,97},{65,1},{97,33},{2,66}... | collective-permute-start | bytes 258056 | tf_op jit(solution)/shard_map/ppermute | solution.py:731
  25.8 5.4 %collective-permute-start.6 = (bf16[48,896]{1,0:T(8,128)(2,1)S(1)}, bf16[48,896]{1,0:T(8,128)(2,1)S(1)}, u32[]{:S(2)}, u32[]{:S(2)}) collective-permute-start(bf16[48,896]{1,0:T(8,128)(2,1)S(1)} %get-tuple-element.158), channel_id=1, source_target_pairs={{0,96},{32,0},{64,32},{96,64},{1,97},{33,1},{65,33},{97,65},{2,98}... | collective-permute-start | bytes 258056 | tf_op jit(solution)/shard_map/ppermute | solution.py:731
  26.5 6.0 %collective-permute-start.8 = (bf16[48,896]{1,0:T(8,128)(2,1)S(1)}, bf16[48,896]{1,0:T(8,128)(2,1)S(1)}, u32[]{:S(2)}, u32[]{:S(2)}) collective-permute-start(bf16[48,896]{1,0:T(8,128)(2,1)S(1)} %get-tuple-element.158), channel_id=1, source_target_pairs={{0,32},{32,64},{64,96},{96,0},{1,33},{33,65},{65,97},{97,1},{2,34}... | collective-permute-start | bytes 258056 | tf_op jit(solution)/shard_map/ppermute | solution.py:731
  32.6 12.9 %collective-permute-start.10 = (bf16[4,48,896]{2,1,0:T(8,128)(2,1)S(1)}, bf16[4,48,896]{2,1,0:T(8,128)(2,1)S(1)}, u32[]{:S(2)}, u32[]{:S(2)}) collective-permute-start(bf16[4,48,896]{2,1,0:T(8,128)(2,1)S(1)} %get-tuple-element.149), channel_id=1, source_target_pairs={{0,16},{8,24},{16,0},{24,8},{1,17},{9,25},{17,1},{25,9},{2,18},{10... | collective-permute-start | bytes 1032200 | tf_op jit(solution)/shard_map/ppermute | solution.py:731
  36.6 14.3 %collective-permute-start.9 = (bf16[4,48,896]{2,1,0:T(8,128)(2,1)S(1)}, bf16[4,48,896]{2,1,0:T(8,128)(2,1)S(1)}, u32[]{:S(2)}, u32[]{:S(2)}) collective-permute-start(bf16[4,48,896]{2,1,0:T(8,128)(2,1)S(1)} %get-tuple-element.149), channel_id=1, source_target_pairs={{0,24},{8,0},{16,8},{24,16},{1,25},{9,1},{17,9},{25,17},{2,26},{10... | collective-permute-start | bytes 1032200 | tf_op jit(solution)/shard_map/ppermute | solution.py:731
  37.6 13.4 %collective-permute-start.11 = (bf16[4,48,896]{2,1,0:T(8,128)(2,1)S(1)}, bf16[4,48,896]{2,1,0:T(8,128)(2,1)S(1)}, u32[]{:S(2)}, u32[]{:S(2)}) collective-permute-start(bf16[4,48,896]{2,1,0:T(8,128)(2,1)S(1)} %get-tuple-element.149), channel_id=1, source_target_pairs={{0,8},{8,16},{16,24},{24,0},{1,9},{9,17},{17,25},{25,1},{2,10},{10... | collective-permute-start | bytes 1032200 | tf_op jit(solution)/shard_map/ppermute | solution.py:731
  51.1 5.9 %copy-start.32 = (s32[2,1]{0,1:T(1,128)S(1)}, s32[2,1]{0,1:T(1,128)}, u32[]{:S(2)}) copy-start(s32[2,1]{0,1:T(1,128)} %param.17) | copy-start | bytes 28
  51.3 8.2 %copy-start = (bf16[4,4,48,896]{3,2,1,0:T(8,128)(2,1)}, bf16[4,4,48,896]{3,2,1,0:T(8,128)(2,1)S(1)}, u32[]{:S(2)}) copy-start(bf16[4,4,48,896]{3,2,1,0:T(8,128)(2,1)S(1)} %pad_maximum_fusion) | copy-start | bytes 4128772
  51.3 8.2 %collective-permute-start.12 = (bf16[16,48,896]{2,1,0:T(8,128)(2,1)S(1)}, bf16[16,48,896]{2,1,0:T(8,128)(2,1)}, u32[]{:S(2)}, u32[]{:S(2)}) collective-permute-start(bf16[16,48,896]{2,1,0:T(8,128)(2,1)S(1)} %bitcast.72), channel_id=1, source_target_pairs={{0,4},{4,0},{1,5},{5,1},{2,6},{6,2},{3,7},{7,3},{8,12},{12,8},{9,1... | collective-permute-start | bytes 4128776 | tf_op jit(solution)/shard_map/ppermute | solution.py:731
  52.2 13.0 %copy-start.1 = (bf16[2,160,384]{2,1,0:T(8,128)(2,1)}, bf16[2,160,384]{2,1,0:T(8,128)(2,1)S(1)}, u32[]{:S(2)}) copy-start(bf16[2,160,384]{2,1,0:T(8,128)(2,1)S(1)} %fusion.1.t0) | copy-start | bytes 737284
  52.2 13.0 %collective-permute-start.2 = (bf16[2,160,384]{2,1,0:T(8,128)(2,1)S(1)}, bf16[2,160,384]{2,1,0:T(8,128)(2,1)S(1)}, u32[]{:S(2)}, u32[]{:S(2)}) collective-permute-start(bf16[2,160,384]{2,1,0:T(8,128)(2,1)S(1)} %fusion.1.t0), channel_id=1, source_target_pairs={{0,1},{1,2},{2,3},{3,0},{4,5},{5,6},{6,7},{7,4},{8,9},{9,10},{10,1... | collective-permute-start | bytes 737288 | tf_op jit(solution)/shard_map/ppermute | solution.py:731
  52.9 14.5 %collective-permute-start.1 = (bf16[2,160,384]{2,1,0:T(8,128)(2,1)S(1)}, bf16[2,160,384]{2,1,0:T(8,128)(2,1)}, u32[]{:S(2)}, u32[]{:S(2)}) collective-permute-start(bf16[2,160,384]{2,1,0:T(8,128)(2,1)S(1)} %fusion.1.t0), channel_id=1, source_target_pairs={{0,2},{1,3},{2,0},{3,1},{4,6},{5,7},{6,4},{7,5},{8,10},{9,11},{10,... | collective-permute-start | bytes 737288 | tf_op jit(solution)/shard_map/ppermute | solution.py:731
  56.4 10.9 %collective-permute-start = (bf16[2,160,384]{2,1,0:T(8,128)(2,1)S(1)}, bf16[2,160,384]{2,1,0:T(8,128)(2,1)}, u32[]{:S(2)}, u32[]{:S(2)}) collective-permute-start(bf16[2,160,384]{2,1,0:T(8,128)(2,1)S(1)} %fusion.1.t0), channel_id=1, source_target_pairs={{0,3},{1,0},{2,1},{3,2},{4,7},{5,4},{6,5},{7,6},{8,11},{9,8},{10,9... | collective-permute-start | bytes 737288 | tf_op jit(solution)/shard_map/ppermute | solution.py:731
  67.4 40.7 %copy-start.5 = (bf16[2,1,144,384]{3,2,1,0:T(8,128)(2,1)S(1)}, bf16[2,1,144,384]{3,2,1,0:T(8,128)(2,1)}, u32[]{:S(2)}) copy-start(bf16[2,1,144,384]{3,2,1,0:T(8,128)(2,1)} %param.31) | copy-start | bytes 663556
  103.6 10.1 %collective-permute-start.13 = (bf16[2,144,384]{2,1,0:T(8,128)(2,1)}, bf16[2,144,384]{2,1,0:T(8,128)(2,1)S(1)}, u32[]{:S(2)}, u32[]{:S(2)}) collective-permute-start(bf16[2,144,384]{2,1,0:T(8,128)(2,1)} %get-tuple-element.69), channel_id=1, source_target_pairs={{0,1},{1,2},{2,3},{3,0},{4,5},{5,6},{6,7},{7,4},{8,9},{9,10},{10,1... | collective-permute-start | bytes 663560 | tf_op jit(solution)/shard_map/ppermute | solution.py:731
  104.7 14.1 %collective-permute-start.14 = (bf16[2,144,384]{2,1,0:T(8,128)(2,1)}, bf16[2,144,384]{2,1,0:T(8,128)(2,1)S(1)}, u32[]{:S(2)}, u32[]{:S(2)}) collective-permute-start(bf16[2,144,384]{2,1,0:T(8,128)(2,1)} %get-tuple-element.70), channel_id=1, source_target_pairs={{0,2},{1,3},{2,0},{3,1},{4,6},{5,7},{6,4},{7,5},{8,10},{9,11},{10,... | collective-permute-start | bytes 663560 | tf_op jit(solution)/shard_map/ppermute | solution.py:731
  107.5 11.5 %collective-permute-start.15 = (bf16[2,144,384]{2,1,0:T(8,128)(2,1)}, bf16[2,144,384]{2,1,0:T(8,128)(2,1)S(1)}, u32[]{:S(2)}, u32[]{:S(2)}) collective-permute-start(bf16[2,144,384]{2,1,0:T(8,128)(2,1)} %get-tuple-element.71), channel_id=1, source_target_pairs={{0,3},{1,0},{2,1},{3,2},{4,7},{5,4},{6,5},{7,6},{8,11},{9,8},{10,9... | collective-permute-start | bytes 663560 | tf_op jit(solution)/shard_map/ppermute | solution.py:731
  108.1 18.2 %collective-permute-start.21 = (bf16[2,144,384]{2,1,0:T(8,128)(2,1)S(1)}, bf16[2,144,384]{2,1,0:T(8,128)(2,1)S(1)}, u32[]{:S(2)}, u32[]{:S(2)}) collective-permute-start(bf16[2,144,384]{2,1,0:T(8,128)(2,1)S(1)} %bitcast.80), channel_id=1, source_target_pairs={{0,1},{1,2},{2,3},{3,0},{4,5},{5,6},{6,7},{7,4},{8,9},{9,10},{10,1... | collective-permute-start | bytes 663560 | tf_op jit(solution)/shard_map/ppermute | solution.py:731
  109.5 18.2 %collective-permute-start.20 = (bf16[2,144,384]{2,1,0:T(8,128)(2,1)S(1)}, bf16[2,144,384]{2,1,0:T(8,128)(2,1)S(1)}, u32[]{:S(2)}, u32[]{:S(2)}) collective-permute-start(bf16[2,144,384]{2,1,0:T(8,128)(2,1)S(1)} %bitcast.81), channel_id=1, source_target_pairs={{0,2},{1,3},{2,0},{3,1},{4,6},{5,7},{6,4},{7,5},{8,10},{9,11},{10,... | collective-permute-start | bytes 663560 | tf_op jit(solution)/shard_map/ppermute | solution.py:731
  113.7 5.4 %copy-start.16 = (bf16[2,144,384]{2,1,0:T(8,128)(2,1)}, bf16[2,144,384]{2,1,0:T(8,128)(2,1)S(1)}, u32[]{:S(2)}) copy-start(bf16[2,144,384]{2,1,0:T(8,128)(2,1)S(1)} %collective-permute-done.13.p1) | copy-start | bytes 663556
  113.7 14.1 %collective-permute-start.19 = (bf16[2,144,384]{2,1,0:T(8,128)(2,1)S(1)}, bf16[2,144,384]{2,1,0:T(8,128)(2,1)S(1)}, u32[]{:S(2)}, u32[]{:S(2)}) collective-permute-start(bf16[2,144,384]{2,1,0:T(8,128)(2,1)S(1)} %bitcast.82), channel_id=1, source_target_pairs={{0,3},{1,0},{2,1},{3,2},{4,7},{5,4},{6,5},{7,6},{8,11},{9,8},{10,9... | collective-permute-start | bytes 663560 | tf_op jit(solution)/shard_map/ppermute | solution.py:731
  122.1 10.7 %collective-permute-start.18 = (bf16[2,144,384]{2,1,0:T(8,128)(2,1)}, bf16[2,144,384]{2,1,0:T(8,128)(2,1)S(1)}, u32[]{:S(2)}, u32[]{:S(2)}) collective-permute-start(bf16[2,144,384]{2,1,0:T(8,128)(2,1)} %get-tuple-element.73.x0), channel_id=1, source_target_pairs={{0,1},{1,2},{2,3},{3,0},{4,5},{5,6},{6,7},{7,4},{8,9},{9,10},{10,1... | collective-permute-start | bytes 663560 | tf_op jit(solution)/shard_map/ppermute | solution.py:731
  123.4 13.4 %collective-permute-start.17 = (bf16[2,144,384]{2,1,0:T(8,128)(2,1)}, bf16[2,144,384]{2,1,0:T(8,128)(2,1)S(1)}, u32[]{:S(2)}, u32[]{:S(2)}) collective-permute-start(bf16[2,144,384]{2,1,0:T(8,128)(2,1)} %get-tuple-element.73.x0), channel_id=1, source_target_pairs={{0,2},{1,3},{2,0},{3,1},{4,6},{5,7},{6,4},{7,5},{8,10},{9,11},{10,... | collective-permute-start | bytes 663560 | tf_op jit(solution)/shard_map/ppermute | solution.py:731
  126.3 10.6 %copy-start.19 = (bf16[2,144,384]{2,1,0:T(8,128)(2,1)}, bf16[2,144,384]{2,1,0:T(8,128)(2,1)S(1)}, u32[]{:S(2)}) copy-start(bf16[2,144,384]{2,1,0:T(8,128)(2,1)S(1)} %collective-permute-done.21.g3) | copy-start | bytes 663556
  126.3 10.5 %collective-permute-start.16 = (bf16[2,144,384]{2,1,0:T(8,128)(2,1)}, bf16[2,144,384]{2,1,0:T(8,128)(2,1)S(1)}, u32[]{:S(2)}, u32[]{:S(2)}) collective-permute-start(bf16[2,144,384]{2,1,0:T(8,128)(2,1)} %get-tuple-element.73.x0), channel_id=1, source_target_pairs={{0,3},{1,0},{2,1},{3,2},{4,7},{5,4},{6,5},{7,6},{8,11},{9,8},{10,9... | collective-permute-start | bytes 663560 | tf_op jit(solution)/shard_map/ppermute | solution.py:731
  127.8 9.1 %copy-start.20 = (bf16[2,144,384]{2,1,0:T(8,128)(2,1)}, bf16[2,144,384]{2,1,0:T(8,128)(2,1)S(1)}, u32[]{:S(2)}) copy-start(bf16[2,144,384]{2,1,0:T(8,128)(2,1)S(1)} %collective-permute-done.20.g2) | copy-start | bytes 663556
  127.8 9.1 %copy-start.21 = (bf16[2,144,384]{2,1,0:T(8,128)(2,1)}, bf16[2,144,384]{2,1,0:T(8,128)(2,1)S(1)}, u32[]{:S(2)}) copy-start(bf16[2,144,384]{2,1,0:T(8,128)(2,1)S(1)} %collective-permute-done.19.g1) | copy-start | bytes 663556
  182.1 7.9 %collective-permute-start.25 = (bf16[2,144,384]{2,1,0:T(8,128)(2,1)S(1)}, bf16[2,144,384]{2,1,0:T(8,128)(2,1)S(1)}, u32[]{:S(2)}, u32[]{:S(2)}) collective-permute-start(bf16[2,144,384]{2,1,0:T(8,128)(2,1)S(1)} %copy-done.41), channel_id=1, source_target_pairs={{0,1},{1,2},{2,3},{3,0},{4,5},{5,6},{6,7},{7,4},{8,9},{9,10},{10,1... | collective-permute-start | bytes 663560 | tf_op jit(solution)/shard_map/ppermute | solution.py:731
  182.8 12.9 %collective-permute-start.26 = (bf16[2,144,384]{2,1,0:T(8,128)(2,1)S(1)}, bf16[2,144,384]{2,1,0:T(8,128)(2,1)S(1)}, u32[]{:S(2)}, u32[]{:S(2)}) collective-permute-start(bf16[2,144,384]{2,1,0:T(8,128)(2,1)S(1)} %copy-done.40), channel_id=1, source_target_pairs={{0,2},{1,3},{2,0},{3,1},{4,6},{5,7},{6,4},{7,5},{8,10},{9,11},{10,... | collective-permute-start | bytes 663560 | tf_op jit(solution)/shard_map/ppermute | solution.py:731
  185.7 10.1 %collective-permute-start.27 = (bf16[2,144,384]{2,1,0:T(8,128)(2,1)S(1)}, bf16[2,144,384]{2,1,0:T(8,128)(2,1)S(1)}, u32[]{:S(2)}, u32[]{:S(2)}) collective-permute-start(bf16[2,144,384]{2,1,0:T(8,128)(2,1)S(1)} %copy-done.39), channel_id=1, source_target_pairs={{0,3},{1,0},{2,1},{3,2},{4,7},{5,4},{6,5},{7,6},{8,11},{9,8},{10,9... | collective-permute-start | bytes 663560 | tf_op jit(solution)/shard_map/ppermute | solution.py:731
  190.0 5.7 %copy-start.13 = (bf16[2,144,384]{2,1,0:T(8,128)(2,1)}, bf16[2,144,384]{2,1,0:T(8,128)(2,1)S(1)}, u32[]{:S(2)}) copy-start(bf16[2,144,384]{2,1,0:T(8,128)(2,1)S(1)} %collective-permute-done.25.p1) | copy-start | bytes 663556
  199.3 8.0 %collective-permute-start.30 = (bf16[2,144,384]{2,1,0:T(8,128)(2,1)}, bf16[2,144,384]{2,1,0:T(8,128)(2,1)S(1)}, u32[]{:S(2)}, u32[]{:S(2)}) collective-permute-start(bf16[2,144,384]{2,1,0:T(8,128)(2,1)} %get-tuple-element.83.g0), channel_id=1, source_target_pairs={{0,1},{1,2},{2,3},{3,0},{4,5},{5,6},{6,7},{7,4},{8,9},{9,10},{10,1... | collective-permute-start | bytes 663560 | tf_op jit(solution)/shard_map/ppermute | solution.py:731
  199.9 13.4 %collective-permute-start.29 = (bf16[2,144,384]{2,1,0:T(8,128)(2,1)}, bf16[2,144,384]{2,1,0:T(8,128)(2,1)S(1)}, u32[]{:S(2)}, u32[]{:S(2)}) collective-permute-start(bf16[2,144,384]{2,1,0:T(8,128)(2,1)} %get-tuple-element.83.g0), channel_id=1, source_target_pairs={{0,2},{1,3},{2,0},{3,1},{4,6},{5,7},{6,4},{7,5},{8,10},{9,11},{10,... | collective-permute-start | bytes 663560 | tf_op jit(solution)/shard_map/ppermute | solution.py:731
  203.0 10.3 %collective-permute-start.28 = (bf16[2,144,384]{2,1,0:T(8,128)(2,1)}, bf16[2,144,384]{2,1,0:T(8,128)(2,1)S(1)}, u32[]{:S(2)}, u32[]{:S(2)}) collective-permute-start(bf16[2,144,384]{2,1,0:T(8,128)(2,1)} %get-tuple-element.83.g0), channel_id=1, source_target_pairs={{0,3},{1,0},{2,1},{3,2},{4,7},{5,4},{6,5},{7,6},{8,11},{9,8},{10,9... | collective-permute-start | bytes 663560 | tf_op jit(solution)/shard_map/ppermute | solution.py:731
  207.3 5.9 %copy-start.6 = (bf16[2,144,384]{2,1,0:T(8,128)(2,1)}, bf16[2,144,384]{2,1,0:T(8,128)(2,1)S(1)}, u32[]{:S(2)}) copy-start(bf16[2,144,384]{2,1,0:T(8,128)(2,1)S(1)} %collective-permute-done.30.g3) | copy-start | bytes 663556
  252.2 9.6 %collective-permute-start.36 = (bf16[96,896]{1,0:T(8,128)(2,1)S(1)}, bf16[96,896]{1,0:T(8,128)(2,1)S(1)}, u32[]{:S(2)}, u32[]{:S(2)}) collective-permute-start(bf16[96,896]{1,0:T(8,128)(2,1)S(1)} %get-tuple-element.144), channel_id=1, source_target_pairs={{0,3},{1,0},{2,1},{3,2},{4,7},{5,4},{6,5},{7,6},{8,11},{9,8},{10,9... | collective-permute-start | bytes 516104 | tf_op jit(solution)/shard_map/ppermute | solution.py:731
  254.4 8.8 %collective-permute-start.35 = (bf16[96,896]{1,0:T(8,128)(2,1)S(1)}, bf16[96,896]{1,0:T(8,128)(2,1)S(1)}, u32[]{:S(2)}, u32[]{:S(2)}) collective-permute-start(bf16[96,896]{1,0:T(8,128)(2,1)S(1)} %get-tuple-element.145), channel_id=1, source_target_pairs={{0,2},{1,3},{2,0},{3,1},{4,6},{5,7},{6,4},{7,5},{8,10},{9,11},{10,... | collective-permute-start | bytes 516104 | tf_op jit(solution)/shard_map/ppermute | solution.py:731
  254.9 10.6 %collective-permute-start.34 = (bf16[96,896]{1,0:T(8,128)(2,1)S(1)}, bf16[96,896]{1,0:T(8,128)(2,1)S(1)}, u32[]{:S(2)}, u32[]{:S(2)}) collective-permute-start(bf16[96,896]{1,0:T(8,128)(2,1)S(1)} %get-tuple-element.146), channel_id=1, source_target_pairs={{0,1},{1,2},{2,3},{3,0},{4,5},{5,6},{6,7},{7,4},{8,9},{9,10},{10,1... | collective-permute-start | bytes 516104 | tf_op jit(solution)/shard_map/ppermute | solution.py:731
  270.2 3.1 collective-permute-start.37
  274.9 10.7 %copy-start.33 = (bf16[2,144,384]{2,1,0:T(8,128)(2,1)S(1)}, bf16[2,144,384]{2,1,0:T(8,128)(2,1)}, u32[]{:S(2)}) copy-start(bf16[2,144,384]{2,1,0:T(8,128)(2,1)} %get-tuple-element.77) | copy-start | bytes 663556
  274.9 16.1 %copy-start.38 = (bf16[2,144,384]{2,1,0:T(8,128)(2,1)S(1)}, bf16[2,144,384]{2,1,0:T(8,128)(2,1)}, u32[]{:S(2)}) copy-start(bf16[2,144,384]{2,1,0:T(8,128)(2,1)} %get-tuple-element.99) | copy-start | bytes 663556
  274.9 17.4 %copy-start.37 = (bf16[2,144,384]{2,1,0:T(8,128)(2,1)S(1)}, bf16[2,144,384]{2,1,0:T(8,128)(2,1)}, u32[]{:S(2)}) copy-start(bf16[2,144,384]{2,1,0:T(8,128)(2,1)} %get-tuple-element.100) | copy-start | bytes 663556
  275.0 18.3 %copy-start.36 = (bf16[2,144,384]{2,1,0:T(8,128)(2,1)S(1)}, bf16[2,144,384]{2,1,0:T(8,128)(2,1)}, u32[]{:S(2)}) copy-start(bf16[2,144,384]{2,1,0:T(8,128)(2,1)} %get-tuple-element.101) | copy-start | bytes 663556
  275.0 29.9 %copy-start.4 = (f32[2,144,384]{2,1,0:T(8,128)S(1)}, f32[2,144,384]{2,1,0:T(8,128)}, u32[]{:S(2)}) copy-start(f32[2,144,384]{2,1,0:T(8,128)} %get-tuple-element.72.mixed) | copy-start | bytes 1327108
  275.0 29.9 %copy-start.9 = (bf16[2,144,384]{2,1,0:T(8,128)(2,1)S(1)}, bf16[2,144,384]{2,1,0:T(8,128)(2,1)}, u32[]{:S(2)}) copy-start(bf16[2,144,384]{2,1,0:T(8,128)(2,1)} %get-tuple-element.74) | copy-start | bytes 663556
  275.0 10.5 %collective-permute-start.38 = (bf16[4,48,768]{2,1,0:T(8,128)(2,1)S(1)}, bf16[4,48,768]{2,1,0:T(8,128)(2,1)S(1)}, u32[]{:S(2)}, u32[]{:S(2)}) collective-permute-start(bf16[4,48,768]{2,1,0:T(8,128)(2,1)S(1)} %get-tuple-element.141), channel_id=1, source_target_pairs={{0,8},{8,16},{16,24},{24,0},{1,9},{9,17},{17,25},{25,1},{2,10},{10... | collective-permute-start | bytes 884744 | tf_op jit(solution)/shard_map/ppermute | solution.py:731
  275.9 15.0 %collective-permute-start.40 = (bf16[4,48,768]{2,1,0:T(8,128)(2,1)S(1)}, bf16[4,48,768]{2,1,0:T(8,128)(2,1)S(1)}, u32[]{:S(2)}, u32[]{:S(2)}) collective-permute-start(bf16[4,48,768]{2,1,0:T(8,128)(2,1)S(1)} %get-tuple-element.142), channel_id=1, source_target_pairs={{0,24},{8,0},{16,8},{24,16},{1,25},{9,1},{17,9},{25,17},{2,26},{10... | collective-permute-start | bytes 884744 | tf_op jit(solution)/shard_map/ppermute | solution.py:731
  278.3 13.9 %collective-permute-start.39 = (bf16[4,48,768]{2,1,0:T(8,128)(2,1)S(1)}, bf16[4,48,768]{2,1,0:T(8,128)(2,1)S(1)}, u32[]{:S(2)}, u32[]{:S(2)}) collective-permute-start(bf16[4,48,768]{2,1,0:T(8,128)(2,1)S(1)} %get-tuple-element.143), channel_id=1, source_target_pairs={{0,16},{8,24},{16,0},{24,8},{1,17},{9,25},{17,1},{25,9},{2,18},{10... | collective-permute-start | bytes 884744 | tf_op jit(solution)/shard_map/ppermute | solution.py:731
  279.2 14.1 %collective-permute-start.22 = (bf16[2,144,384]{2,1,0:T(8,128)(2,1)S(1)}, bf16[2,144,384]{2,1,0:T(8,128)(2,1)S(1)}, u32[]{:S(2)}, u32[]{:S(2)}) collective-permute-start(bf16[2,144,384]{2,1,0:T(8,128)(2,1)S(1)} %copy-done.35), channel_id=1, source_target_pairs={{0,1},{1,2},{2,3},{3,0},{4,5},{5,6},{6,7},{7,4},{8,9},{9,10},{10,1... | collective-permute-start | bytes 663560 | tf_op jit(solution)/shard_map/ppermute | solution.py:731
  279.4 15.1 %collective-permute-start.23 = (bf16[2,144,384]{2,1,0:T(8,128)(2,1)S(1)}, bf16[2,144,384]{2,1,0:T(8,128)(2,1)S(1)}, u32[]{:S(2)}, u32[]{:S(2)}) collective-permute-start(bf16[2,144,384]{2,1,0:T(8,128)(2,1)S(1)} %copy-done.34), channel_id=1, source_target_pairs={{0,2},{1,3},{2,0},{3,1},{4,6},{5,7},{6,4},{7,5},{8,10},{9,11},{10,... | collective-permute-start | bytes 663560 | tf_op jit(solution)/shard_map/ppermute | solution.py:731
  285.6 9.6 %collective-permute-start.24 = (bf16[2,144,384]{2,1,0:T(8,128)(2,1)S(1)}, bf16[2,144,384]{2,1,0:T(8,128)(2,1)S(1)}, u32[]{:S(2)}, u32[]{:S(2)}) collective-permute-start(bf16[2,144,384]{2,1,0:T(8,128)(2,1)S(1)} %copy-done.33), channel_id=1, source_target_pairs={{0,3},{1,0},{2,1},{3,2},{4,7},{5,4},{6,5},{7,6},{8,11},{9,8},{10,9... | collective-permute-start | bytes 663560 | tf_op jit(solution)/shard_map/ppermute | solution.py:731
  291.0 11.9 %collective-permute-start.31 = (bf16[2,144,384]{2,1,0:T(8,128)(2,1)S(1)}, bf16[2,144,384]{2,1,0:T(8,128)(2,1)S(1)}, u32[]{:S(2)}, u32[]{:S(2)}) collective-permute-start(bf16[2,144,384]{2,1,0:T(8,128)(2,1)S(1)} %copy-done.38), channel_id=1, source_target_pairs={{0,1},{1,2},{2,3},{3,0},{4,5},{5,6},{6,7},{7,4},{8,9},{9,10},{10,1... | collective-permute-start | bytes 663560 | tf_op jit(solution)/shard_map/ppermute | solution.py:731
  292.3 13.5 %collective-permute-start.32 = (bf16[2,144,384]{2,1,0:T(8,128)(2,1)S(1)}, bf16[2,144,384]{2,1,0:T(8,128)(2,1)S(1)}, u32[]{:S(2)}, u32[]{:S(2)}) collective-permute-start(bf16[2,144,384]{2,1,0:T(8,128)(2,1)S(1)} %copy-done.37), channel_id=1, source_target_pairs={{0,2},{1,3},{2,0},{3,1},{4,6},{5,7},{6,4},{7,5},{8,10},{9,11},{10,... | collective-permute-start | bytes 663560 | tf_op jit(solution)/shard_map/ppermute | solution.py:731
  293.3 12.5 %collective-permute-start.33 = (bf16[2,144,384]{2,1,0:T(8,128)(2,1)S(1)}, bf16[2,144,384]{2,1,0:T(8,128)(2,1)S(1)}, u32[]{:S(2)}, u32[]{:S(2)}) collective-permute-start(bf16[2,144,384]{2,1,0:T(8,128)(2,1)S(1)} %copy-done.36), channel_id=1, source_target_pairs={{0,3},{1,0},{2,1},{3,2},{4,7},{5,4},{6,5},{7,6},{8,11},{9,8},{10,9... | collective-permute-start | bytes 663560 | tf_op jit(solution)/shard_map/ppermute | solution.py:731
  294.5 14.5 %collective-permute-start.41 = (bf16[48,768]{1,0:T(8,128)(2,1)S(1)}, bf16[48,768]{1,0:T(8,128)(2,1)S(1)}, u32[]{:S(2)}, u32[]{:S(2)}) collective-permute-start(bf16[48,768]{1,0:T(8,128)(2,1)S(1)} %get-tuple-element.150), channel_id=1, source_target_pairs={{0,32},{32,64},{64,96},{96,0},{1,33},{33,65},{65,97},{97,1},{2,34}... | collective-permute-start | bytes 221192 | tf_op jit(solution)/shard_map/ppermute | solution.py:731
  295.2 13.9 %collective-permute-start.43 = (bf16[48,768]{1,0:T(8,128)(2,1)S(1)}, bf16[48,768]{1,0:T(8,128)(2,1)S(1)}, u32[]{:S(2)}, u32[]{:S(2)}) collective-permute-start(bf16[48,768]{1,0:T(8,128)(2,1)S(1)} %get-tuple-element.151), channel_id=1, source_target_pairs={{0,96},{32,0},{64,32},{96,64},{1,97},{33,1},{65,33},{97,65},{2,98}... | collective-permute-start | bytes 221192 | tf_op jit(solution)/shard_map/ppermute | solution.py:731
  302.8 6.2 %collective-permute-start.42 = (bf16[48,768]{1,0:T(8,128)(2,1)S(1)}, bf16[48,768]{1,0:T(8,128)(2,1)S(1)}, u32[]{:S(2)}, u32[]{:S(2)}) collective-permute-start(bf16[48,768]{1,0:T(8,128)(2,1)S(1)} %get-tuple-element.152), channel_id=1, source_target_pairs={{0,64},{32,96},{64,0},{96,32},{1,65},{33,97},{65,1},{97,33},{2,66}... | collective-permute-start | bytes 221192 | tf_op jit(solution)/shard_map/ppermute | solution.py:731
  (24 other events, 41.5 us)
Sparse Core Ops, SparseCore 0:
  10.9 62.3 all-gather.2
  181.3 89.6 reduce-scatter.1

commit v2 on v1

v2 whole, which is shorter than its diff:
```python
import jax
import jax.numpy as jnp
from jax import lax
from jax.experimental import pallas as pl
from jax.experimental.pallas import tpu as pltpu
from jax.sharding import Mesh, PartitionSpec as P

BF = jnp.bfloat16
F32 = jnp.float32
EPSILON = 1e-06
MASKED = -1e30
MB, NX, SQ, SLOTS, D = 2, 4, 144, 576, 384
EXP, CAP, HEADS, FF = 3, 256, 6, 1536
PACK = 160
TOKS = ("z", "y", "c")
VMEM = 62 * 1024 * 1024


def params(n, mib=60):
    return pltpu.CompilerParams(
        dimension_semantics=("arbitrary",) * n, vmem_limit_bytes=mib * 1024 * 1024
    )


def cost(us):
    return pl.CostEstimate(flops=int(us * 1e9), bytes_accessed=0, transcendentals=0)


def dot(a, b):
    return jnp.dot(a, b, preferred_element_type=F32)


def dot_nt(a, b):
    return lax.dot_general(a, b, (((1,), (1,)), ((), ())), preferred_element_type=F32)


def dot_tn(a, b):
    return lax.dot_general(a, b, (((0,), (0,)), ((), ())), preferred_element_type=F32)


def iota(shape, dim):
    return lax.broadcasted_iota(jnp.int32, shape, dim)


def hot(cond):
    return jnp.where(cond, 1.0, 0.0).astype(BF)


def eye(n):
    return hot(iota((n, n), 0) == iota((n, n), 1))


def flip(a):
    return dot_nt(eye(a.shape[1]), a)


def tok_of(place, sc, plain=False):
    c = (sc[1] + (place >> 4)) & 1
    if plain:
        return (place & 15) * 2 + c
    z = (sc[2] + (place & 3)) & 3
    y = (sc[3] + ((place >> 2) & 3)) & 3
    return z * 8 + y * 2 + c


def third(v):
    return (v * 11) >> 5


def owned_feature(k, sc, plain=False):
    r = k & 15
    return jnp.where(r < 12, tok_of(k >> 4, sc, plain) * 12 + r, -1)


def shared_feature(place, idx, valid, sc, plain=False):
    s = third(idx)
    feature = tok_of(place, sc, plain) * 12 + ((sc[0] + s) & 3) * 3 + idx - 3 * s
    return jnp.where(valid, feature, -1)


def canonical_feature(col):
    r = col & 15
    return jnp.where(r < 12, (col >> 4) * 12 + r, -1)


def native_lane(sc):
    j = iota((1, 128), 1)
    n = j + 3 * sc[0]
    n = jnp.where(n >= 12, n - 12, n)
    return jnp.where(j < 12, n, -1)


def router_turn(sc, offset):
    n = native_lane(sc)
    return hot((iota((128, 128), 0) == n + offset) & (n >= 0))


def norm_parts(x):
    mu = jnp.mean(x, -1, keepdims=True)
    c = x - mu
    var = jnp.mean(c * c, -1, keepdims=True)
    inv = lax.rsqrt(var + EPSILON)
    return c * inv, inv


def norm_back(grad, normed, inv, gain):
    u = grad * gain
    a = jnp.mean(u, -1, keepdims=True)
    b = jnp.mean(u * normed, -1, keepdims=True)
    return (u - a - normed * b) * inv


def routing(rcol, first, x, router, sc):
    nat = native_lane(sc).astype(F32)
    member = jnp.zeros((SLOTS, 128), F32)
    for k in range(4):
        member = member + jnp.where(rcol[:, first + k : first + k + 1] == nat, 1.0, 0.0)
    inside = member > 0.5
    logits = jnp.where(inside, dot(x, router), MASKED)
    top = jnp.max(logits, -1, keepdims=True)
    ex = jnp.where(inside, jnp.exp(logits - top), 0.0)
    gates = ex / jnp.sum(ex, -1, keepdims=True)
    mb = member.astype(BF)
    lower = hot(iota((SLOTS, SLOTS), 1) < iota((SLOTS, SLOTS), 0))
    mt = dot_nt(hot(iota((16, 128), 0) == iota((16, 128), 1)), mb)
    posc = jnp.where(inside, dot(lower, mb), -1.0)
    posr = jnp.where(mt > 0.5, dot_nt(mt.astype(BF), lower), -1.0)
    return gates, posc, posr


def route_columns(refs, m):
    unit = hot(iota((SQ, 256), 0) == iota((SQ, 256), 1))
    return jnp.concatenate([dot_nt(unit, r[m, SQ:PACK, 0:256]) for r in refs], 0)


def gate_lanes(gates):
    hi = gates.astype(BF).astype(F32)
    lo = pltpu.roll(gates - hi, 64, 1)
    return jnp.where(iota(gates.shape, 1) < 64, hi, lo).astype(BF)


def pick(ext, e):
    lane = iota(ext.shape, 1)
    return jnp.sum(jnp.where((lane == e) | (lane == 64 + e), ext, 0.0), -1, keepdims=True)


def split_lanes(col, e):
    hi = col.astype(BF).astype(F32)
    lane = iota((col.shape[0], 128), 1)
    both = jnp.where(lane == e, hi, 0.0) + jnp.where(lane == 64 + e, col - hi, 0.0)
    return both.astype(BF)


def gather_matrix(row):
    return hot(row == iota((CAP, SLOTS), 0).astype(F32))


def scatter_matrix(posc, e):
    col = jnp.sum(jnp.where(iota(posc.shape, 1) == e, posc, 0.0), -1, keepdims=True)
    return hot(col == iota((SLOTS, CAP), 1).astype(F32))


def router_grad(gates, lanes):
    t = lanes + pltpu.roll(lanes, 64, 1)
    inner = jnp.sum(gates * t, -1, keepdims=True)
    return (gates * (t - inner)).astype(BF)


def smem():
    return pl.BlockSpec(memory_space=pltpu.SMEM)


def full(shape):
    return pl.BlockSpec(shape, lambda *_: (0,) * len(shape))


def sds(shape, dtype):
    return jax.ShapeDtypeStruct(shape, dtype)


def pack_kernel(wkv, rattn, rmlp, vecs, wq, wo, wup, wdown, shared, own, mlp):
    shared[...] = jnp.zeros_like(shared)
    own[...] = jnp.zeros_like(own)
    mlp[...] = jnp.zeros_like(mlp)
    shared[0:3, 0:768] = wkv[...]
    shared[0:3, 768:780] = rattn[...]
    shared[0:3, 780:792] = rmlp[...]
    lane, row = iota((3, 12), 1), iota((3, 12), 0)
    v = vecs[...].astype(F32)
    cols = [
        jnp.sum(jnp.where(lane == 3 * i + row, v, 0.0), -1, keepdims=True) for i in range(4)
    ]
    shared[0:3, 792:796] = jnp.concatenate(cols, 1).astype(BF)
    for e in range(EXP):
        own[e, 0:12, 0:D] = wq[e]
        own[e, 0:12, D : 2 * D] = wo[e]
        for g in range(4):
            mlp[e, 16 * g : 16 * g + 12, :] = wup[e, :, D * g : D * g + D]
        mlp[e, 64:112, :] = wdown[e]


def pack(wkv, rattn, rmlp, vecs, wq, wo, wup, wdown):
    shapes = [(16, 896), (EXP, 16, 768), (EXP, 112, D)]
    args = (wkv, rattn, rmlp, vecs, wq, wo, wup, wdown)
    return pl.pallas_call(
        pack_kernel,
        grid=(1,),
        in_specs=[full(v.shape) for v in args],
        out_specs=[full(v) for v in shapes],
        out_shape=[sds(v, BF) for v in shapes],
        compiler_params=params(1, 62),
        cost_estimate=cost(2),
        name="pack",
    )(*args)


def prep_kernel(sc, a0, a1, wq, wo, wkv, wkvt, sm, vec):
    take = hot(iota((D, 512), 0) == owned_feature(iota((1, 512), 1), sc))
    for e in range(EXP):
        rows = jnp.concatenate(
            [a[:, 16 * e : 16 * e + 16, 0:768].reshape(256, 768) for a in (a0, a1)], 0
        )
        nat = dot(take, rows).astype(BF)
        wq[e] = nat[:, :D]
        wo[e] = nat[:, D:]
    k = iota((1, 1536), 1)
    place = (k * 1366) >> 16
    r48 = k - place * 48
    r16 = r48 & 15
    d = iota((D, 1536), 0)
    kv_feature = shared_feature(place, (r48 >> 4) * 4 + r16 - 12, r16 >= 12, sc)
    everything = jnp.concatenate([a[:, :, 0:768].reshape(768, 768) for a in (a0, a1)], 0)
    kv = dot(hot(d == kv_feature), everything).astype(BF)
    wkv[...] = kv
    wkvt[...] = kv.T
    side = jnp.concatenate([a[:, 0:16, 768:].reshape(256, 128) for a in (a0, a1)], 0)
    k = iota((1, 512), 1)
    sm_feature = shared_feature(k >> 4, k & 15, (k & 15) < 12, sc)
    small = dot(hot(iota((D, 512), 0) == sm_feature), side).astype(BF)
    sm[...] = small
    vec[...] = dot_nt(hot(iota((8, 128), 1) == iota((8, 128), 0) + 24), small)


def prep(sc, a0, a1):
    return pl.pallas_call(
        prep_kernel,
        grid=(1,),
        in_specs=[smem()] + [full((16, 48, 896))] * 2,
        out_specs=[
            full((EXP, D, D)),
            full((EXP, D, D)),
            full((D, 768)),
            full((768, D)),
            full((D, 128)),
            full((8, D)),
        ],
        out_shape=[
            sds((EXP, D, D), BF),
            sds((EXP, D, D), BF),
            sds((D, 768), BF),
            sds((768, D), BF),
            sds((D, 128), BF),
            sds((8, D), F32),
        ],
        compiler_params=params(1, 62),
        cost_estimate=cost(5),
        name="prep",
    )(sc, a0, a1)


ROWS = EXP * CAP


def gather_all(posr):
    return jnp.concatenate([gather_matrix(posr[e : e + 1, :]) for e in range(EXP)], 0)


def scatter_all(posc):
    return jnp.concatenate([scatter_matrix(posc, e) for e in range(EXP)], 1)


def by_expert(f):
    return jnp.concatenate([f(e, slice(CAP * e, CAP * e + CAP)) for e in range(EXP)], 0)


def own_half(rows, side):
    lane = iota((rows, 128), 1)
    return lane < 64 if side == 0 else lane >= 64


def spare(side):
    return 64 if side == 0 else 0


def with_ones(v, side):
    lane, at = iota(v.shape, 1), spare(side)
    ones = jnp.where((lane == at) | (lane == at + 1), 1.0, 0.0)
    return jnp.where(own_half(v.shape[0], side), v.astype(F32), ones).astype(BF)


def attend_kernel(
    sc, t0, t1, t2, t3, wq, wo, wkv, sm, vec,
    o0, o1, o2, o3, xo, kvo, gateo, poso, posco, rowso, qo, atto, bro, grow, rin, exo,
):
    m = pl.program_id(0)
    toks = (t0, t1, t2, t3)
    x = jnp.concatenate([t[0, 0:SQ, :].astype(F32) for t in toks], 0)
    n, _ = norm_parts(x)
    a = (n * vec[0:1, :] + vec[1:2, :]).astype(BF)
    xo[0] = a
    router = dot(sm[...], router_turn(sc, 0)).astype(BF)
    gates, posc, posr = routing(route_columns(toks, 0), 0, a, router, sc)
    gateo[0] = gates
    posco[0] = posc
    poso[0] = posr
    kv = dot(a, wkv[...]).astype(BF)
    kvo[0] = kv

    ext = dot(gather_all(posr), jnp.concatenate([a, gate_lanes(gates)], 1))
    rows = ext[:, 0:D].astype(BF)
    gate = by_expert(lambda e, r: pick(ext[r, D:512], e))
    rowso[0] = rows
    grow[0] = jnp.broadcast_to(gate, (ROWS, 128))
    q = by_expert(lambda e, r: dot(rows[r], wq[e])).astype(BF)
    q = q * jnp.asarray(0.125, BF)
    qo[0] = q
    slot = iota((SLOTS, 1), 0) + SQ * sc[0]
    slot = jnp.where(slot >= SLOTS, slot - SLOTS, slot)
    bias = jnp.where(slot < sc[4 + m], 0.0, MASKED)
    lane = iota((ROWS, 128), 1)
    inv_lanes = jnp.zeros((ROWS, 128), F32)
    for hp in range(3):
        span = slice(128 * hp, 128 * hp + 128)
        halves = []
        for side in range(2):
            h = 2 * hp + side
            at = spare(side)
            ka = jnp.where(own_half(SLOTS, side), kv[:, span].astype(F32), jnp.where(iota((SLOTS, 128), 1) == at, bias, 0.0)).astype(BF)
            one = jnp.where(lane == at, 1.0, 0.0)
            qa = jnp.where(own_half(ROWS, side), q[:, span].astype(F32), one).astype(BF)
            va = with_ones(kv[:, D + 128 * hp : D + 128 * hp + 128], side)
            s = dot_nt(qa, ka)
            ex = jnp.exp(s - jnp.max(s, -1, keepdims=True)).astype(BF)
            exo[0, h] = ex
            pv = dot(ex, va)
            inv = 1.0 / pv[:, at : at + 1]
            inv_lanes = jnp.where(lane == h, inv, inv_lanes)
            halves.append(pv * inv)
        atto[0, :, span] = jnp.where(lane < 64, halves[0], halves[1]).astype(BF)
    rin[0] = inv_lanes
    br = by_expert(lambda e, r: dot(atto[0, r, :], wo[e])).astype(BF)
    bro[0] = br
    acc = dot(scatter_all(posc), (gate * br.astype(F32)).astype(BF))
    for s, o in enumerate((o0, o1, o2, o3)):
        o[0] = acc[SQ * s : SQ * s + SQ, :].astype(BF)


def per_m(*shape):
    return pl.BlockSpec((1,) + shape, lambda m: (m,) + (0,) * len(shape))


def attend(sc, toks, weights):
    saved = [
        (SLOTS, D, BF),
        (SLOTS, 768, BF),
        (SLOTS, 128, F32),
        (16, SLOTS, F32),
        (SLOTS, 128, F32),
        (ROWS, D, BF),
        (ROWS, D, BF),
        (ROWS, D, BF),
        (ROWS, D, BF),
        (ROWS, 128, F32),
        (ROWS, 128, F32),
        (HEADS, ROWS, SLOTS, BF),
    ]
    outs = [(SQ, D, BF)] * 4 + saved
    out = pl.pallas_call(
        attend_kernel,
        grid=(MB,),
        in_specs=[smem()]
        + [per_m(PACK, D)] * 4
        + [full((EXP, D, D)), full((EXP, D, D)), full((D, 768)), full((D, 128)), full((8, D))],
        out_specs=[per_m(*o[:-1]) for o in outs],
        out_shape=[sds((MB,) + o[:-1], o[-1]) for o in outs],
        compiler_params=params(1, 62),
        cost_estimate=cost(24),
        name="attend",
    )(sc, *toks, *weights)
    return out[:4], out[4:]


def mix_kernel(t, p0, p1, p2, p3, vec, mixed, mlp_in):
    for m in range(MB):
        x = t[m].astype(F32)
        for p in (p0, p1, p2, p3):
            x = x + p[m].astype(F32)
        mixed[m] = x
        n, _ = norm_parts(x)
        mlp_in[m] = (n * vec[2:3, :] + vec[3:4, :]).astype(BF)


def mix(tokens, parts, vec):
    shape = (MB, SQ, D)
    return pl.pallas_call(
        mix_kernel,
        grid=(1,),
        in_specs=[full(shape)] * 5 + [full((8, D))],
        out_specs=[full(shape)] * 2,
        out_shape=[sds(shape, F32), sds(shape, BF)],
        compiler_params=params(1, 8),
        cost_estimate=cost(2),
        name="mix",
    )(tokens, *parts, vec)


def gelu_both(v):
    phi = 0.5 + 0.5 * lax.erf(v * 0.7071067811865476)
    density = jnp.exp(-0.5 * (v * v)) * 0.3989422804014327
    return v * phi, phi + v * density


FC = 768


def experts_kernel(
    sc, x0, x1, x2, x3, g0, g1, g2, g3, t0, t1, t2, t3, sm, w_ref,
    oo0, oo1, oo2, oo3, og0, og1, og2, og3, rmlp, rowso, gbo, hido, gpo,
    xe, gin, gates, posr, posc, acco, accg,
):
    e = pl.program_id(0)
    router = None

    @pl.when(e == 0)
    def _():
        turn = dot(sm[...], router_turn(sc, 12)).astype(BF)
        pad = hot(iota((D, 512), 0) == canonical_feature(iota((1, 512), 1)))
        for m in range(MB):
            a = jnp.concatenate([x[m] for x in (x0, x1, x2, x3)], 0)
            gt, pc, pr = routing(route_columns((t0, t1, t2, t3), m), 4, a, turn, sc)
            gates[m] = gt
            posc[m] = pc
            posr[m] = pr
            xe[m, :, 0:512] = dot(a, pad).astype(BF)
            xe[m, :, 512:640] = gate_lanes(gt)
            gin[m] = jnp.concatenate([g[m] for g in (g0, g1, g2, g3)], 0)
        acco[...] = jnp.zeros_like(acco)
        accg[...] = jnp.zeros_like(accg)

    exts, grs = [], []
    for m in range(MB):
        g = gather_matrix(posr[m, pl.ds(e, 1), :])
        exts.append(dot(g, xe[m]))
        grs.append(dot(g, gin[m]))
    ext = jnp.concatenate(exts, 0)
    gr = jnp.concatenate(grs, 0)
    rows = ext[:, 0:512].astype(BF)
    gate = pick(ext[:, 512:640], e)
    gb = (gate * gr).astype(BF)
    rowso[0] = rows
    gbo[0] = gb
    branch = jnp.zeros((512, D), F32)
    back = jnp.zeros((512, 512), F32)
    for c in range(FF // FC):
        span = slice(c * FC, c * FC + FC)
        w = jnp.concatenate(
            [w_ref[:, 0, 16 * g : 16 * g + 16, :].reshape(512, D) for g in (2 * c, 2 * c + 1)], 1
        )
        wd = w_ref[16 * c : 16 * c + 16, 0, 64:112, :].reshape(FC, D)
        act, slope = gelu_both(dot(rows, w))
        hid = act.astype(BF)
        gp = (dot_nt(gb, wd) * slope).astype(BF)
        hido[0, :, span] = hid
        gpo[0, :, span] = gp
        branch = branch + dot(hid, wd)
        back = back + dot_nt(gp, w)
    br = branch.astype(BF).astype(F32)
    t = jnp.sum(gr * br, -1, keepdims=True)
    scaled = (gate * br).astype(BF)
    lanes = split_lanes(t, e)
    backb = back.astype(BF)
    for m in range(MB):
        r = slice(CAP * m, CAP * m + CAP)
        sca = scatter_matrix(posc[m], e)
        acco[m] += dot(sca, jnp.concatenate([scaled[r], lanes[r]], 1))
        accg[m] += dot(sca, backb[r])

    @pl.when(e == EXP - 1)
    def _():
        turn = dot(sm[...], router_turn(sc, 12)).astype(BF)
        pad = hot(iota((D, 512), 0) == canonical_feature(iota((1, 512), 1)))
        total = jnp.zeros((D, 128), F32)
        for m in range(MB):
            dl = router_grad(gates[m], acco[m, :, D:512])
            a = jnp.concatenate([x[m] for x in (x0, x1, x2, x3)], 0)
            total = total + dot(flip(a).astype(BF), dl)
            part = dot_nt(accg[m].astype(BF), pad) + dot_nt(dl, turn)
            for s, (o, og) in enumerate(zip((oo0, oo1, oo2, oo3), (og0, og1, og2, og3))):
                r = slice(SQ * s, SQ * s + SQ)
                o[m] = acco[m, r, 0:D].astype(BF)
                og[m] = part[r].astype(BF)
        rmlp[...] = total


def experts(sc, xs, gs, toks, sm, wmlp):
    piece = (full((MB, SQ, D)), sds((MB, SQ, D), BF))

    def by_e(*shape):
        return pl.BlockSpec((1,) + shape, lambda e: (e,) + (0,) * len(shape))

    saved = [
        (full((D, 128)), sds((D, 128), F32)),
        (by_e(512, 512), sds((EXP, 512, 512), BF)),
        (by_e(512, D), sds((EXP, 512, D), BF)),
        (by_e(512, FF), sds((EXP, 512, FF), BF)),
        (by_e(512, FF), sds((EXP, 512, FF), BF)),
    ]
    outs = [piece] * 8 + saved
    got = pl.pallas_call(
        experts_kernel,
        grid=(EXP,),
        in_specs=[smem()]
        + [full((MB, SQ, D))] * 8
        + [full((MB, PACK, D))] * 4
        + [
            full((D, 128)),
            pl.BlockSpec((32, 1, 112, D), lambda e: (0, e, 0, 0)),
        ],
        out_specs=[o[0] for o in outs],
        out_shape=[o[1] for o in outs],
        scratch_shapes=[
            pltpu.VMEM((MB, SLOTS, 640), BF),
            pltpu.VMEM((MB, SLOTS, D), BF),
            pltpu.VMEM((MB, SLOTS, 128), F32),
            pltpu.VMEM((MB, 16, SLOTS), F32),
            pltpu.VMEM((MB, SLOTS, 128), F32),
            pltpu.VMEM((MB, SLOTS, 512), F32),
            pltpu.VMEM((MB, SLOTS, 512), F32),
        ],
        compiler_params=params(1, 62),
        cost_estimate=cost(26),
        name="experts",
    )(sc, *xs, *gs, *toks, sm, wmlp)
    return got[:4], got[4:8], got[8], got[9:]


def expert_grads_kernel(rows, gb, hid, gp, out):
    du = dot_tn(rows[0], gp[0]).astype(BF)
    for g in range(4):
        out[:, 0, 16 * g : 16 * g + 16, :] = du[:, D * g : D * g + D].reshape(32, 16, D)
    out[:, 0, 64:112, :] = dot_tn(hid[0], gb[0]).astype(BF).reshape(32, 48, D)


def expert_grads(saved):
    def by_e(*shape):
        return pl.BlockSpec((1,) + shape, lambda e: (e,) + (0,) * len(shape))

    return pl.pallas_call(
        expert_grads_kernel,
        grid=(EXP,),
        in_specs=[by_e(512, 512), by_e(512, D), by_e(512, FF), by_e(512, FF)],
        out_specs=pl.BlockSpec((32, 1, 112, D), lambda e: (0, e, 0, 0)),
        out_shape=sds((32, EXP, 112, D), BF),
        compiler_params=params(1, 62),
        cost_estimate=cost(11),
        name="expert_grads",
    )(*saved)


def turn_kernel(mixed, cot, p0, p1, p2, p3, vec, gmix, gmixb, gv):
    rows = [jnp.zeros((1, D), F32)] * 2
    for m in range(MB):
        n, inv = norm_parts(mixed[m])
        grad = jnp.zeros((SQ, D), F32)
        for p in (p0, p1, p2, p3):
            grad = grad + p[m].astype(F32)
        gm = cot[m].astype(F32) + norm_back(grad, n, inv, vec[2:3, :])
        gmix[m] = gm
        gmixb[m] = gm.astype(BF)
        rows[0] = rows[0] + jnp.sum(grad * n, 0, keepdims=True)
        rows[1] = rows[1] + jnp.sum(grad, 0, keepdims=True)
    gv[...] = jnp.concatenate(rows + [jnp.zeros((6, D), F32)], 0)


def turn(mixed, cot, parts, vec):
    shape = (MB, SQ, D)
    return pl.pallas_call(
        turn_kernel,
        grid=(1,),
        in_specs=[full(shape)] * 6 + [full((8, D))],
        out_specs=[full(shape), full(shape), full((8, D))],
        out_shape=[sds(shape, F32), sds(shape, BF), sds((8, D), F32)],
        compiler_params=params(1, 8),
        cost_estimate=cost(3),
        name="turn",
    )(mixed, cot, *parts, vec)


def attend_back_kernel(
    sc, g0, g1, g2, g3, t0, t1, t2, t3, x, kv, gates, posr, posc, rows, q, att, br, grow, rin, ex,
    wq, wo, wkvt, sm, vec, gv, rmlp,
    o0, o1, o2, o3, ta0, ta1,
    dkvt, dwq, dwo, dwkvt, dsm, dvec,
):
    m = pl.program_id(0)

    @pl.when(m == 0)
    def _():
        dwq[...] = jnp.zeros_like(dwq)
        dwo[...] = jnp.zeros_like(dwo)
        dwkvt[...] = jnp.zeros_like(dwkvt)
        dsm[...] = jnp.zeros_like(dsm)
        dvec[...] = jnp.zeros_like(dvec)

    gin = jnp.concatenate([g[0] for g in (g0, g1, g2, g3)], 0)
    gr = dot(gather_all(posr[0]), gin)
    gb = (grow[0][:, 0:1] * gr).astype(BF)
    t = jnp.sum(gr * br[0].astype(F32), -1, keepdims=True)
    ga = by_expert(lambda e, r: dot_nt(gb[r], wo[e])).astype(BF)
    for e in range(EXP):
        r = slice(CAP * e, CAP * e + CAP)
        dwo[:, D * e : D * e + D] += dot_tn(att[0, r, :], gb[r])
    lane = iota((ROWS, 128), 1)
    low = lane < 64
    dqs = []
    for hp in range(3):
        span = slice(128 * hp, 128 * hp + 128)
        inv = jnp.where(low, rin[0, :, 2 * hp : 2 * hp + 1], rin[0, :, 2 * hp + 1 : 2 * hp + 2])
        gap = ga[:, span].astype(F32) * inv
        inner = gap * att[0, :, span].astype(F32)
        gapt = flip(gap.astype(BF)).astype(BF)
        qt = flip(q[0, :, span]).astype(BF)
        outs = []
        for side in range(2):
            h = 2 * hp + side
            at = spare(side)
            own = own_half(ROWS, side)
            ri = jnp.sum(jnp.where(own, inner, 0.0), -1, keepdims=True)
            hi = ri.astype(BF).astype(F32)
            rest = jnp.where(lane == at, -hi, jnp.where(lane == at + 1, hi - ri, 0.0))
            gaa = jnp.where(own, gap, rest).astype(BF)
            va = with_ones(kv[0, :, D + 128 * hp : D + 128 * hp + 128], side)
            p = ex[0, h]
            ds = (p.astype(F32) * dot_nt(gaa, va)).astype(BF)
            outs.append(dot(ds, kv[0, :, span]))
            hs = slice(64 * side, 64 * side + 64)
            dkvt[64 * h : 64 * h + 64, :] = dot(qt[hs, :], ds)
            dkvt[D + 64 * h : D + 64 * h + 64, :] = dot(gapt[hs, :], p)
        dqs.append((jnp.where(low, outs[0], outs[1]) * 0.125).astype(BF))
    dq = jnp.concatenate(dqs, 1)
    for e in range(EXP):
        r = slice(CAP * e, CAP * e + CAP)
        dwq[:, D * e : D * e + D] += dot_tn(rows[0, r, :], dq[r])
    back = by_expert(lambda e, r: dot_nt(dq[r], wq[e])).astype(BF)
    lanes = by_expert(lambda e, r: split_lanes(t[r], e))
    acc = dot(scatter_all(posc[0]), jnp.concatenate([back, lanes], 1))

    dl = router_grad(gates[0], acc[:, D:512])
    router = dot(sm[...], router_turn(sc, 0)).astype(BF)
    dkvb = dkvt[...].astype(BF)
    part = acc[:, 0:D] + dot_nt(dl, router) + dot_tn(dkvb, wkvt[...])
    tk = jnp.concatenate([r[0, 0:SQ, :].astype(F32) for r in (t0, t1, t2, t3)], 0)
    n, _ = norm_parts(tk)
    dvec[0:1, :] += jnp.sum(part * n, 0, keepdims=True)
    dvec[1:2, :] += jnp.sum(part, 0, keepdims=True)
    dsm[...] += dot_tn(x[0], dl)
    dwkvt[...] += dot(dkvb, x[0])
    for s, o in enumerate((o0, o1, o2, o3)):
        o[0] = part[SQ * s : SQ * s + SQ].astype(BF)

    @pl.when(m == MB - 1)
    def _():
        small = dot_nt(dsm[...].astype(BF), router_turn(sc, 0))
        small = small + dot_nt(rmlp[...].astype(BF), router_turn(sc, 12))
        vecs = jnp.concatenate(
            [jnp.zeros((24, D), F32), dvec[0:2, :], gv[0:2, :], jnp.zeros((100, D), F32)], 0
        ).astype(BF)
        small = (small + dot_nt(eye(D), vecs)).astype(BF)
        k, d = iota((512, 1), 0), iota((512, D), 1)
        r = k & 15
        own = hot(owned_feature(k, sc, True) == d)
        kvb = flip(dwkvt[...].astype(BF)).astype(BF)
        for e in range(EXP):
            span = slice(D * e, D * e + D)
            shared = hot(shared_feature(k >> 4, 4 * e + r - 12, r >= 12, sc, True) == d)
            weights = jnp.concatenate([dwq[:, span], dwo[:, span]], 1).astype(BF)
            wide = dot(jnp.concatenate([own, shared], 1), jnp.concatenate([weights, kvb], 0))
            wide = wide.astype(BF)
            rows = slice(16 * e, 16 * e + 16)
            for i, t in enumerate((ta0, ta1)):
                t[:, rows, 0:768] = wide[256 * i : 256 * i + 256].reshape(16, 16, 768)
            if e == 0:
                side = dot(hot(shared_feature(k >> 4, r, r < 12, sc, True) == d), small).astype(BF)
            else:
                side = jnp.zeros((512, 128), BF)
            for i, t in enumerate((ta0, ta1)):
                t[:, rows, 768:896] = side[256 * i : 256 * i + 256].reshape(16, 16, 128)


def attend_back(sc, gs, toks, saved, wq, wo, wkvt, sm, vec, gv, rmlp):
    piece = [(per_m(SQ, D), sds((MB, SQ, D), BF))] * 4
    outs = piece + [
        (full((16, 48, 896)), sds((16, 48, 896), BF)),
        (full((16, 48, 896)), sds((16, 48, 896), BF)),
    ]
    got = pl.pallas_call(
        attend_back_kernel,
        grid=(MB,),
        in_specs=[smem()]
        + [per_m(SQ, D)] * 4
        + [per_m(PACK, D)] * 4
        + [per_m(*v.shape[1:]) for v in saved]
        + [
            full((EXP, D, D)), full((EXP, D, D)), full((768, D)), full((D, 128)), full((8, D)),
            full((8, D)), full((D, 128)),
        ],
        out_specs=[o[0] for o in outs],
        out_shape=[o[1] for o in outs],
        scratch_shapes=[
            pltpu.VMEM((768, SLOTS), F32),
            pltpu.VMEM((D, EXP * D), F32),
            pltpu.VMEM((D, EXP * D), F32),
            pltpu.VMEM((768, D), F32),
            pltpu.VMEM((D, 128), F32),
            pltpu.VMEM((8, D), F32),
        ],
        compiler_params=params(1, 62),
        cost_estimate=cost(120),
        name="attend_back",
    )(sc, *gs, *toks, *saved, wq, wo, wkvt, sm, vec, gv, rmlp)
    return got[:4], got[4:]


def finish_kernel(gmix, tokens, p0, p1, p2, p3, vec, out):
    for m in range(MB):
        n, inv = norm_parts(tokens[m].astype(F32))
        grad = jnp.zeros((SQ, D), F32)
        for p in (p0, p1, p2, p3):
            grad = grad + p[m].astype(F32)
        out[m] = (gmix[m] + norm_back(grad, n, inv, vec[0:1, :])).astype(BF)


def finish(gmix, tokens, parts, vec):
    shape = (MB, SQ, D)
    return pl.pallas_call(
        finish_kernel,
        grid=(1,),
        in_specs=[full(shape)] * 6 + [full((8, D))],
        out_specs=full(shape),
        out_shape=sds(shape, BF),
        compiler_params=params(1, 8),
        cost_estimate=cost(2),
        name="finish",
    )(gmix, tokens, *parts, vec)


def shift(a, axis, s):
    n = lax.axis_size(axis)
    return lax.ppermute(a, axis, [(i, (i + s) % n) for i in range(n)])


def fetch(a, axis):
    one, three, two = [shift(a, axis, 4 - s) for s in (1, 3, 2)]
    return [a, one, two, three]


def send(parts, axis):
    two, one, three = [shift(parts[s], axis, s) for s in (2, 1, 3)]
    return [parts[0], one, two, three]


def add2(a, b):
    return (a.astype(F32) + b.astype(F32)).astype(BF)


def tie(*arrays):
    return lax.optimization_barrier(arrays)


def fold(a, axis):
    got = send([a[s] for s in range(a.shape[0])], axis)
    return sum(v.astype(F32) for v in got)


def local(
    tokens, patch_counts, attn_routes, mlp_routes, gain1, bias1, gain2, bias2, wkv, rattn, rmlp,
    wq, wo, wup, wdown, cotangent,
):
    tokens = tokens.reshape(MB, SQ, D)
    cot = cotangent.reshape(MB, SQ, D)
    index = [lax.axis_index(a) for a in ("x", "c", "z", "y")]
    sc = jnp.stack(index + [patch_counts[0, 0], patch_counts[1, 0], 0, 0]).astype(jnp.int32)

    vecs = jnp.concatenate([gain1, bias1, gain2, bias2]).reshape(1, 12)
    shared, own, mlp_shard = pack(wkv, rattn, rmlp, vecs, wq, wo, wup, wdown)
    routes = jnp.concatenate([attn_routes, mlp_routes], -1).reshape(MB, SQ, 8)
    routes = jnp.moveaxis(routes, 1, 2).astype(BF)
    packed = jnp.concatenate([tokens, jnp.pad(routes, ((0, 0), (0, 8), (0, D - SQ)))], 1)
    kv12 = jnp.concatenate([v[0:3] for v in fetch(shared, "x")], 0)
    shard = jnp.concatenate([own[:, 0:12], kv12[:, :768].reshape(3, 4, 768)], 1).reshape(48, 768)
    shard = jnp.concatenate([shard, jnp.pad(kv12[:, 768:], ((0, 36), (0, 0)))], 1)
    zs = jnp.stack(fetch(shard, "z"))
    toks = fetch(packed, "x")
    a0 = jnp.stack(fetch(zs, "y")).reshape(16, 48, 896)
    a0, toks, mlp_shard = tie(a0, toks, mlp_shard)
    wmlp = lax.all_gather(mlp_shard, TOKS, axis=0).reshape(32, EXP, 112, D)
    fq, fo, fkv, fkvt, sm, vec = prep(sc, a0, shift(a0, "c", 1))

    gs = fetch(cot, "x")
    parts, saved = attend(sc, toks, (fq, fo, fkv, sm, vec))
    parts, gs = tie(parts, gs)
    mixed, mlp_in = mix(tokens, send(parts, "x"), vec)
    xs = fetch(mlp_in, "x")
    outp, gradp, rm, kept = experts(sc, xs, gs, toks, sm, wmlp)
    gradp = send(gradp, "x")
    dmlp = expert_grads(kept)
    gradp, dmlp = tie(gradp, dmlp)
    dmlp = lax.psum_scatter(dmlp, TOKS, scatter_dimension=0, tiled=True)
    gmix, gmixb, gv = turn(mixed, cot, gradp, vec)
    gms = fetch(gmixb, "x")
    back, (ta, ta1) = attend_back(sc, gms, toks, saved, fq, fo, fkvt, sm, vec, gv, rm)
    ta1 = shift(ta1, "c", 1)
    ta1, back, outp = tie(ta1, back, outp)
    ta = lax.all_to_all(add2(ta, ta1), ("z", "y"), 0, 0, tiled=True)
    ta = jnp.sum(ta.astype(F32), 0)
    back = send(back, "x")
    outp, back = tie(outp, back)
    tokens_grad = finish(gmix, tokens, back, vec)
    result = mixed
    for o in send(outp, "x"):
        result = result + o.astype(F32)
    result = result.astype(BF)
    t3 = ta.reshape(3, 16, 896)
    kv = jnp.concatenate([t3[:, 12:16, :768].reshape(12, 768), ta[0:12, 768:]], 1)
    small = fold(kv.astype(BF).reshape(4, 3, 896), "x")

    mlp = dmlp.astype(F32)
    mlp = mlp.reshape(EXP, 112, D)
    dup = mlp[:, 0:64].reshape(EXP, 4, 16, D)[:, :, 0:12]
    dup = jnp.moveaxis(dup, 1, 2).reshape(EXP, 12, FF)
    ddown = mlp[:, 64:112]
    dq, do = t3[:, :12, :D], t3[:, :12, D:768]
    shape = (MB, 1, SQ, D)
    return (
        result.reshape(shape),
        tokens_grad.reshape(shape),
        small[:, 792],
        small[:, 793],
        small[:, 794],
        small[:, 795],
        small[:, 0:768],
        small[:, 768:780],
        small[:, 780:792],
        dq,
        do,
        dup,
        ddown,
    )


def solution(mesh):
    fine = Mesh(mesh.devices.reshape(4, 4, 2, 4), ("z", "y", "c", "x"))
    every = TOKS + ("x",)
    act = P(None, TOKS, "x", None)
    row, mat, own = P(every), P(every, None), P("x", TOKS, None)
    return jax.shard_map(
        local,
        mesh=fine,
        in_specs=(
            act, P(None, TOKS), act, act, row, row, row, row, mat, mat, mat, own, own, own, own, act,
        ),
        out_specs=(act, act, row, row, row, row, mat, mat, mat, own, own, own, own),
        check_vma=False,
    )
```

time: 326 us -> 285 us (0.87)
  Pallas kernels: 134 us -> 102 us
  waiting for transfers between devices: 87.5 us -> 75.4 us
  local copies, waits for them, and re-layouts: 20.4 us -> 12.1 us
  starting transfers between devices: 60.4 us -> 66.7 us
  other arithmetic: 4.7 us -> 8.74 us
    ppermute x44 -> x38, waiting for transfers between devices: 87.4 us -> 64.2 us  [shift(): return lax.ppermute(a, axis, [(i, (i + s) % n) for i in range(n)])]
    pallas_call x4, Pallas kernels: 82.4 us -> 61.9 us  [the longest x1 31.1 us: attend_back(): pl.pallas_call(attend_back_kernel, grid=(MB,), in_specs=[smem()] + [per_m...]
    reduce_scatter x1, waiting for transfers between devices: 0.01 us -> 7.59 us  [local(): dmlp = lax.psum_scatter(dmlp, TOKS, scatter_dimension=0, tiled=True)]
    pallas_call x1, Pallas kernels: 32.4 us -> 26.3 us  [experts(): pl.pallas_call(experts_kernel, grid=(EXP,), in_specs=[smem()] + [full((MB...]
    all_to_all x0 -> x1, starting transfers between devices: none -> 4.87 us  [local(): ta = lax.all_to_all(add2(ta, ta1), ('z', 'y'), 0, 0, tiled=True)]
    all_to_all x0 -> x1, waiting for transfers between devices: none -> 3.53 us  [local(): ta = lax.all_to_all(add2(ta, ta1), ('z', 'y'), 0, 0, tiled=True)]
    unnamed x85 -> x68, local copies, waits for them, and re-layouts: 6.78 us -> 4.49 us
    ppermute x44 -> x38, starting transfers between devices: 60.3 us -> 61.7 us  [shift(): return lax.ppermute(a, axis, [(i, (i + s) % n) for i in range(n)])]
  transfers between devices with their start and end apart: 46 -> 41, of which waited for: 27 -> 24; matrix products, arithmetic and copies ran while one was open for 4% -> 4% of each run, Pallas kernels for 28% -> 26%
where the time goes in v2:
time: 285 us; the launch traced here: 279 us
  Pallas kernels  102 us (36%)
  waiting for transfers between devices  75.4 us (26%)
  starting transfers between devices  66.7 us (23%)
  between operations  14.8 us (5%)
  local copies, waits for them, and re-layouts  12.1 us (4%)
  other arithmetic  8.74 us (3%)
    ppermute x38, waiting for transfers between devices, shift(): return lax.ppermute(a, axis, [(i, (i + s) % n) for i in range(n)])  64.2 us
    ppermute x38, starting transfers between devices, shift(): return lax.ppermute(a, axis, [(i, (i + s) % n) for i in range(n)])  61.7 us
    pallas_call x1, Pallas kernels, attend_back(): pl.pallas_call(attend_back_kernel, grid=(MB,), in_specs=[smem()] + [per_m...  31.1 us
    pallas_call x1, Pallas kernels, experts(): pl.pallas_call(experts_kernel, grid=(EXP,), in_specs=[smem()] + [full((MB...  26.3 us
    pallas_call x1, Pallas kernels, attend(): pl.pallas_call(attend_kernel, grid=(MB,), in_specs=[smem()] + [per_m(PACK...  23.9 us
    pallas_call x1, Pallas kernels, expert_grads(): pl.pallas_call(expert_grads_kernel, grid=(EXP,), in_specs=[by_e(512, 512)...  11.5 us
    reduce_scatter x1, waiting for transfers between devices, local(): dmlp = lax.psum_scatter(dmlp, TOKS, scatter_dimension=0, tiled=True)  7.59 us
  transfers between devices with their start and end apart: 41, of which 24 were waited for; matrix products, arithmetic and copies ran while one was open for 4% of the time, Pallas kernels for 26%

profile of v2, /device:TPU:0, one launch (start us, length us, event | category | flops | bytes accessed | tf_op | source)
XLA Modules:
  0.0 279.2 jit_solution(14356479225230963450)
XLA Ops:
  7.2 1.3 maximum_bitcast_fusion.1.vecs
  8.5 1.9 pack.1
  10.4 1.6 collective-permute-start.2
  12.0 2.7 collective-permute-start.1
  14.8 1.4 collective-permute-start
  17.6 1.2 collective-permute-done
  18.9 0.9 pad_maximum_fusion.3
  19.9 4.0 %collective-permute-start.4 = (bf16[48,896]{1,0:T(8,128)(2,1)S(1)}, bf16[48,896]{1,0:T(8,128)(2,1)S(1)}, u32[]{:S(2)}, u32[]{:S(2)}) collective-permute-start(bf16[48,896]{1,0:T(8,128)(2,1)S(1)} %get-tuple-element.218), channel_id=1, source_target_pairs={{0,64},{32,96},{64,0},{96,32},{1,65},{33,97},{65,1},{97,33},{2,66}... | collective-permute-start | bytes 258056 | tf_op jit(solution)/shard_map/ppermute | solution.py:759
  24.6 1.3 collective-permute-start.5
  25.9 1.1 collective-permute-done.4
  27.0 1.4 collective-permute-done.3
  28.3 1.9 collective-permute-done.5
  30.3 3.3 %collective-permute-start.7 = (bf16[4,48,896]{2,1,0:T(8,128)(2,1)S(1)}, bf16[4,48,896]{2,1,0:T(8,128)(2,1)S(1)}, u32[]{:S(2)}, u32[]{:S(2)}) collective-permute-start(bf16[4,48,896]{2,1,0:T(8,128)(2,1)S(1)} %get-tuple-element.214), channel_id=1, source_target_pairs={{0,16},{8,24},{16,0},{24,8},{1,17},{9,25},{17,1},{25,9},{2,18},{10... | collective-permute-start | bytes 1032200 | tf_op jit(solution)/shard_map/ppermute | solution.py:759
  33.6 1.1 collective-permute-start.6
  34.7 1.0 collective-permute-start.8
  36.1 3.8 %collective-permute-start.10 = (bf16[2,160,384]{2,1,0:T(8,128)(2,1)S(1)}, bf16[2,160,384]{2,1,0:T(8,128)(2,1)S(1)}, u32[]{:S(2)}, u32[]{:S(2)}) collective-permute-start(bf16[2,160,384]{2,1,0:T(8,128)(2,1)S(1)} %fusion.1.t0), channel_id=1, source_target_pairs={{0,2},{1,3},{2,0},{3,1},{4,6},{5,7},{6,4},{7,5},{8,10},{9,11},{10,... | collective-permute-start | bytes 737288 | tf_op jit(solution)/shard_map/ppermute | solution.py:759
  39.9 2.8 collective-permute-done.7
  42.7 2.6 collective-permute-start.9
  45.3 1.4 collective-permute-done.6
  47.2 1.8 collective-permute-done.9.t1
  50.1 5.0 %collective-permute-start.14 = (bf16[2,144,384]{2,1,0:T(8,128)(2,1)S(1)}, bf16[2,144,384]{2,1,0:T(8,128)(2,1)}, u32[]{:S(2)}, u32[]{:S(2)}) collective-permute-start(bf16[2,144,384]{2,1,0:T(8,128)(2,1)S(1)} %bitcast.51), channel_id=1, source_target_pairs={{0,2},{1,3},{2,0},{3,1},{4,6},{5,7},{6,4},{7,5},{8,10},{9,11},{10,... | collective-permute-start | bytes 663560 | tf_op jit(solution)/shard_map/ppermute | solution.py:759
  55.9 1.9 stack.49.sc
  57.8 5.0 %prep.1 = (bf16[3,384,384]{2,1,0:T(8,128)(2,1)}, bf16[3,384,384]{2,1,0:T(8,128)(2,1)}, bf16[384,768]{1,0:T(8,128)(2,1)}, bf16[768,384]{1,0:T(8,128)(2,1)}, bf16[384,128]{1,0:T(8,128)(2,1)}, /*index=5*/f32[8,384]{1,0:T(8,128)}) custom-call(s32[8]{0:T(128)} %stack.49.sc, bf16[16,48,896]{2,1,0:T(8,128)(2,1)} %bitcast.55, ...), custom_call_target="tpu_custom_call" | custom-call | flops 5000000000 | tf_op jit(solution)/shard_map/prep/pallas_call | solution.py:245
  62.8 23.9 %attend.1 = (bf16[2,144,384]{2,1,0:T(8,128)(2,1)}, bf16[2,144,384]{2,1,0:T(8,128)(2,1)}, bf16[2,144,384]{2,1,0:T(8,128)(2,1)}, bf16[2,144,384]{2,1,0:T(8,128)(2,...) custom-call(s32[8]{0:T(128)} %stack.49.sc, ...), custom_call_target="tpu_custom_call" | custom-call | flops 24000000000 | tf_op jit(solution)/shard_map/attend/pallas_call | solution.py:378
  86.8 2.1 collective-permute-start.16
  88.9 2.8 collective-permute-start.18
  91.6 8.6 %collective-permute-done.16.p1 = bf16[2,144,384]{2,1,0:T(8,128)(2,1)S(1)} collective-permute-done((bf16[2,144,384]{2,1,0:T(8,128)(2,1)}, bf16[2,144,384]{2,1,0:T(8,128)(2,1)S(1)}, u32[]{:S(2)}, u32[]{:S(2)}) %collective-permute-start.16) | collective-permute-done | bytes 221216 | tf_op jit(solution)/shard_map/ppermute | solution.py:759
  100.8 0.9 copy-done.8
  102.1 2.0 collective-permute-start.21
  104.1 2.6 collective-permute-start.20
  107.4 3.4 %collective-permute-done.21.x3 = bf16[2,144,384]{2,1,0:T(8,128)(2,1)S(1)} collective-permute-done((bf16[2,144,384]{2,1,0:T(8,128)(2,1)S(1)}, bf16[2,144,384]{2,1,0:T(8,128)(2,1)S(1)}, u32[]{:S(2)}, u32[]{:S(2)}) %collective-permute-start.21) | collective-permute-done | bytes 221216 | tf_op jit(solution)/shard_map/ppermute | solution.py:759
  110.8 5.9 %collective-permute-done.20.x2 = bf16[2,144,384]{2,1,0:T(8,128)(2,1)S(1)} collective-permute-done((bf16[2,144,384]{2,1,0:T(8,128)(2,1)S(1)}, bf16[2,144,384]{2,1,0:T(8,128)(2,1)S(1)}, u32[]{:S(2)}, u32[]{:S(2)}) %collective-permute-start.20) | collective-permute-done | bytes 221216 | tf_op jit(solution)/shard_map/ppermute | solution.py:759
  117.5 26.3 %experts.1 = (bf16[2,144,384]{2,1,0:T(8,128)(2,1)}, bf16[2,144,384]{2,1,0:T(8,128)(2,1)}, bf16[2,144,384]{2,1,0:T(8,128)(2,1)}, bf16[2,144,384]{2,1,0:T(8,128)(2...) custom-call(s32[8]{0:T(128)} %stack.49.sc, ...), custom_call_target="tpu_custom_call" | custom-call | flops 25999998976 | tf_op jit(solution)/shard_map/experts/pallas_call | solution.py:519
  143.8 1.0 collective-permute-start.22
  144.8 2.6 collective-permute-start.23
  147.4 0.8 collective-permute-start.24
  148.2 11.5 %expert_grads.1 = bf16[32,3,112,384]{3,2,1,0:T(8,128)(2,1)} custom-call(bf16[3,512,512]{2,1,0:T(8,128)(2,1)} %get-tuple-element.130.rows, bf16[3,512,384]{2,1,0:T(8,128)(2,1)} %get-tuple-element.131.gb, bf16[3,512,1536]{2,1,0:T(8,128)(2,1)} %get-tuple-element.132.hid, bf16[3,512,1536]{2,1,0:T(8,128)(2,1)} %get-tuple-element.133.gp), custom_call_target="tpu_custom_call" | custom-call | flops 11000000512 | tf_op jit(solution)/shard_map/expert_grads/pallas_call | solution.py:558
  161.6 1.4 collective-permute-start.27
  162.9 0.9 collective-permute-start.26
  163.8 2.3 collective-permute-start.25
  166.2 7.6 %collective-permute-done.27.g3 = bf16[2,144,384]{2,1,0:T(8,128)(2,1)S(1)} collective-permute-done((bf16[2,144,384]{2,1,0:T(8,128)(2,1)S(1)}, bf16[2,144,384]{2,1,0:T(8,128)(2,1)S(1)}, u32[]{:S(2)}, u32[]{:S(2)}) %collective-permute-start.27) | collective-permute-done | bytes 221216 | tf_op jit(solution)/shard_map/ppermute | solution.py:759
  175.1 31.1 %attend_back.1 = (bf16[2,144,384]{2,1,0:T(8,128)(2,1)}, bf16[2,144,384]{2,1,0:T(8,128)(2,1)}, bf16[2,144,384]{2,1,0:T(8,128)(2,1)}, bf16[2,144,384]{2,1,0:T(8,12...) custom-call(s32[8]{0:T(128)} %stack.49.sc, bf16[2,144,384]{2,1,0:T(8,128)(2,1)} %copy-done.3, ...), custom_call_target="tpu_custom_call" | custom-call | flops 120000004096 | tf_op jit(solution)/shard_map/attend_back/pallas_call | solution.py:706
  206.3 3.3 %collective-permute-done.28 = bf16[16,48,896]{2,1,0:T(8,128)(2,1)S(1)} collective-permute-done((bf16[16,48,896]{2,1,0:T(8,128)(2,1)}, bf16[16,48,896]{2,1,0:T(8,128)(2,1)S(1)}, u32[]{:S(2)}, u32[]{:S(2)}) %collective-permute-start.28) | collective-permute-done | bytes 1376288 | tf_op jit(solution)/shard_map/ppermute | solution.py:759
  209.6 2.8 add_convert_fusion
  212.5 4.9 %all-to-all-start = ((bf16[16,48,896]{2,1,0:T(8,128)(2,1)}), bf16[16,48,896]{2,1,0:T(8,128)(2,1)}, u32[]{:S(2)}, u32[]{:S(2)}) async-start(bf16[16,48,896]{2,1,0:T(8,128)(2,1)} %add_convert_fusion), calls=%async_computation | async-start | bytes 2752512 | tf_op jit(solution)/shard_map/all_to_all | solution.py:824
  217.3 1.5 collective-permute-start.29
  218.8 2.8 collective-permute-start.30
  222.0 4.0 %collective-permute-done.29.p1 = bf16[2,144,384]{2,1,0:T(8,128)(2,1)S(1)} collective-permute-done((bf16[2,144,384]{2,1,0:T(8,128)(2,1)S(1)}, bf16[2,144,384]{2,1,0:T(8,128)(2,1)S(1)}, u32[]{:S(2)}, u32[]{:S(2)}) %collective-permute-start.29) | collective-permute-done | bytes 221216 | tf_op jit(solution)/shard_map/ppermute | solution.py:759
  226.0 5.5 %collective-permute-done.30.p2 = bf16[2,144,384]{2,1,0:T(8,128)(2,1)S(1)} collective-permute-done((bf16[2,144,384]{2,1,0:T(8,128)(2,1)S(1)}, bf16[2,144,384]{2,1,0:T(8,128)(2,1)S(1)}, u32[]{:S(2)}, u32[]{:S(2)}) %collective-permute-start.30) | collective-permute-done | bytes 221216 | tf_op jit(solution)/shard_map/ppermute | solution.py:759
  231.5 1.0 collective-permute-start.32
  232.5 2.8 collective-permute-start.33
  235.8 1.1 finish.1
  236.9 2.6 collective-permute-done.32
  239.5 5.9 %collective-permute-done.33 = bf16[2,144,384]{2,1,0:T(8,128)(2,1)S(1)} collective-permute-done((bf16[2,144,384]{2,1,0:T(8,128)(2,1)S(1)}, bf16[2,144,384]{2,1,0:T(8,128)(2,1)S(1)}, u32[]{:S(2)}, u32[]{:S(2)}) %collective-permute-start.33) | collective-permute-done | bytes 221216 | tf_op jit(solution)/shard_map/ppermute | solution.py:759
  245.5 0.8 fusion.2
  246.3 3.5 %all-to-all-done = bf16[16,48,896]{2,1,0:T(8,128)(2,1)} async-done(((bf16[16,48,896]{2,1,0:T(8,128)(2,1)}), bf16[16,48,896]{2,1,0:T(8,128)(2,1)}, u32[]{:S(2)}, u32[]{:S(2)}) %all-to-all-start) | async-done | bytes 1376288 | tf_op jit(solution)/shard_map/all_to_all | solution.py:824
  249.8 1.5 convert_reduce_fusion
  251.4 1.5 collective-permute-start.35
  252.9 1.9 collective-permute-start.37
  254.7 0.9 collective-permute-start.36
  256.5 3.4 %collective-permute-done.36 = bf16[3,896]{1,0:T(4,128)(2,1)S(1)} collective-permute-done((bf16[3,896]{1,0:T(4,128)(2,1)S(1)}, bf16[3,896]{1,0:T(4,128)(2,1)S(1)}, u32[]{:S(2)}, u32[]{:S(2)}) %collective-permute-start.36) | collective-permute-done | bytes 5408 | tf_op jit(solution)/shard_map/ppermute | solution.py:759
  261.9 7.6 %reduce-scatter.2.cloned.1.call-done = bf16[1,3,112,384]{3,2,1,0:T(8,128)(2,1)} async-done(((bf16[32,3,112,384]{3,2,1,0:T(8,128)(2,1)}), bf16[1,3,112,384]{3,2,1,0:T(8,128)(2,1)}) %reduce-scatter.2.cloned.1.call-update) | async-done | bytes 258064 | tf_op jit(solution)/shard_map/reduce_scatter | solution.py:818
  269.5 1.0 bitcast_convert_fusion
  271.3 0.8 reshape.93
  (134 shorter events, 15.3 us)
Async XLA Ops:
  7.2 109.6 %all-gather.3.cloned.1.call-start = ((), (), s32[]{:S(2)}) async-start(), calls=%async_computation.3 | async-start | bytes 8515584 | tf_op jit(solution)/shard_map/all_gather | solution.py:806
  10.4 25.2 %copy-start.16 = (s32[2,1,144,4]{2,3,1,0:T(4,128)S(1)}, s32[2,1,144,4]{2,3,1,0:T(4,128)}, u32[]{:S(2)}) copy-start(s32[2,1,144,4]{2,3,1,0:T(4,128)} %param.19) | copy-start | bytes 13828
  10.4 25.2 %copy-start.17 = (s32[2,1,144,4]{2,3,1,0:T(4,128)S(1)}, s32[2,1,144,4]{2,3,1,0:T(4,128)}, u32[]{:S(2)}) copy-start(s32[2,1,144,4]{2,3,1,0:T(4,128)} %param.18) | copy-start | bytes 13828
  10.4 25.3 %copy-start = (bf16[2,1,144,384]{3,2,1,0:T(8,128)(2,1)S(1)}, bf16[2,1,144,384]{3,2,1,0:T(8,128)(2,1)}, u32[]{:S(2)}) copy-start(bf16[2,1,144,384]{3,2,1,0:T(8,128)(2,1)} %param.16) | copy-start | bytes 663556
  10.4 6.6 %collective-permute-start.2 = (bf16[16,896]{1,0:T(8,128)(2,1)}, bf16[16,896]{1,0:T(8,128)(2,1)S(1)}, u32[]{:S(2)}, u32[]{:S(2)}) collective-permute-start(bf16[16,896]{1,0:T(8,128)(2,1)} %get-tuple-element.99), channel_id=1, source_target_pairs={{0,1},{1,2},{2,3},{3,0},{4,5},{5,6},{6,7},{7,4},{8,9},{9,10},{10,1... | collective-permute-start | bytes 86024 | tf_op jit(solution)/shard_map/ppermute | solution.py:759
  12.0 5.6 %collective-permute-start.1 = (bf16[16,896]{1,0:T(8,128)(2,1)}, bf16[16,896]{1,0:T(8,128)(2,1)S(1)}, u32[]{:S(2)}, u32[]{:S(2)}) collective-permute-start(bf16[16,896]{1,0:T(8,128)(2,1)} %get-tuple-element.99), channel_id=1, source_target_pairs={{0,2},{1,3},{2,0},{3,1},{4,6},{5,7},{6,4},{7,5},{8,10},{9,11},{10,... | collective-permute-start | bytes 86024 | tf_op jit(solution)/shard_map/ppermute | solution.py:759
  14.8 4.1 %collective-permute-start = (bf16[16,896]{1,0:T(8,128)(2,1)}, bf16[16,896]{1,0:T(8,128)(2,1)S(1)}, u32[]{:S(2)}, u32[]{:S(2)}) collective-permute-start(bf16[16,896]{1,0:T(8,128)(2,1)} %get-tuple-element.99), channel_id=1, source_target_pairs={{0,3},{1,0},{2,1},{3,2},{4,7},{5,4},{6,5},{7,6},{8,11},{9,8},{10,9... | collective-permute-start | bytes 86024 | tf_op jit(solution)/shard_map/ppermute | solution.py:759
  19.9 7.1 %collective-permute-start.4 = (bf16[48,896]{1,0:T(8,128)(2,1)S(1)}, bf16[48,896]{1,0:T(8,128)(2,1)S(1)}, u32[]{:S(2)}, u32[]{:S(2)}) collective-permute-start(bf16[48,896]{1,0:T(8,128)(2,1)S(1)} %get-tuple-element.218), channel_id=1, source_target_pairs={{0,64},{32,96},{64,0},{96,32},{1,65},{33,97},{65,1},{97,33},{2,66}... | collective-permute-start | bytes 258056 | tf_op jit(solution)/shard_map/ppermute | solution.py:759
  23.8 4.5 %collective-permute-start.3 = (bf16[48,896]{1,0:T(8,128)(2,1)S(1)}, bf16[48,896]{1,0:T(8,128)(2,1)S(1)}, u32[]{:S(2)}, u32[]{:S(2)}) collective-permute-start(bf16[48,896]{1,0:T(8,128)(2,1)S(1)} %get-tuple-element.218), channel_id=1, source_target_pairs={{0,96},{32,0},{64,32},{96,64},{1,97},{33,1},{65,33},{97,65},{2,98}... | collective-permute-start | bytes 258056 | tf_op jit(solution)/shard_map/ppermute | solution.py:759
  24.6 5.7 %collective-permute-start.5 = (bf16[48,896]{1,0:T(8,128)(2,1)S(1)}, bf16[48,896]{1,0:T(8,128)(2,1)S(1)}, u32[]{:S(2)}, u32[]{:S(2)}) collective-permute-start(bf16[48,896]{1,0:T(8,128)(2,1)S(1)} %get-tuple-element.218), channel_id=1, source_target_pairs={{0,32},{32,64},{64,96},{96,0},{1,33},{33,65},{65,97},{97,1},{2,34}... | collective-permute-start | bytes 258056 | tf_op jit(solution)/shard_map/ppermute | solution.py:759
  30.3 12.4 %collective-permute-start.7 = (bf16[4,48,896]{2,1,0:T(8,128)(2,1)S(1)}, bf16[4,48,896]{2,1,0:T(8,128)(2,1)S(1)}, u32[]{:S(2)}, u32[]{:S(2)}) collective-permute-start(bf16[4,48,896]{2,1,0:T(8,128)(2,1)S(1)} %get-tuple-element.214), channel_id=1, source_target_pairs={{0,16},{8,24},{16,0},{24,8},{1,17},{9,25},{17,1},{25,9},{2,18},{10... | collective-permute-start | bytes 1032200 | tf_op jit(solution)/shard_map/ppermute | solution.py:759
  33.6 13.1 %collective-permute-start.6 = (bf16[4,48,896]{2,1,0:T(8,128)(2,1)S(1)}, bf16[4,48,896]{2,1,0:T(8,128)(2,1)S(1)}, u32[]{:S(2)}, u32[]{:S(2)}) collective-permute-start(bf16[4,48,896]{2,1,0:T(8,128)(2,1)S(1)} %get-tuple-element.214), channel_id=1, source_target_pairs={{0,24},{8,0},{16,8},{24,16},{1,25},{9,1},{17,9},{25,17},{2,26},{10... | collective-permute-start | bytes 1032200 | tf_op jit(solution)/shard_map/ppermute | solution.py:759
  34.7 12.1 %collective-permute-start.8 = (bf16[4,48,896]{2,1,0:T(8,128)(2,1)S(1)}, bf16[4,48,896]{2,1,0:T(8,128)(2,1)S(1)}, u32[]{:S(2)}, u32[]{:S(2)}) collective-permute-start(bf16[4,48,896]{2,1,0:T(8,128)(2,1)S(1)} %get-tuple-element.214), channel_id=1, source_target_pairs={{0,8},{8,16},{16,24},{24,0},{1,9},{9,17},{17,25},{25,1},{2,10},{10... | collective-permute-start | bytes 1032200 | tf_op jit(solution)/shard_map/ppermute | solution.py:759
  35.7 11.2 %copy-start.14 = (bf16[2,160,384]{2,1,0:T(8,128)(2,1)}, bf16[2,160,384]{2,1,0:T(8,128)(2,1)S(1)}, u32[]{:S(2)}) copy-start(bf16[2,160,384]{2,1,0:T(8,128)(2,1)S(1)} %fusion.1.t0) | copy-start | bytes 737284
  35.7 11.2 %collective-permute-start.11 = (bf16[2,160,384]{2,1,0:T(8,128)(2,1)S(1)}, bf16[2,160,384]{2,1,0:T(8,128)(2,1)S(1)}, u32[]{:S(2)}, u32[]{:S(2)}) collective-permute-start(bf16[2,160,384]{2,1,0:T(8,128)(2,1)S(1)} %fusion.1.t0), channel_id=1, source_target_pairs={{0,1},{1,2},{2,3},{3,0},{4,5},{5,6},{6,7},{7,4},{8,9},{9,10},{10,1... | collective-permute-start | bytes 737288 | tf_op jit(solution)/shard_map/ppermute | solution.py:759
  36.1 11.1 %collective-permute-start.10 = (bf16[2,160,384]{2,1,0:T(8,128)(2,1)S(1)}, bf16[2,160,384]{2,1,0:T(8,128)(2,1)S(1)}, u32[]{:S(2)}, u32[]{:S(2)}) collective-permute-start(bf16[2,160,384]{2,1,0:T(8,128)(2,1)S(1)} %fusion.1.t0), channel_id=1, source_target_pairs={{0,2},{1,3},{2,0},{3,1},{4,6},{5,7},{6,4},{7,5},{8,10},{9,11},{10,... | collective-permute-start | bytes 737288 | tf_op jit(solution)/shard_map/ppermute | solution.py:759
  42.7 6.3 %collective-permute-start.9 = (bf16[2,160,384]{2,1,0:T(8,128)(2,1)S(1)}, bf16[2,160,384]{2,1,0:T(8,128)(2,1)S(1)}, u32[]{:S(2)}, u32[]{:S(2)}) collective-permute-start(bf16[2,160,384]{2,1,0:T(8,128)(2,1)S(1)} %fusion.1.t0), channel_id=1, source_target_pairs={{0,3},{1,0},{2,1},{3,2},{4,7},{5,4},{6,5},{7,6},{8,11},{9,8},{10,9... | collective-permute-start | bytes 737288 | tf_op jit(solution)/shard_map/ppermute | solution.py:759
  46.7 3.2 %copy-start.1 = (bf16[2,1,144,384]{3,2,1,0:T(8,128)(2,1)S(1)}, bf16[2,1,144,384]{3,2,1,0:T(8,128)(2,1)}, u32[]{:S(2)}) copy-start(bf16[2,1,144,384]{3,2,1,0:T(8,128)(2,1)} %param.31) | copy-start | bytes 663556
  46.7 8.6 %copy-start.18 = (s32[2,1]{0,1:T(1,128)S(1)}, s32[2,1]{0,1:T(1,128)}, u32[]{:S(2)}) copy-start(s32[2,1]{0,1:T(1,128)} %param.17) | copy-start | bytes 28
  47.0 10.8 %copy-start.13 = (bf16[4,4,48,896]{3,2,1,0:T(8,128)(2,1)}, bf16[4,4,48,896]{3,2,1,0:T(8,128)(2,1)S(1)}, u32[]{:S(2)}) copy-start(bf16[4,4,48,896]{3,2,1,0:T(8,128)(2,1)S(1)} %pad_maximum_fusion) | copy-start | bytes 4128772
  49.7 219.7 %reduce-scatter.2.cloned.1.call-start = ((), (), s32[]{:S(2)}) async-start(), calls=%async_computation.2 | async-start | bytes 8515584 | tf_op jit(solution)/shard_map/reduce_scatter | solution.py:818
  49.8 8.0 %collective-permute-start.12 = (bf16[16,48,896]{2,1,0:T(8,128)(2,1)S(1)}, bf16[16,48,896]{2,1,0:T(8,128)(2,1)}, u32[]{:S(2)}, u32[]{:S(2)}) collective-permute-start(bf16[16,48,896]{2,1,0:T(8,128)(2,1)S(1)} %bitcast.54), channel_id=1, source_target_pairs={{0,4},{4,0},{1,5},{5,1},{2,6},{6,2},{3,7},{7,3},{8,12},{12,8},{9,1... | collective-permute-start | bytes 4128776 | tf_op jit(solution)/shard_map/ppermute | solution.py:759
  49.9 36.9 %collective-permute-start.15 = (bf16[2,144,384]{2,1,0:T(8,128)(2,1)S(1)}, bf16[2,144,384]{2,1,0:T(8,128)(2,1)}, u32[]{:S(2)}, u32[]{:S(2)}) collective-permute-start(bf16[2,144,384]{2,1,0:T(8,128)(2,1)S(1)} %bitcast.50), channel_id=1, source_target_pairs={{0,1},{1,2},{2,3},{3,0},{4,5},{5,6},{6,7},{7,4},{8,9},{9,10},{10,1... | collective-permute-start | bytes 663560 | tf_op jit(solution)/shard_map/ppermute | solution.py:759
  50.1 36.6 %collective-permute-start.14 = (bf16[2,144,384]{2,1,0:T(8,128)(2,1)S(1)}, bf16[2,144,384]{2,1,0:T(8,128)(2,1)}, u32[]{:S(2)}, u32[]{:S(2)}) collective-permute-start(bf16[2,144,384]{2,1,0:T(8,128)(2,1)S(1)} %bitcast.51), channel_id=1, source_target_pairs={{0,2},{1,3},{2,0},{3,1},{4,6},{5,7},{6,4},{7,5},{8,10},{9,11},{10,... | collective-permute-start | bytes 663560 | tf_op jit(solution)/shard_map/ppermute | solution.py:759
  55.1 31.6 %collective-permute-start.13 = (bf16[2,144,384]{2,1,0:T(8,128)(2,1)S(1)}, bf16[2,144,384]{2,1,0:T(8,128)(2,1)}, u32[]{:S(2)}, u32[]{:S(2)}) collective-permute-start(bf16[2,144,384]{2,1,0:T(8,128)(2,1)S(1)} %bitcast.52), channel_id=1, source_target_pairs={{0,3},{1,0},{2,1},{3,2},{4,7},{5,4},{6,5},{7,6},{8,11},{9,8},{10,9... | collective-permute-start | bytes 663560 | tf_op jit(solution)/shard_map/ppermute | solution.py:759
  62.8 38.0 %copy-start.10 = (f32[8,384]{1,0:T(8,128)S(1)}, f32[8,384]{1,0:T(8,128)}, u32[]{:S(2)}) copy-start(f32[8,384]{1,0:T(8,128)} %get-tuple-element.110.vec) | copy-start | bytes 36868
  86.8 13.4 %collective-permute-start.16 = (bf16[2,144,384]{2,1,0:T(8,128)(2,1)}, bf16[2,144,384]{2,1,0:T(8,128)(2,1)S(1)}, u32[]{:S(2)}, u32[]{:S(2)}) collective-permute-start(bf16[2,144,384]{2,1,0:T(8,128)(2,1)} %get-tuple-element.116), channel_id=1, source_target_pairs={{0,1},{1,2},{2,3},{3,0},{4,5},{5,6},{6,7},{7,4},{8,9},{9,10},{10,1... | collective-permute-start | bytes 663560 | tf_op jit(solution)/shard_map/ppermute | solution.py:759
  88.9 11.3 %collective-permute-start.17 = (bf16[2,144,384]{2,1,0:T(8,128)(2,1)}, bf16[2,144,384]{2,1,0:T(8,128)(2,1)S(1)}, u32[]{:S(2)}, u32[]{:S(2)}) collective-permute-start(bf16[2,144,384]{2,1,0:T(8,128)(2,1)} %get-tuple-element.117), channel_id=1, source_target_pairs={{0,2},{1,3},{2,0},{3,1},{4,6},{5,7},{6,4},{7,5},{8,10},{9,11},{10,... | collective-permute-start | bytes 663560 | tf_op jit(solution)/shard_map/ppermute | solution.py:759
  88.9 12.0 %collective-permute-start.18 = (bf16[2,144,384]{2,1,0:T(8,128)(2,1)}, bf16[2,144,384]{2,1,0:T(8,128)(2,1)S(1)}, u32[]{:S(2)}, u32[]{:S(2)}) collective-permute-start(bf16[2,144,384]{2,1,0:T(8,128)(2,1)} %get-tuple-element.118), channel_id=1, source_target_pairs={{0,3},{1,0},{2,1},{3,2},{4,7},{5,4},{6,5},{7,6},{8,11},{9,8},{10,9... | collective-permute-start | bytes 663560 | tf_op jit(solution)/shard_map/ppermute | solution.py:759
  102.1 14.7 %copy-start.4 = (bf16[2,144,384]{2,1,0:T(8,128)(2,1)}, bf16[2,144,384]{2,1,0:T(8,128)(2,1)S(1)}, u32[]{:S(2)}) copy-start(bf16[2,144,384]{2,1,0:T(8,128)(2,1)S(1)} %get-tuple-element.120.x0) | copy-start | bytes 663556
  102.1 8.7 %collective-permute-start.21 = (bf16[2,144,384]{2,1,0:T(8,128)(2,1)S(1)}, bf16[2,144,384]{2,1,0:T(8,128)(2,1)S(1)}, u32[]{:S(2)}, u32[]{:S(2)}) collective-permute-start(bf16[2,144,384]{2,1,0:T(8,128)(2,1)S(1)} %get-tuple-element.120.x0), channel_id=1, source_target_pairs={{0,1},{1,2},{2,3},{3,0},{4,5},{5,6},{6,7},{7,4},{8,9},{9,10},{10,1... | collective-permute-start | bytes 663560 | tf_op jit(solution)/shard_map/ppermute | solution.py:759
  104.1 12.6 %collective-permute-start.20 = (bf16[2,144,384]{2,1,0:T(8,128)(2,1)S(1)}, bf16[2,144,384]{2,1,0:T(8,128)(2,1)S(1)}, u32[]{:S(2)}, u32[]{:S(2)}) collective-permute-start(bf16[2,144,384]{2,1,0:T(8,128)(2,1)S(1)} %get-tuple-element.120.x0), channel_id=1, source_target_pairs={{0,2},{1,3},{2,0},{3,1},{4,6},{5,7},{6,4},{7,5},{8,10},{9,11},{10,... | collective-permute-start | bytes 663560 | tf_op jit(solution)/shard_map/ppermute | solution.py:759
  106.7 10.0 %collective-permute-start.19 = (bf16[2,144,384]{2,1,0:T(8,128)(2,1)S(1)}, bf16[2,144,384]{2,1,0:T(8,128)(2,1)S(1)}, u32[]{:S(2)}, u32[]{:S(2)}) collective-permute-start(bf16[2,144,384]{2,1,0:T(8,128)(2,1)S(1)} %get-tuple-element.120.x0), channel_id=1, source_target_pairs={{0,3},{1,0},{2,1},{3,2},{4,7},{5,4},{6,5},{7,6},{8,11},{9,8},{10,9... | collective-permute-start | bytes 663560 | tf_op jit(solution)/shard_map/ppermute | solution.py:759
  110.8 6.0 %copy-start.31 = (bf16[2,144,384]{2,1,0:T(8,128)(2,1)}, bf16[2,144,384]{2,1,0:T(8,128)(2,1)S(1)}, u32[]{:S(2)}) copy-start(bf16[2,144,384]{2,1,0:T(8,128)(2,1)S(1)} %collective-permute-done.21.x3) | copy-start | bytes 663556
  143.8 15.9 %collective-permute-start.22 = (bf16[2,144,384]{2,1,0:T(8,128)(2,1)}, bf16[2,144,384]{2,1,0:T(8,128)(2,1)S(1)}, u32[]{:S(2)}, u32[]{:S(2)}) collective-permute-start(bf16[2,144,384]{2,1,0:T(8,128)(2,1)} %get-tuple-element.127), channel_id=1, source_target_pairs={{0,1},{1,2},{2,3},{3,0},{4,5},{5,6},{6,7},{7,4},{8,9},{9,10},{10,1... | collective-permute-start | bytes 663560 | tf_op jit(solution)/shard_map/ppermute | solution.py:759
  144.8 14.9 %collective-permute-start.23 = (bf16[2,144,384]{2,1,0:T(8,128)(2,1)}, bf16[2,144,384]{2,1,0:T(8,128)(2,1)S(1)}, u32[]{:S(2)}, u32[]{:S(2)}) collective-permute-start(bf16[2,144,384]{2,1,0:T(8,128)(2,1)} %get-tuple-element.128), channel_id=1, source_target_pairs={{0,2},{1,3},{2,0},{3,1},{4,6},{5,7},{6,4},{7,5},{8,10},{9,11},{10,... | collective-permute-start | bytes 663560 | tf_op jit(solution)/shard_map/ppermute | solution.py:759
  147.4 12.3 %collective-permute-start.24 = (bf16[2,144,384]{2,1,0:T(8,128)(2,1)}, bf16[2,144,384]{2,1,0:T(8,128)(2,1)S(1)}, u32[]{:S(2)}, u32[]{:S(2)}) collective-permute-start(bf16[2,144,384]{2,1,0:T(8,128)(2,1)} %get-tuple-element.129), channel_id=1, source_target_pairs={{0,3},{1,0},{2,1},{3,2},{4,7},{5,4},{6,5},{7,6},{8,11},{9,8},{10,9... | collective-permute-start | bytes 663560 | tf_op jit(solution)/shard_map/ppermute | solution.py:759
  148.2 11.5 %copy-start.2 = (bf16[2,1,144,384]{3,2,1,0:T(8,128)(2,1)S(1)}, bf16[2,1,144,384]{3,2,1,0:T(8,128)(2,1)}, u32[]{:S(2)}) copy-start(bf16[2,1,144,384]{3,2,1,0:T(8,128)(2,1)} %param.31) | copy-start | bytes 663556
  148.2 11.5 %copy-start.9 = (bf16[2,144,384]{2,1,0:T(8,128)(2,1)S(1)}, bf16[2,144,384]{2,1,0:T(8,128)(2,1)}, u32[]{:S(2)}) copy-start(bf16[2,144,384]{2,1,0:T(8,128)(2,1)} %get-tuple-element.134.p0) | copy-start | bytes 663556
  161.6 4.6 %copy-start.3 = (bf16[2,144,384]{2,1,0:T(8,128)(2,1)}, bf16[2,144,384]{2,1,0:T(8,128)(2,1)S(1)}, u32[]{:S(2)}) copy-start(bf16[2,144,384]{2,1,0:T(8,128)(2,1)S(1)} %get-tuple-element.138.g0) | copy-start | bytes 663556
  161.6 12.2 %collective-permute-start.27 = (bf16[2,144,384]{2,1,0:T(8,128)(2,1)S(1)}, bf16[2,144,384]{2,1,0:T(8,128)(2,1)S(1)}, u32[]{:S(2)}, u32[]{:S(2)}) collective-permute-start(bf16[2,144,384]{2,1,0:T(8,128)(2,1)S(1)} %get-tuple-element.138.g0), channel_id=1, source_target_pairs={{0,1},{1,2},{2,3},{3,0},{4,5},{5,6},{6,7},{7,4},{8,9},{9,10},{10,1... | collective-permute-start | bytes 663560 | tf_op jit(solution)/shard_map/ppermute | solution.py:759
  162.9 10.9 %collective-permute-start.26 = (bf16[2,144,384]{2,1,0:T(8,128)(2,1)S(1)}, bf16[2,144,384]{2,1,0:T(8,128)(2,1)S(1)}, u32[]{:S(2)}, u32[]{:S(2)}) collective-permute-start(bf16[2,144,384]{2,1,0:T(8,128)(2,1)S(1)} %get-tuple-element.138.g0), channel_id=1, source_target_pairs={{0,2},{1,3},{2,0},{3,1},{4,6},{5,7},{6,4},{7,5},{8,10},{9,11},{10,... | collective-permute-start | bytes 663560 | tf_op jit(solution)/shard_map/ppermute | solution.py:759
  163.8 10.5 %collective-permute-start.25 = (bf16[2,144,384]{2,1,0:T(8,128)(2,1)S(1)}, bf16[2,144,384]{2,1,0:T(8,128)(2,1)S(1)}, u32[]{:S(2)}, u32[]{:S(2)}) collective-permute-start(bf16[2,144,384]{2,1,0:T(8,128)(2,1)S(1)} %get-tuple-element.138.g0), channel_id=1, source_target_pairs={{0,3},{1,0},{2,1},{3,2},{4,7},{5,4},{6,5},{7,6},{8,11},{9,8},{10,9... | collective-permute-start | bytes 663560 | tf_op jit(solution)/shard_map/ppermute | solution.py:759
  206.2 3.4 %collective-permute-start.28 = (bf16[16,48,896]{2,1,0:T(8,128)(2,1)}, bf16[16,48,896]{2,1,0:T(8,128)(2,1)S(1)}, u32[]{:S(2)}, u32[]{:S(2)}) collective-permute-start(bf16[16,48,896]{2,1,0:T(8,128)(2,1)} %get-tuple-element.154), channel_id=1, source_target_pairs={{0,4},{4,0},{1,5},{5,1},{2,6},{6,2},{3,7},{7,3},{8,12},{12,8},{9,1... | collective-permute-start | bytes 4128776 | tf_op jit(solution)/shard_map/ppermute | solution.py:759
  212.4 4.9 %copy-start.27 = (bf16[2,144,384]{2,1,0:T(8,128)(2,1)S(1)}, bf16[2,144,384]{2,1,0:T(8,128)(2,1)}, u32[]{:S(2)}) copy-start(bf16[2,144,384]{2,1,0:T(8,128)(2,1)} %get-tuple-element.168) | copy-start | bytes 663556
  212.4 6.4 %copy-start.26 = (bf16[2,144,384]{2,1,0:T(8,128)(2,1)S(1)}, bf16[2,144,384]{2,1,0:T(8,128)(2,1)}, u32[]{:S(2)}) copy-start(bf16[2,144,384]{2,1,0:T(8,128)(2,1)} %get-tuple-element.169) | copy-start | bytes 663556
  212.4 9.2 %copy-start.25 = (bf16[2,144,384]{2,1,0:T(8,128)(2,1)S(1)}, bf16[2,144,384]{2,1,0:T(8,128)(2,1)}, u32[]{:S(2)}) copy-start(bf16[2,144,384]{2,1,0:T(8,128)(2,1)} %get-tuple-element.170) | copy-start | bytes 663556
  212.4 19.1 %copy-start.24 = (bf16[2,144,384]{2,1,0:T(8,128)(2,1)S(1)}, bf16[2,144,384]{2,1,0:T(8,128)(2,1)}, u32[]{:S(2)}) copy-start(bf16[2,144,384]{2,1,0:T(8,128)(2,1)} %get-tuple-element.172) | copy-start | bytes 663556
  212.4 20.1 %copy-start.23 = (bf16[2,144,384]{2,1,0:T(8,128)(2,1)S(1)}, bf16[2,144,384]{2,1,0:T(8,128)(2,1)}, u32[]{:S(2)}) copy-start(bf16[2,144,384]{2,1,0:T(8,128)(2,1)} %get-tuple-element.173) | copy-start | bytes 663556
  212.4 22.9 %copy-start.22 = (bf16[2,144,384]{2,1,0:T(8,128)(2,1)S(1)}, bf16[2,144,384]{2,1,0:T(8,128)(2,1)}, u32[]{:S(2)}) copy-start(bf16[2,144,384]{2,1,0:T(8,128)(2,1)} %get-tuple-element.174) | copy-start | bytes 663556
  212.4 23.4 %copy-start.6 = (f32[2,144,384]{2,1,0:T(8,128)S(1)}, f32[2,144,384]{2,1,0:T(8,128)}, u32[]{:S(2)}) copy-start(f32[2,144,384]{2,1,0:T(8,128)} %copy-done.5) | copy-start | bytes 1327108
  212.4 23.4 %copy-start.7 = (bf16[2,144,384]{2,1,0:T(8,128)(2,1)S(1)}, bf16[2,144,384]{2,1,0:T(8,128)(2,1)}, u32[]{:S(2)}) copy-start(bf16[2,144,384]{2,1,0:T(8,128)(2,1)} %get-tuple-element.176.p0) | copy-start | bytes 663556
  212.4 23.3 %copy-start.11 = (f32[8,384]{1,0:T(8,128)S(1)}, f32[8,384]{1,0:T(8,128)}, u32[]{:S(2)}) copy-start(f32[8,384]{1,0:T(8,128)} %get-tuple-element.110.vec) | copy-start | bytes 36868
  212.5 37.3 %all-to-all-start = ((bf16[16,48,896]{2,1,0:T(8,128)(2,1)}), bf16[16,48,896]{2,1,0:T(8,128)(2,1)}, u32[]{:S(2)}, u32[]{:S(2)}) async-start(bf16[16,48,896]{2,1,0:T(8,128)(2,1)} %add_convert_fusion), calls=%async_computation | async-start | bytes 2752512 | tf_op jit(solution)/shard_map/all_to_all | solution.py:824
  217.3 8.6 %collective-permute-start.29 = (bf16[2,144,384]{2,1,0:T(8,128)(2,1)S(1)}, bf16[2,144,384]{2,1,0:T(8,128)(2,1)S(1)}, u32[]{:S(2)}, u32[]{:S(2)}) collective-permute-start(bf16[2,144,384]{2,1,0:T(8,128)(2,1)S(1)} %copy-done.27), channel_id=1, source_target_pairs={{0,1},{1,2},{2,3},{3,0},{4,5},{5,6},{6,7},{7,4},{8,9},{9,10},{10,1... | collective-permute-start | bytes 663560 | tf_op jit(solution)/shard_map/ppermute | solution.py:759
  218.8 12.7 %collective-permute-start.30 = (bf16[2,144,384]{2,1,0:T(8,128)(2,1)S(1)}, bf16[2,144,384]{2,1,0:T(8,128)(2,1)S(1)}, u32[]{:S(2)}, u32[]{:S(2)}) collective-permute-start(bf16[2,144,384]{2,1,0:T(8,128)(2,1)S(1)} %copy-done.26), channel_id=1, source_target_pairs={{0,2},{1,3},{2,0},{3,1},{4,6},{5,7},{6,4},{7,5},{8,10},{9,11},{10,... | collective-permute-start | bytes 663560 | tf_op jit(solution)/shard_map/ppermute | solution.py:759
  221.6 9.9 %collective-permute-start.31 = (bf16[2,144,384]{2,1,0:T(8,128)(2,1)S(1)}, bf16[2,144,384]{2,1,0:T(8,128)(2,1)S(1)}, u32[]{:S(2)}, u32[]{:S(2)}) collective-permute-start(bf16[2,144,384]{2,1,0:T(8,128)(2,1)S(1)} %copy-done.25), channel_id=1, source_target_pairs={{0,3},{1,0},{2,1},{3,2},{4,7},{5,4},{6,5},{7,6},{8,11},{9,8},{10,9... | collective-permute-start | bytes 663560 | tf_op jit(solution)/shard_map/ppermute | solution.py:759
  231.5 8.0 %collective-permute-start.32 = (bf16[2,144,384]{2,1,0:T(8,128)(2,1)S(1)}, bf16[2,144,384]{2,1,0:T(8,128)(2,1)S(1)}, u32[]{:S(2)}, u32[]{:S(2)}) collective-permute-start(bf16[2,144,384]{2,1,0:T(8,128)(2,1)S(1)} %copy-done.24), channel_id=1, source_target_pairs={{0,1},{1,2},{2,3},{3,0},{4,5},{5,6},{6,7},{7,4},{8,9},{9,10},{10,1... | collective-permute-start | bytes 663560 | tf_op jit(solution)/shard_map/ppermute | solution.py:759
  232.5 12.9 %collective-permute-start.33 = (bf16[2,144,384]{2,1,0:T(8,128)(2,1)S(1)}, bf16[2,144,384]{2,1,0:T(8,128)(2,1)S(1)}, u32[]{:S(2)}, u32[]{:S(2)}) collective-permute-start(bf16[2,144,384]{2,1,0:T(8,128)(2,1)S(1)} %copy-done.23), channel_id=1, source_target_pairs={{0,2},{1,3},{2,0},{3,1},{4,6},{5,7},{6,4},{7,5},{8,10},{9,11},{10,... | collective-permute-start | bytes 663560 | tf_op jit(solution)/shard_map/ppermute | solution.py:759
  235.3 10.2 %collective-permute-start.34 = (bf16[2,144,384]{2,1,0:T(8,128)(2,1)S(1)}, bf16[2,144,384]{2,1,0:T(8,128)(2,1)S(1)}, u32[]{:S(2)}, u32[]{:S(2)}) collective-permute-start(bf16[2,144,384]{2,1,0:T(8,128)(2,1)S(1)} %copy-done.22), channel_id=1, source_target_pairs={{0,3},{1,0},{2,1},{3,2},{4,7},{5,4},{6,5},{7,6},{8,11},{9,8},{10,9... | collective-permute-start | bytes 663560 | tf_op jit(solution)/shard_map/ppermute | solution.py:759
  235.8 9.7 %copy-start.15 = (bf16[2,144,384]{2,1,0:T(8,128)(2,1)S(1)}, bf16[2,144,384]{2,1,0:T(8,128)(2,1)}, u32[]{:S(2)}) copy-start(bf16[2,144,384]{2,1,0:T(8,128)(2,1)} %get-tuple-element.171) | copy-start | bytes 663556
  251.4 4.9 %collective-permute-start.35 = (bf16[3,896]{1,0:T(4,128)(2,1)S(1)}, bf16[3,896]{1,0:T(4,128)(2,1)S(1)}, u32[]{:S(2)}, u32[]{:S(2)}) collective-permute-start(bf16[3,896]{1,0:T(4,128)(2,1)S(1)} %get-tuple-element.219), channel_id=1, source_target_pairs={{0,1},{1,2},{2,3},{3,0},{4,5},{5,6},{6,7},{7,4},{8,9},{9,10},{10,1... | collective-permute-start | bytes 16136 | tf_op jit(solution)/shard_map/ppermute | solution.py:759
  252.9 3.6 %collective-permute-start.37 = (bf16[3,896]{1,0:T(4,128)(2,1)S(1)}, bf16[3,896]{1,0:T(4,128)(2,1)S(1)}, u32[]{:S(2)}, u32[]{:S(2)}) collective-permute-start(bf16[3,896]{1,0:T(4,128)(2,1)S(1)} %get-tuple-element.220), channel_id=1, source_target_pairs={{0,3},{1,0},{2,1},{3,2},{4,7},{5,4},{6,5},{7,6},{8,11},{9,8},{10,9... | collective-permute-start | bytes 16136 | tf_op jit(solution)/shard_map/ppermute | solution.py:759
  254.7 5.1 %collective-permute-start.36 = (bf16[3,896]{1,0:T(4,128)(2,1)S(1)}, bf16[3,896]{1,0:T(4,128)(2,1)S(1)}, u32[]{:S(2)}, u32[]{:S(2)}) collective-permute-start(bf16[3,896]{1,0:T(4,128)(2,1)S(1)} %get-tuple-element.221), channel_id=1, source_target_pairs={{0,2},{1,3},{2,0},{3,1},{4,6},{5,7},{6,4},{7,5},{8,10},{9,11},{10,... | collective-permute-start | bytes 16136 | tf_op jit(solution)/shard_map/ppermute | solution.py:759
  (11 other events, 10.4 us)
Sparse Core Ops, SparseCore 0:
  49.9 52.4 all-gather.2
  166.3 103.1 reduce-scatter.1
